TPU v7x, 256 devices: a whole 4x4x8 slice. The times are simulated.
256 devices in a mesh: seq: 32 (over z, y_lo, core), head: 8 (over x, y_hi).
Axes of the slice: x: 4, y: 4 (y_hi: 2, y_lo: 2; y = y_hi * 2 + y_lo), z: 8, core: 2. Of those that a mesh axis runs over, the one named last changes fastest.
Arguments:
- queries: bfloat16 [2048, 8192], P('seq', 'head'), may hold values from -15 to 15
- cache_keys: bfloat16 [8, 32768, 128], P('head', 'seq'), may hold values from -6 to 6
- cache_values: bfloat16 [8, 32768, 128], P('head', 'seq'), may hold values from -6 to 6
- new_keys: bfloat16 [2048, 1024], P('seq', 'head'), may hold values from -9.5625 to 9.5625
- new_values: bfloat16 [2048, 1024], P('seq', 'head'), may hold values from -6 to 6
- cache_len: int32 [32], P('seq'), may hold values from 256 to 1024, as said below
- span_rank: int32 [2048], replicated, may hold values from 0 to 2047, each once
- out_weight: bfloat16 [8192, 8192], P('head', 'seq'), may hold values from -0.0625 to 0.0625
Outputs:
- projected: bfloat16 [2048, 8192], P('head', 'seq')
Inputs may be any that keep to these rules, and one draw needn't show every extreme that they name: `cache_len`: each shard holds at least 256 filled positions; one shard is full in every draw.
All inputs are finite; a program needn't handle non-finite values.
Results may differ from a plain program's by a relative error of at most 0.006.
Values may be sent and summed in bfloat16 or wider, within the bound.
No kernel may reach another device: no remote copies, remote signals or barrier semaphores. Data moves between devices by JAX's collectives and lax.ppermute only.
A program may use at most 64 MiB of HBM per device.

v0:
```python
import functools
import math

import jax
import jax.numpy as jnp
from jax import lax
from jax.experimental import pallas as pl
from jax.experimental.pallas import tpu as pltpu
from jax.sharding import PartitionSpec as P

NEG_FILL = -1e30
BF16 = jnp.bfloat16
F32 = jnp.float32
Z, YC = 8, 4
QPH, HD = 8, 128
TOK = 64
CACHE = 1024
GRAN = 128
CHUNK = 512
BLOCKS = 4
ROWS = TOK * QPH
TILE = 2 * ROWS
VROWS = 144
WIDE = QPH * HD + 128
KEY_AT = 2 * TOK
VALUE_AT = KEY_AT + CACHE
META_AT = VALUE_AT + CACHE
BLOCK_ROWS = META_AT + 16
PLANES = [[z * YC + i for i in range(YC)] for z in range(Z)]


def seq_permute(value, move):
    pairs = []
    for z in range(Z):
        for y in range(2):
            for c in range(2):
                to_z, to_y, to_c = move(z, y, c)
                pairs.append((z * 4 + y * 2 + c, (to_z % Z) * 4 + to_y * 2 + to_c))
    return lax.ppermute(value, "seq", pairs)


def pack_kernel(length_ref, k_ref, v_ref, nk_ref, nv_ref, out_ref):
    length = length_ref[0]
    out_ref[0:TOK, :] = nk_ref[...]
    out_ref[TOK:KEY_AT, :] = nv_ref[...]
    out_ref[KEY_AT:VALUE_AT, :] = k_ref[0]
    out_ref[VALUE_AT:META_AT, :] = v_ref[0]
    row = lax.broadcasted_iota(jnp.int32, (16, HD), 0)
    meta = jnp.where(row < 8, length // 32, length % 32)
    out_ref[META_AT:BLOCK_ROWS, :] = meta.astype(F32).astype(BF16)


def pack(length, keys, values, new_keys, new_values):
    whole = pl.BlockSpec(memory_space=pltpu.VMEM)
    return pl.pallas_call(
        pack_kernel,
        out_shape=jax.ShapeDtypeStruct((BLOCK_ROWS, HD), BF16),
        in_specs=[pl.BlockSpec(memory_space=pltpu.SMEM)] + [whole] * 4,
        out_specs=whole,
        name="pack",
    )(length, keys, values, new_keys, new_values)


def attention_kernel(shards, first, last, *refs):
    refs = list(refs)
    take = lambda n: [refs.pop(0) for _ in range(n)]
    q_refs, shard_refs = take(BLOCKS), take(shards)
    if not first:
        m_in, acc_in = take(2)
    if last:
        new_refs = take(8)
        q_rank, k_rank = take(2)
        out_refs = take(BLOCKS)
    m_all, acc = take(2)
    q_all, k_all, v_all, s0, s1, p0, p1, scale0, scale1 = take(9)
    if last:
        new_k, new_v = take(2)
    factor = F32(math.log2(math.e) / math.sqrt(HD))
    for b in range(BLOCKS):
        for h in range(QPH):
            scaled = q_refs[b][:, h * HD : (h + 1) * HD].astype(F32) * factor
            high = scaled.astype(BF16)
            rows = pl.ds(b * ROWS + h * TOK, TOK)
            q_all[rows, 0:HD] = high
            q_all[rows, HD : 2 * HD] = (scaled - high.astype(F32)).astype(BF16)
    if first:
        m_all[...] = jnp.full(m_all.shape, NEG_FILL, F32)
        acc[...] = jnp.zeros(acc.shape, F32)
    else:
        m_all[...] = m_in[...]
        acc[...] = acc_in[...]

    position = lax.broadcasted_iota(jnp.int32, (CACHE, HD), 0)
    lane_position = lax.broadcasted_iota(jnp.int32, (16, CACHE), 1)
    row16 = lax.broadcasted_iota(jnp.int32, (16, CACHE), 0)
    total = jnp.int32(0)
    for ref in shard_refs:
        meta = ref[META_AT:BLOCK_ROWS, :].astype(F32).astype(jnp.int32)
        length = jnp.max(meta[0:8, :]) * 32 + jnp.max(meta[8:16, :])
        start = pl.multiple_of(total, GRAN)
        counted = position < length
        keys = ref[KEY_AT:VALUE_AT, :]
        keys = jnp.where(counted, keys, jnp.broadcast_to(keys[0:1, :], keys.shape))
        k_all[pl.ds(start, CACHE), 0:HD] = keys
        k_all[pl.ds(start, CACHE), HD : 2 * HD] = keys
        values = ref[VALUE_AT:META_AT, :]
        values = jnp.where(counted, values, jnp.zeros_like(values))
        v_all[0:HD, pl.ds(start, CACHE)] = values.T
        flags = jnp.logical_and(lane_position < length, row16 == 0)
        v_all[HD:VROWS, pl.ds(start, CACHE)] = jnp.where(flags, 1.0, 0.0).astype(BF16)
        total = total + ((length + GRAN - 1) // GRAN) * GRAN
    filler = pl.ds(pl.multiple_of(total, GRAN), CHUNK)
    k_all[filler, :] = jnp.broadcast_to(k_all[0:1, :], (CHUNK, 2 * HD))
    v_all[:, filler] = jnp.zeros((VROWS, CHUNK), BF16)

    left, right = slice(0, TILE), slice(TILE, 2 * TILE)

    def scores(s, k, rows):
        s[...] = lax.dot_general(
            k, q_all[rows, :], (((1,), (1,)), ((), ())), preferred_element_type=F32
        )

    def weigh(s, p, scale, rows):
        before = m_all[:, rows]
        top = jnp.maximum(before, jnp.max(s, axis=0, keepdims=True))
        m_all[:, rows] = top
        p[...] = jnp.exp2(s - top).astype(BF16)
        scale[...] = jnp.exp2(before - top)

    def add(p, scale, v, rows):
        acc[:, rows] = acc[:, rows] * scale[...] + jnp.dot(
            v, p[...], preferred_element_type=F32
        )

    def chunk(i):
        return pl.ds(pl.multiple_of(i * CHUNK, CHUNK), CHUNK)

    count = (total + CHUNK - 1) // CHUNK
    p1[...] = jnp.zeros(p1.shape, BF16)
    scale1[...] = jnp.ones(scale1.shape, F32)
    scores(s0, k_all[0:CHUNK, :], left)

    @pl.loop(0, count)
    def _(i):
        before, here = chunk(jnp.maximum(i - 1, 0)), chunk(i)
        after = chunk(jnp.minimum(i + 1, count - 1))
        scores(s1, k_all[here, :], right)
        weigh(s0[...], p0, scale0, left)
        add(p1, scale1, v_all[:, before], right)
        scores(s0, k_all[after, :], left)
        weigh(s1[...], p1, scale1, right)
        add(p0, scale0, v_all[:, here], left)

    add(p1, scale1, v_all[:, chunk(count - 1)], right)
    if not last:
        return
    for s in range(8):
        rows = pl.ds(s * TOK, TOK)
        fresh = new_refs[s][0:TOK, :]
        new_k[rows, 0:HD] = fresh
        new_k[rows, HD : 2 * HD] = fresh
        new_v[rows, :] = new_refs[s][TOK : 2 * TOK, :]
    ones16 = jnp.where(row16[:, 0:CHUNK] == 0, 1.0, 0.0).astype(BF16)
    values = jnp.concatenate([new_v[...].T, ones16], axis=0)
    scores(s0, new_k[...], left)
    scores(s1, new_k[...], right)
    ranks = k_rank[:, 0:1]
    weigh(jnp.where(ranks <= q_rank[:, left], s0[...], NEG_FILL), p0, scale0, left)
    add(p0, scale0, values, left)
    weigh(jnp.where(ranks <= q_rank[:, right], s1[...], NEG_FILL), p1, scale1, right)
    add(p1, scale1, values, right)
    for b in range(BLOCKS):
        stats = []
        for h in range(QPH):
            cols = slice(b * ROWS + h * TOK, b * ROWS + (h + 1) * TOK)
            held = acc[:, cols]
            weight = held[HD : HD + 1, :]
            out_refs[b][:, h * HD : (h + 1) * HD] = (held[0:HD, :] / weight).T.astype(BF16)
            stats.append(m_all[:, cols] + jnp.log2(weight))
        stats = jnp.concatenate(stats, axis=0)
        high = stats.astype(BF16).astype(F32)
        middle = (stats - high).astype(BF16).astype(F32)
        low = stats - high - middle
        stats = jnp.concatenate([high, middle, low, jnp.zeros((104, TOK), F32)], axis=0)
        out_refs[b][:, QPH * HD : WIDE] = stats.T.astype(BF16)


def attention(q_blocks, shards, state=None, new=None, q_rank=None, k_rank=None):
    first, last = state is None, new is not None
    m_shape, acc_shape = (1, BLOCKS * ROWS), (VROWS, BLOCKS * ROWS)
    args = [*q_blocks, *shards]
    whole = pl.BlockSpec(memory_space=pltpu.VMEM)
    specs = [whole] * len(args)
    if not first:
        args += state
        specs += [whole] * 2
    keys = len(shards) * CACHE + CHUNK
    scratch = [
        pltpu.VMEM((BLOCKS * ROWS, 2 * HD), BF16),
        pltpu.VMEM((keys, 2 * HD), BF16),
        pltpu.VMEM((VROWS, keys), BF16),
        pltpu.VMEM((CHUNK, TILE), F32),
        pltpu.VMEM((CHUNK, TILE), F32),
        pltpu.VMEM((CHUNK, TILE), BF16),
        pltpu.VMEM((CHUNK, TILE), BF16),
        pltpu.VMEM((1, TILE), F32),
        pltpu.VMEM((1, TILE), F32),
    ]
    if last:
        args += [*new, q_rank, k_rank]
        specs += [pl.BlockSpec((2 * TOK, HD), lambda i: (0, 0))] * 8 + [whole] * 2
        out_shape = [jax.ShapeDtypeStruct((TOK, WIDE), BF16)] * BLOCKS
        out_specs = [whole] * BLOCKS
        scratch = [
            pltpu.VMEM(m_shape, F32),
            pltpu.VMEM(acc_shape, F32),
            *scratch,
            pltpu.VMEM((8 * TOK, 2 * HD), BF16),
            pltpu.VMEM((8 * TOK, HD), BF16),
        ]
    else:
        out_shape = [jax.ShapeDtypeStruct(m_shape, F32), jax.ShapeDtypeStruct(acc_shape, F32)]
        out_specs = [whole] * 2
    return pl.pallas_call(
        functools.partial(attention_kernel, len(shards), first, last),
        grid=(1,),
        out_shape=out_shape,
        in_specs=specs,
        out_specs=out_specs,
        scratch_shapes=scratch,
        compiler_params=pltpu.CompilerParams(vmem_limit_bytes=56 * 2**20),
        name="attention",
    )(*args)


def merge_kernel(*refs):
    parts, out_ref = refs[:BLOCKS], refs[BLOCKS]
    stats = []
    for b in range(BLOCKS):
        lanes = parts[b][:, QPH * HD : WIDE].astype(F32)
        stats.append(lanes[:, 0:8] + lanes[:, 8:16] + lanes[:, 16:24])
    top = functools.reduce(jnp.maximum, stats)
    shares = [jnp.exp2(s - top) for s in stats]
    whole = functools.reduce(jnp.add, shares)
    shares = [s / whole for s in shares]
    for h in range(QPH):
        cols = slice(h * HD, (h + 1) * HD)
        out_ref[:, cols] = functools.reduce(
            jnp.add,
            [parts[b][:, cols].astype(F32) * shares[b][:, h : h + 1] for b in range(BLOCKS)],
        ).astype(BF16)


def merge(parts):
    return pl.pallas_call(
        merge_kernel,
        out_shape=jax.ShapeDtypeStruct((TOK, QPH * HD), BF16),
        name="merge",
    )(*parts)


def product_kernel(place_ref, *refs):
    blocks, weights, out_ref, every = refs[:8], refs[8:12], refs[12], refs[13]
    z, yc = place_ref[0], place_ref[1]
    for k in range(Z):
        every[(z + k) % Z] = blocks[k][...]
    rows = every[...].reshape(Z * TOK, QPH * HD)
    for r in range(YC):
        part = jnp.dot(rows, weights[r][...], preferred_element_type=F32)
        out_ref[:, yc ^ r] = part.astype(BF16).reshape(Z, TOK, 256)


def product(place, blocks, weights):
    whole = pl.BlockSpec(memory_space=pltpu.VMEM)
    return pl.pallas_call(
        product_kernel,
        out_shape=jax.ShapeDtypeStruct((Z, YC, TOK, 256), BF16),
        in_specs=[pl.BlockSpec(memory_space=pltpu.SMEM)] + [whole] * 12,
        out_specs=whole,
        scratch_shapes=[pltpu.VMEM((Z, TOK, QPH * HD), BF16)],
        compiler_params=pltpu.CompilerParams(vmem_limit_bytes=56 * 2**20),
        name="product",
    )(place, *blocks, *weights)


def body(queries, cache_keys, cache_values, new_keys, new_values, cache_len, span_rank, out_weight):
    seq = lax.axis_index("seq")
    z, yc = seq // YC, seq % YC
    y, c = yc // 2, yc % 2

    own = pack(cache_len, cache_keys, cache_values, new_keys, new_values)
    over_c = lambda v: seq_permute(v, lambda z, y, c: (z, y, 1 - c))
    over_y = lambda v: seq_permute(v, lambda z, y, c: (z, 1 - y, c))
    over_z = lambda v: seq_permute(v, lambda z, y, c: (z ^ 1, y, c))
    shift = lambda v, n: seq_permute(v, lambda z, y, c: (z + n, y, c))

    kv_y = over_y(own)
    own_pair = (own, over_c(own))
    q_blocks = (shift(queries, 4), shift(queries, -2), shift(queries, 2), queries)
    sent, *q_blocks = lax.optimization_barrier((own, *q_blocks))
    kv_z = over_z(sent)
    kv_yz = over_z(kv_y)

    ranks = span_rank.reshape(Z, 2, 2, TOK)
    flip = lambda a, on, dim: jnp.where(on == 1, jnp.flip(a, dim), a)
    near = lax.dynamic_slice_in_dim(ranks, (z // 2) * 2, 2, 0)
    near = flip(flip(flip(near, z % 2, 0), y, 1), c, 2)
    k_rank = jnp.stack([near[0, 0], near[0, 1], near[1, 0], near[1, 1]]).reshape(8 * TOK, 1)
    k_rank = jnp.broadcast_to(k_rank, (8 * TOK, HD))
    by_z = lax.dynamic_index_in_dim(span_rank.reshape(Z, YC, TOK), yc, 1, False)
    steps = (z + jnp.array([4, 2, 6, 0])) % Z
    q_rank = jnp.tile(by_z[steps], (1, QPH)).reshape(1, BLOCKS * ROWS)

    y_pair = (kv_y, over_c(kv_y))
    state = attention(q_blocks, (*own_pair, *y_pair))
    kv_z, kv_yz, *state = lax.optimization_barrier((kv_z, kv_yz, *state))
    z_pair = (kv_z, over_c(kv_z))
    yz_pair = (kv_yz, over_c(kv_yz))
    state = attention(q_blocks, z_pair, state)
    new = (*own_pair, *y_pair, *z_pair, *yz_pair)
    far, up, down, mine = attention(q_blocks, yz_pair, state, new, q_rank, k_rank)
    attended = merge((shift(far, 4), shift(up, 2), shift(down, -2), mine))

    weight = lax.optimization_barrier((out_weight, kv_yz))[0]
    weight_y = over_y(weight)
    weights = [out_weight, over_c(weight), weight_y, over_c(weight_y)]

    blocks = [None] * Z
    blocks[0] = attended
    for k in (1, 2, 3):
        blocks[k] = shift(blocks[k - 1], -1)
        blocks[Z - k] = shift(blocks[(Z - k + 1) % Z], 1)
    blocks[4] = shift(blocks[3], -1)
    shares = product(jnp.stack([z, yc]), blocks, weights)
    shares = lax.all_to_all(shares, "head", 0, 0, tiled=True)
    projected = jnp.sum(shares.astype(F32), axis=0).astype(BF16)
    projected = lax.all_to_all(projected, "seq", 0, 0, axis_index_groups=PLANES, tiled=True)
    return projected.reshape(YC * TOK, 256)


def solution(mesh):
    return jax.shard_map(
        body,
        mesh=mesh,
        in_specs=(
            P("seq", "head"),
            P("head", "seq", None),
            P("head", "seq", None),
            P("seq", "head"),
            P("seq", "head"),
            P("seq"),
            P(),
            P("head", "seq"),
        ),
        out_specs=P("head", "seq"),
        check_vma=False,
    )
```

profile of v0, /device:TPU:1, one launch (start us, length us, event | category | flops | bytes accessed | tf_op | source)
XLA Modules:
  0.0 155.5 jit_solution(15848226937327086515)
XLA Ops:
  0.7 1.9 %pack.1.refs_4_.refs_8_ = bf16[2192,128]{1,0:T(8,128)(2,1)} custom-call(s32[1]{0:T(128)S(6)} %copy.11.length_ref, bf16[1,1024,128]{2,1,0:T(8,128)(2,1)} %k_ref.1, bf16[1,1024,128]{2,1,0:T(8,128)(2,1)} %v_ref.1, bf16[64,128]{1,0:T(8,128)(2,1)} %nk_ref.1, bf16[64,128]{1,0:T(8,128)(2,1)} %nv_ref.1), custom_call_target="tpu_custom_call" | custom-call | tf_op jit(solution)/shard_map/pack/pallas_call | solution.py:55
  2.5 2.1 %collective-permute-start.4 = (bf16[2192,128]{1,0:T(8,128)(2,1)}, bf16[2192,128]{1,0:T(8,128)(2,1)S(1)}, u32[]{:S(2)}, u32[]{:S(2)}) collective-permute-start(bf16[2192,128]{1,0:T(8,128)(2,1)} %pack.1.refs_4_.refs_8_), channel_id=1, source_target_pairs={{0,16},{8,24},{16,0},{24,8},{32,48},{40,56},{48,32},{56,40},{64,80... | collective-permute-start | bytes 1683464 | tf_op jit(solution)/shard_map/ppermute | solution.py:39
  4.7 6.9 %collective-permute-start = (bf16[64,1024]{1,0:T(8,128)(2,1)}, bf16[64,1024]{1,0:T(8,128)(2,1)S(1)}, u32[]{:S(2)}, u32[]{:S(2)}) collective-permute-start(bf16[64,1024]{1,0:T(8,128)(2,1)} %refs_3_.2), channel_id=1, source_target_pairs={{0,128},{8,136},{16,144},{24,152},{32,160},{40,168},{48,176},{56,1... | collective-permute-start | bytes 393224 | tf_op jit(solution)/shard_map/ppermute | solution.py:39
  11.6 2.4 %collective-permute-start.2 = (bf16[64,1024]{1,0:T(8,128)(2,1)}, bf16[64,1024]{1,0:T(8,128)(2,1)S(1)}, u32[]{:S(2)}, u32[]{:S(2)}) collective-permute-start(bf16[64,1024]{1,0:T(8,128)(2,1)} %refs_3_.2), channel_id=1, source_target_pairs={{0,64},{8,72},{16,80},{24,88},{32,96},{40,104},{48,112},{56,120},{... | collective-permute-start | bytes 393224 | tf_op jit(solution)/shard_map/ppermute | solution.py:39
  13.9 1.8 %collective-permute-start.6 = (bf16[2192,128]{1,0:T(8,128)(2,1)}, bf16[2192,128]{1,0:T(8,128)(2,1)S(1)}, u32[]{:S(2)}, u32[]{:S(2)}) collective-permute-start(bf16[2192,128]{1,0:T(8,128)(2,1)} %pack.1.refs_4_.refs_8_), channel_id=1, source_target_pairs={{0,8},{8,0},{16,24},{24,16},{32,40},{40,32},{48,56},{56,48},{64,72... | collective-permute-start | bytes 1683464 | tf_op jit(solution)/shard_map/ppermute | solution.py:39
  15.7 0.1 reshape.18
  15.9 8.8 %collective-permute-done.1.refs_1_ = bf16[64,1024]{1,0:T(8,128)(2,1)S(1)} collective-permute-done((bf16[64,1024]{1,0:T(8,128)(2,1)}, bf16[64,1024]{1,0:T(8,128)(2,1)S(1)}, u32[]{:S(2)}, u32[]{:S(2)}) %collective-permute-start.1) | collective-permute-done | bytes 131104 | tf_op jit(solution)/shard_map/ppermute | solution.py:39
  24.7 0.1 collective-permute-start.3
  24.8 0.8 collective-permute-start.7
  25.6 1.5 collective-permute-start.5
  27.3 0.7 copy-done.3
  28.0 0.8 copy-done.5
  28.8 14.5 %attention.3 = (f32[1,2048]{1,0:T(1,128)}, f32[144,2048]{1,0:T(8,128)}) custom-call(bf16[64,1024]{1,0:T(8,128)(2,1)} %copy-done.7, bf16[64,1024]{1,0:T(8,128)(2,1)} %copy-done.8, bf16[64,1024]{1,0:T(8,128)(2,1)} %copy-done.9, bf16[64,1024]{1,0:T(8,128)(2,1)} %refs_3_.2, bf16[2192,128]{1,0:T(8,128)(2,1)} %pack.1.refs_4_.refs_8_, bf16[2192,128]{1,0:T(8,128)(2,1)} %copy-done.3, ...), custom_call_target="tpu_custom_call" | custom-call | tf_op jit(solution)/shard_map/attention/pallas_call | solution.py:224
  43.3 7.4 %collective-permute-done.5.refs_4_.refs_14_ = bf16[2192,128]{1,0:T(8,128)(2,1)S(1)} collective-permute-done((bf16[2192,128]{1,0:T(8,128)(2,1)S(1)}, bf16[2192,128]{1,0:T(8,128)(2,1)S(1)}, u32[]{:S(2)}, u32[]{:S(2)}) %collective-permute-start.5) | collective-permute-done | bytes 561184 | tf_op jit(solution)/shard_map/ppermute | solution.py:39
  50.7 1.4 collective-permute-start.9
  52.1 0.1 broadcast_in_dim.11
  52.2 0.2 collective-permute-start.21
  52.5 0.6 gather_fusion
  53.0 0.7 tile.9.refs_16_
  53.7 0.8 copy-done.6
  54.5 9.4 %attention.4 = (f32[1,2048]{1,0:T(1,128)}, f32[144,2048]{1,0:T(8,128)}) custom-call(bf16[64,1024]{1,0:T(8,128)(2,1)} %copy-done.7, bf16[64,1024]{1,0:T(8,128)(2,1)} %copy-done.8, bf16[64,1024]{1,0:T(8,128)(2,1)} %copy-done.9, bf16[64,1024]{1,0:T(8,128)(2,1)} %refs_3_.2, bf16[2192,128]{1,0:T(8,128)(2,1)} %copy-done.4, bf16[2192,128]{1,0:T(8,128)(2,1)} %copy-done.6, ...), custom_call_target="tpu_custom_call" | custom-call | tf_op jit(solution)/shard_map/attention/pallas_call | solution.py:224
  64.0 0.9 broadcast_in_dim.12.refs_17_
  64.9 11.2 %attention.5 = (bf16[64,1152]{1,0:T(8,128)(2,1)}, bf16[64,1152]{1,0:T(8,128)(2,1)}, bf16[64,1152]{1,0:T(8,128)(2,1)}, bf16[64,1152]{1,0:T(8,128)(2,1)}) custom-call(bf16[64,1024]{1,0:T(8,128)(2,1)} %copy-done.7, bf16[64,1024]{1,0:T(8,128)(2,1)} %copy-done.8, bf16[64,1024]{1,0:T(8,128)(2,1)} %copy-done.9, bf16[64,1024]{1,0:T(8,128)(2,1)} %refs_3_.2, ...), custom_call_target="tpu_custom_call" | custom-call | tf_op jit(solution)/shard_map/attention/pallas_call | solution.py:224
  76.1 5.3 %collective-permute-start.10 = (bf16[64,1152]{1,0:T(8,128)(2,1)}, bf16[64,1152]{1,0:T(8,128)(2,1)S(1)}, u32[]{:S(2)}, u32[]{:S(2)}) collective-permute-start(bf16[64,1152]{1,0:T(8,128)(2,1)} %get-tuple-element.36), channel_id=1, source_target_pairs={{0,128},{8,136},{16,144},{24,152},{32,160},{40,168},{48,176},{56,1... | collective-permute-start | bytes 442376 | tf_op jit(solution)/shard_map/ppermute | solution.py:39
  81.4 2.5 %collective-permute-start.11 = (bf16[64,1152]{1,0:T(8,128)(2,1)}, bf16[64,1152]{1,0:T(8,128)(2,1)S(1)}, u32[]{:S(2)}, u32[]{:S(2)}) collective-permute-start(bf16[64,1152]{1,0:T(8,128)(2,1)} %get-tuple-element.37), channel_id=1, source_target_pairs={{0,64},{8,72},{16,80},{24,88},{32,96},{40,104},{48,112},{56,120},{... | collective-permute-start | bytes 442376 | tf_op jit(solution)/shard_map/ppermute | solution.py:39
  83.9 1.1 collective-permute-start.12
  85.0 1.6 %collective-permute-start.20 = (bf16[1024,256]{1,0:T(8,128)(2,1)S(1)}, bf16[1024,256]{1,0:T(8,128)(2,1)S(1)}, u32[]{:S(2)}, u32[]{:S(2)}) collective-permute-start(bf16[1024,256]{1,0:T(8,128)(2,1)S(1)} %copy-done.10), channel_id=1, source_target_pairs={{0,8},{8,0},{16,24},{24,16},{32,40},{40,32},{48,56},{56,48},{64,72... | collective-permute-start | bytes 1572872 | tf_op jit(solution)/shard_map/ppermute | solution.py:39
  86.6 8.1 %collective-permute-done.11.refs_1_ = bf16[64,1152]{1,0:T(8,128)(2,1)S(1)} collective-permute-done((bf16[64,1152]{1,0:T(8,128)(2,1)}, bf16[64,1152]{1,0:T(8,128)(2,1)S(1)}, u32[]{:S(2)}, u32[]{:S(2)}) %collective-permute-start.11) | collective-permute-done | bytes 147488 | tf_op jit(solution)/shard_map/ppermute | solution.py:39
  94.7 1.6 %collective-permute-done.12.refs_2_ = bf16[64,1152]{1,0:T(8,128)(2,1)S(1)} collective-permute-done((bf16[64,1152]{1,0:T(8,128)(2,1)}, bf16[64,1152]{1,0:T(8,128)(2,1)S(1)}, u32[]{:S(2)}, u32[]{:S(2)}) %collective-permute-start.12) | collective-permute-done | bytes 147488 | tf_op jit(solution)/shard_map/ppermute | solution.py:39
  96.3 0.6 copy-done.16
  96.9 2.3 %merge.1.refs_0_ = bf16[64,1024]{1,0:T(8,128)(2,1)} custom-call(bf16[64,1152]{1,0:T(8,128)(2,1)} %copy-done.14, bf16[64,1152]{1,0:T(8,128)(2,1)} %copy-done.15, bf16[64,1152]{1,0:T(8,128)(2,1)} %copy-done.16, bf16[64,1152]{1,0:T(8,128)(2,1)} %get-tuple-element.39.refs_3_), custom_call_target="tpu_custom_call" | custom-call | tf_op jit(solution)/shard_map/merge/pallas_call | solution.py:255
  99.2 1.6 %collective-permute-start.22 = (bf16[1024,256]{1,0:T(8,128)(2,1)S(1)}, bf16[1024,256]{1,0:T(8,128)(2,1)S(1)}, u32[]{:S(2)}, u32[]{:S(2)}) collective-permute-start(bf16[1024,256]{1,0:T(8,128)(2,1)S(1)} %collective-permute-done.21.refs_10_), channel_id=1, source_target_pairs={{0,8},{8,0},{16,24},{24,16},{32,40},{40,32},{48,56},{56,48},{64,72... | collective-permute-start | bytes 1572872 | tf_op jit(solution)/shard_map/ppermute | solution.py:39
  100.8 1.2 collective-permute-start.17
  102.0 1.2 collective-permute-done.13.refs_1_
  103.2 2.8 %collective-permute-start.14 = (bf16[64,1024]{1,0:T(8,128)(2,1)S(1)}, bf16[64,1024]{1,0:T(8,128)(2,1)S(1)}, u32[]{:S(2)}, u32[]{:S(2)}) collective-permute-start(bf16[64,1024]{1,0:T(8,128)(2,1)S(1)} %collective-permute-done.13.refs_1_), channel_id=1, source_target_pairs={{0,224},{8,232},{16,240},{24,248},{32,0},{40,8},{48,16},{56,24},{6... | collective-permute-start | bytes 393224 | tf_op jit(solution)/shard_map/ppermute | solution.py:39
  106.0 2.1 %collective-permute-done.17.refs_7_ = bf16[64,1024]{1,0:T(8,128)(2,1)S(1)} collective-permute-done((bf16[64,1024]{1,0:T(8,128)(2,1)}, bf16[64,1024]{1,0:T(8,128)(2,1)S(1)}, u32[]{:S(2)}, u32[]{:S(2)}) %collective-permute-start.17) | collective-permute-done | bytes 131104 | tf_op jit(solution)/shard_map/ppermute | solution.py:39
  108.1 2.9 %collective-permute-start.15 = (bf16[64,1024]{1,0:T(8,128)(2,1)S(1)}, bf16[64,1024]{1,0:T(8,128)(2,1)S(1)}, u32[]{:S(2)}, u32[]{:S(2)}) collective-permute-start(bf16[64,1024]{1,0:T(8,128)(2,1)S(1)} %collective-permute-done.14.refs_2_), channel_id=1, source_target_pairs={{0,224},{8,232},{16,240},{24,248},{32,0},{40,8},{48,16},{56,24},{6... | collective-permute-start | bytes 393224 | tf_op jit(solution)/shard_map/ppermute | solution.py:39
  111.0 2.6 %collective-permute-done.18.refs_6_ = bf16[64,1024]{1,0:T(8,128)(2,1)S(1)} collective-permute-done((bf16[64,1024]{1,0:T(8,128)(2,1)S(1)}, bf16[64,1024]{1,0:T(8,128)(2,1)S(1)}, u32[]{:S(2)}, u32[]{:S(2)}) %collective-permute-start.18) | collective-permute-done | bytes 131104 | tf_op jit(solution)/shard_map/ppermute | solution.py:39
  113.7 2.7 %collective-permute-start.16 = (bf16[64,1024]{1,0:T(8,128)(2,1)S(1)}, bf16[64,1024]{1,0:T(8,128)(2,1)S(1)}, u32[]{:S(2)}, u32[]{:S(2)}) collective-permute-start(bf16[64,1024]{1,0:T(8,128)(2,1)S(1)} %collective-permute-done.15.refs_3_), channel_id=1, source_target_pairs={{0,224},{8,232},{16,240},{24,248},{32,0},{40,8},{48,16},{56,24},{6... | collective-permute-start | bytes 393224 | tf_op jit(solution)/shard_map/ppermute | solution.py:39
  116.4 0.6 pad_add_fusion.1.place_ref
  117.0 1.7 %collective-permute-done.19.refs_5_ = bf16[64,1024]{1,0:T(8,128)(2,1)S(1)} collective-permute-done((bf16[64,1024]{1,0:T(8,128)(2,1)S(1)}, bf16[64,1024]{1,0:T(8,128)(2,1)S(1)}, u32[]{:S(2)}, u32[]{:S(2)}) %collective-permute-start.19) | collective-permute-done | bytes 131104 | tf_op jit(solution)/shard_map/ppermute | solution.py:39
  118.8 0.6 copy-done.22
  119.4 0.7 copy-done.23
  120.0 4.3 %product.1 = bf16[8,4,64,256]{3,2,1,0:T(8,128)(2,1)} custom-call(s32[2]{0:T(128)} %pad_add_fusion.1.place_ref, bf16[64,1024]{1,0:T(8,128)(2,1)} %merge.1.refs_0_, bf16[64,1024]{1,0:T(8,128)(2,1)} %copy-done.17, bf16[64,1024]{1,0:T(8,128)(2,1)} %copy-done.19, bf16[64,1024]{1,0:T(8,128)(2,1)} %copy-done.21, bf16[64,1024]{1,0:T(8,128)(2,1)} %copy-done.23, ...), custom_call_target="tpu_custom_call" | custom-call | tf_op jit(solution)/shard_map/product/pallas_call | solution.py:275
  124.3 19.3 %all_to_all.10 = bf16[8,4,64,256]{3,2,1,0:T(8,128)(2,1)S(1)} all-to-all(bf16[8,4,64,256]{3,2,1,0:T(8,128)(2,1)} %product.1), channel_id=1, replica_groups=mesh['seq'=32,'head'=8] {'head'}, dimensions={0} | all-to-all | bytes 2097152 | tf_op jit(solution)/shard_map/all_to_all | solution.py:335
  143.6 0.1 reduce_sum.12
  143.8 11.1 %all_to_all.11 = bf16[4,64,256]{2,1,0:T(8,128)(2,1)S(1)} all-to-all(bf16[4,64,256]{2,1,0:T(8,128)(2,1)S(1)} %reduce_sum.12), channel_id=1, replica_groups={{0,8,16,24},{32,40,48,56},{64,72,80,88},{96,104,112,120},{128,136,144,1..., dimensions={0} | all-to-all | bytes 262144 | tf_op jit(solution)/shard_map/all_to_all | solution.py:337
  154.9 0.7 copy.12
  (78 shorter events, 0.3 us)
Async XLA Ops:
  0.0 15.7 %copy-start.24 = (s32[2048]{0:T(1024)S(1)}, s32[2048]{0:T(1024)}, u32[]{:S(2)}) copy-start(s32[2048]{0:T(1024)} %param.15) | copy-start | bytes 24580
  2.5 22.2 %collective-permute-start.4 = (bf16[2192,128]{1,0:T(8,128)(2,1)}, bf16[2192,128]{1,0:T(8,128)(2,1)S(1)}, u32[]{:S(2)}, u32[]{:S(2)}) collective-permute-start(bf16[2192,128]{1,0:T(8,128)(2,1)} %pack.1.refs_4_.refs_8_), channel_id=1, source_target_pairs={{0,16},{8,24},{16,0},{24,8},{32,48},{40,56},{48,32},{56,40},{64,80... | collective-permute-start | bytes 1683464 | tf_op jit(solution)/shard_map/ppermute | solution.py:39
  4.7 11.2 %collective-permute-start = (bf16[64,1024]{1,0:T(8,128)(2,1)}, bf16[64,1024]{1,0:T(8,128)(2,1)S(1)}, u32[]{:S(2)}, u32[]{:S(2)}) collective-permute-start(bf16[64,1024]{1,0:T(8,128)(2,1)} %refs_3_.2), channel_id=1, source_target_pairs={{0,128},{8,136},{16,144},{24,152},{32,160},{40,168},{48,176},{56,1... | collective-permute-start | bytes 393224 | tf_op jit(solution)/shard_map/ppermute | solution.py:39
  11.6 13.1 %collective-permute-start.1 = (bf16[64,1024]{1,0:T(8,128)(2,1)}, bf16[64,1024]{1,0:T(8,128)(2,1)S(1)}, u32[]{:S(2)}, u32[]{:S(2)}) collective-permute-start(bf16[64,1024]{1,0:T(8,128)(2,1)} %refs_3_.2), channel_id=1, source_target_pairs={{0,192},{8,200},{16,208},{24,216},{32,224},{40,232},{48,240},{56,2... | collective-permute-start | bytes 393224 | tf_op jit(solution)/shard_map/ppermute | solution.py:39
  11.6 13.1 %collective-permute-start.2 = (bf16[64,1024]{1,0:T(8,128)(2,1)}, bf16[64,1024]{1,0:T(8,128)(2,1)S(1)}, u32[]{:S(2)}, u32[]{:S(2)}) collective-permute-start(bf16[64,1024]{1,0:T(8,128)(2,1)} %refs_3_.2), channel_id=1, source_target_pairs={{0,64},{8,72},{16,80},{24,88},{32,96},{40,104},{48,112},{56,120},{... | collective-permute-start | bytes 393224 | tf_op jit(solution)/shard_map/ppermute | solution.py:39
  13.9 13.3 %collective-permute-start.6 = (bf16[2192,128]{1,0:T(8,128)(2,1)}, bf16[2192,128]{1,0:T(8,128)(2,1)S(1)}, u32[]{:S(2)}, u32[]{:S(2)}) collective-permute-start(bf16[2192,128]{1,0:T(8,128)(2,1)} %pack.1.refs_4_.refs_8_), channel_id=1, source_target_pairs={{0,8},{8,0},{16,24},{24,16},{32,40},{40,32},{48,56},{56,48},{64,72... | collective-permute-start | bytes 1683464 | tf_op jit(solution)/shard_map/ppermute | solution.py:39
  15.8 11.4 %copy-start.7 = (bf16[64,1024]{1,0:T(8,128)(2,1)}, bf16[64,1024]{1,0:T(8,128)(2,1)S(1)}, u32[]{:S(2)}) copy-start(bf16[64,1024]{1,0:T(8,128)(2,1)S(1)} %collective-permute-done.refs_0_) | copy-start | bytes 393220
  24.7 2.6 %copy-start.8 = (bf16[64,1024]{1,0:T(8,128)(2,1)}, bf16[64,1024]{1,0:T(8,128)(2,1)S(1)}, u32[]{:S(2)}) copy-start(bf16[64,1024]{1,0:T(8,128)(2,1)S(1)} %collective-permute-done.1.refs_1_) | copy-start | bytes 393220
  24.7 2.6 %copy-start.9 = (bf16[64,1024]{1,0:T(8,128)(2,1)}, bf16[64,1024]{1,0:T(8,128)(2,1)S(1)}, u32[]{:S(2)}) copy-start(bf16[64,1024]{1,0:T(8,128)(2,1)S(1)} %collective-permute-done.2.refs_2_) | copy-start | bytes 393220
  24.7 18.7 %collective-permute-start.3 = (bf16[2192,128]{1,0:T(8,128)(2,1)}, bf16[2192,128]{1,0:T(8,128)(2,1)S(1)}, u32[]{:S(2)}, u32[]{:S(2)}) collective-permute-start(bf16[2192,128]{1,0:T(8,128)(2,1)} %pack.1.refs_4_.refs_8_), channel_id=1, source_target_pairs={{0,32},{8,40},{16,48},{24,56},{32,0},{40,8},{48,16},{56,24},{64,96... | collective-permute-start | bytes 1683464 | tf_op jit(solution)/shard_map/ppermute | solution.py:39
  24.8 2.5 %copy-start.2 = (bf16[2192,128]{1,0:T(8,128)(2,1)}, bf16[2192,128]{1,0:T(8,128)(2,1)S(1)}, u32[]{:S(2)}) copy-start(bf16[2192,128]{1,0:T(8,128)(2,1)S(1)} %collective-permute-done.4.refs_6_.refs_10_) | copy-start | bytes 1683460
  24.8 2.5 %collective-permute-start.7 = (bf16[2192,128]{1,0:T(8,128)(2,1)S(1)}, bf16[2192,128]{1,0:T(8,128)(2,1)S(1)}, u32[]{:S(2)}, u32[]{:S(2)}) collective-permute-start(bf16[2192,128]{1,0:T(8,128)(2,1)S(1)} %collective-permute-done.4.refs_6_.refs_10_), channel_id=1, source_target_pairs={{0,8},{8,0},{16,24},{24,16},{32,40},{40,32},{48,56},{56,48},{64,72... | collective-permute-start | bytes 1683464 | tf_op jit(solution)/shard_map/ppermute | solution.py:39
  25.6 25.1 %collective-permute-start.5 = (bf16[2192,128]{1,0:T(8,128)(2,1)S(1)}, bf16[2192,128]{1,0:T(8,128)(2,1)S(1)}, u32[]{:S(2)}, u32[]{:S(2)}) collective-permute-start(bf16[2192,128]{1,0:T(8,128)(2,1)S(1)} %collective-permute-done.4.refs_6_.refs_10_), channel_id=1, source_target_pairs={{0,32},{8,40},{16,48},{24,56},{32,0},{40,8},{48,16},{56,24},{64,96... | collective-permute-start | bytes 1683464 | tf_op jit(solution)/shard_map/ppermute | solution.py:39
  27.2 25.2 %copy-start.25 = (s32[4]{0:T(128)S(1)}, s32[4]{0:T(128)}, u32[]{:S(2)}) copy-start(s32[4]{0:T(128)} %constant.86.clone) | copy-start | bytes 52
  27.2 0.8 copy-start.3
  28.0 0.8 copy-start.5
  43.3 10.4 %copy-start.4 = (bf16[2192,128]{1,0:T(8,128)(2,1)}, bf16[2192,128]{1,0:T(8,128)(2,1)S(1)}, u32[]{:S(2)}) copy-start(bf16[2192,128]{1,0:T(8,128)(2,1)S(1)} %collective-permute-done.3.refs_4_.refs_12_) | copy-start | bytes 1683460
  50.7 13.2 %copy-start = (bf16[2192,128]{1,0:T(8,128)(2,1)}, bf16[2192,128]{1,0:T(8,128)(2,1)S(1)}, u32[]{:S(2)}) copy-start(bf16[2192,128]{1,0:T(8,128)(2,1)S(1)} %collective-permute-done.5.refs_4_.refs_14_) | copy-start | bytes 1683460
  50.7 3.0 %collective-permute-start.9 = (bf16[2192,128]{1,0:T(8,128)(2,1)S(1)}, bf16[2192,128]{1,0:T(8,128)(2,1)S(1)}, u32[]{:S(2)}, u32[]{:S(2)}) collective-permute-start(bf16[2192,128]{1,0:T(8,128)(2,1)S(1)} %collective-permute-done.3.refs_4_.refs_12_), channel_id=1, source_target_pairs={{0,8},{8,0},{16,24},{24,16},{32,40},{40,32},{48,56},{56,48},{64,72... | collective-permute-start | bytes 1683464 | tf_op jit(solution)/shard_map/ppermute | solution.py:39
  52.1 11.8 %collective-permute-start.8 = (bf16[2192,128]{1,0:T(8,128)(2,1)S(1)}, bf16[2192,128]{1,0:T(8,128)(2,1)S(1)}, u32[]{:S(2)}, u32[]{:S(2)}) collective-permute-start(bf16[2192,128]{1,0:T(8,128)(2,1)S(1)} %collective-permute-done.5.refs_4_.refs_14_), channel_id=1, source_target_pairs={{0,8},{8,0},{16,24},{24,16},{32,40},{40,32},{48,56},{56,48},{64,72... | collective-permute-start | bytes 1683464 | tf_op jit(solution)/shard_map/ppermute | solution.py:39
  52.2 47.0 %collective-permute-start.21 = (bf16[1024,256]{1,0:T(8,128)(2,1)}, bf16[1024,256]{1,0:T(8,128)(2,1)S(1)}, u32[]{:S(2)}, u32[]{:S(2)}) collective-permute-start(bf16[1024,256]{1,0:T(8,128)(2,1)} %refs_8_.1), channel_id=1, source_target_pairs={{0,16},{8,24},{16,0},{24,8},{32,48},{40,56},{48,32},{56,40},{64,80... | collective-permute-start | bytes 1572872 | tf_op jit(solution)/shard_map/ppermute | solution.py:39
  53.7 0.8 copy-start.6
  64.0 0.9 copy-start.1
  64.9 20.1 %copy-start.10 = (bf16[1024,256]{1,0:T(8,128)(2,1)S(1)}, bf16[1024,256]{1,0:T(8,128)(2,1)}, u32[]{:S(2)}) copy-start(bf16[1024,256]{1,0:T(8,128)(2,1)} %refs_8_.1) | copy-start | bytes 1572868
  76.1 10.5 %collective-permute-start.10 = (bf16[64,1152]{1,0:T(8,128)(2,1)}, bf16[64,1152]{1,0:T(8,128)(2,1)S(1)}, u32[]{:S(2)}, u32[]{:S(2)}) collective-permute-start(bf16[64,1152]{1,0:T(8,128)(2,1)} %get-tuple-element.36), channel_id=1, source_target_pairs={{0,128},{8,136},{16,144},{24,152},{32,160},{40,168},{48,176},{56,1... | collective-permute-start | bytes 442376 | tf_op jit(solution)/shard_map/ppermute | solution.py:39
  81.4 13.3 %collective-permute-start.11 = (bf16[64,1152]{1,0:T(8,128)(2,1)}, bf16[64,1152]{1,0:T(8,128)(2,1)S(1)}, u32[]{:S(2)}, u32[]{:S(2)}) collective-permute-start(bf16[64,1152]{1,0:T(8,128)(2,1)} %get-tuple-element.37), channel_id=1, source_target_pairs={{0,64},{8,72},{16,80},{24,88},{32,96},{40,104},{48,112},{56,120},{... | collective-permute-start | bytes 442376 | tf_op jit(solution)/shard_map/ppermute | solution.py:39
  83.9 12.4 %collective-permute-start.12 = (bf16[64,1152]{1,0:T(8,128)(2,1)}, bf16[64,1152]{1,0:T(8,128)(2,1)S(1)}, u32[]{:S(2)}, u32[]{:S(2)}) collective-permute-start(bf16[64,1152]{1,0:T(8,128)(2,1)} %get-tuple-element.38), channel_id=1, source_target_pairs={{0,192},{8,200},{16,208},{24,216},{32,224},{40,232},{48,240},{56,2... | collective-permute-start | bytes 442376 | tf_op jit(solution)/shard_map/ppermute | solution.py:39
  85.0 32.0 %collective-permute-start.20 = (bf16[1024,256]{1,0:T(8,128)(2,1)S(1)}, bf16[1024,256]{1,0:T(8,128)(2,1)S(1)}, u32[]{:S(2)}, u32[]{:S(2)}) collective-permute-start(bf16[1024,256]{1,0:T(8,128)(2,1)S(1)} %copy-done.10), channel_id=1, source_target_pairs={{0,8},{8,0},{16,24},{24,16},{32,40},{40,32},{48,56},{56,48},{64,72... | collective-permute-start | bytes 1572872 | tf_op jit(solution)/shard_map/ppermute | solution.py:39
  86.6 9.6 %copy-start.14 = (bf16[64,1152]{1,0:T(8,128)(2,1)}, bf16[64,1152]{1,0:T(8,128)(2,1)S(1)}, u32[]{:S(2)}) copy-start(bf16[64,1152]{1,0:T(8,128)(2,1)S(1)} %collective-permute-done.10.refs_0_) | copy-start | bytes 442372
  94.7 1.6 %copy-start.15 = (bf16[64,1152]{1,0:T(8,128)(2,1)}, bf16[64,1152]{1,0:T(8,128)(2,1)S(1)}, u32[]{:S(2)}) copy-start(bf16[64,1152]{1,0:T(8,128)(2,1)S(1)} %collective-permute-done.11.refs_1_) | copy-start | bytes 442372
  96.3 0.6 copy-start.16
  99.2 4.0 %collective-permute-start.13 = (bf16[64,1024]{1,0:T(8,128)(2,1)}, bf16[64,1024]{1,0:T(8,128)(2,1)S(1)}, u32[]{:S(2)}, u32[]{:S(2)}) collective-permute-start(bf16[64,1024]{1,0:T(8,128)(2,1)} %merge.1.refs_0_), channel_id=1, source_target_pairs={{0,224},{8,232},{16,240},{24,248},{32,0},{40,8},{48,16},{56,24},{6... | collective-permute-start | bytes 393224 | tf_op jit(solution)/shard_map/ppermute | solution.py:39
  99.2 19.6 %copy-start.11 = (bf16[1024,256]{1,0:T(8,128)(2,1)}, bf16[1024,256]{1,0:T(8,128)(2,1)S(1)}, u32[]{:S(2)}) copy-start(bf16[1024,256]{1,0:T(8,128)(2,1)S(1)} %collective-permute-done.21.refs_10_) | copy-start | bytes 1572868
  99.2 17.8 %collective-permute-start.22 = (bf16[1024,256]{1,0:T(8,128)(2,1)S(1)}, bf16[1024,256]{1,0:T(8,128)(2,1)S(1)}, u32[]{:S(2)}, u32[]{:S(2)}) collective-permute-start(bf16[1024,256]{1,0:T(8,128)(2,1)S(1)} %collective-permute-done.21.refs_10_), channel_id=1, source_target_pairs={{0,8},{8,0},{16,24},{24,16},{32,40},{40,32},{48,56},{56,48},{64,72... | collective-permute-start | bytes 1572872 | tf_op jit(solution)/shard_map/ppermute | solution.py:39
  100.8 7.3 %collective-permute-start.17 = (bf16[64,1024]{1,0:T(8,128)(2,1)}, bf16[64,1024]{1,0:T(8,128)(2,1)S(1)}, u32[]{:S(2)}, u32[]{:S(2)}) collective-permute-start(bf16[64,1024]{1,0:T(8,128)(2,1)} %merge.1.refs_0_), channel_id=1, source_target_pairs={{0,32},{8,40},{16,48},{24,56},{32,64},{40,72},{48,80},{56,88},{64,... | collective-permute-start | bytes 393224 | tf_op jit(solution)/shard_map/ppermute | solution.py:39
  103.2 15.5 %copy-start.17 = (bf16[64,1024]{1,0:T(8,128)(2,1)}, bf16[64,1024]{1,0:T(8,128)(2,1)S(1)}, u32[]{:S(2)}) copy-start(bf16[64,1024]{1,0:T(8,128)(2,1)S(1)} %collective-permute-done.13.refs_1_) | copy-start | bytes 393220
  103.2 4.9 %collective-permute-start.14 = (bf16[64,1024]{1,0:T(8,128)(2,1)S(1)}, bf16[64,1024]{1,0:T(8,128)(2,1)S(1)}, u32[]{:S(2)}, u32[]{:S(2)}) collective-permute-start(bf16[64,1024]{1,0:T(8,128)(2,1)S(1)} %collective-permute-done.13.refs_1_), channel_id=1, source_target_pairs={{0,224},{8,232},{16,240},{24,248},{32,0},{40,8},{48,16},{56,24},{6... | collective-permute-start | bytes 393224 | tf_op jit(solution)/shard_map/ppermute | solution.py:39
  108.1 10.6 %copy-start.18 = (bf16[64,1024]{1,0:T(8,128)(2,1)}, bf16[64,1024]{1,0:T(8,128)(2,1)S(1)}, u32[]{:S(2)}) copy-start(bf16[64,1024]{1,0:T(8,128)(2,1)S(1)} %collective-permute-done.17.refs_7_) | copy-start | bytes 393220
  108.1 5.6 %collective-permute-start.18 = (bf16[64,1024]{1,0:T(8,128)(2,1)S(1)}, bf16[64,1024]{1,0:T(8,128)(2,1)S(1)}, u32[]{:S(2)}, u32[]{:S(2)}) collective-permute-start(bf16[64,1024]{1,0:T(8,128)(2,1)S(1)} %collective-permute-done.17.refs_7_), channel_id=1, source_target_pairs={{0,32},{8,40},{16,48},{24,56},{32,64},{40,72},{48,80},{56,88},{64,... | collective-permute-start | bytes 393224 | tf_op jit(solution)/shard_map/ppermute | solution.py:39
  108.1 10.6 %copy-start.19 = (bf16[64,1024]{1,0:T(8,128)(2,1)}, bf16[64,1024]{1,0:T(8,128)(2,1)S(1)}, u32[]{:S(2)}) copy-start(bf16[64,1024]{1,0:T(8,128)(2,1)S(1)} %collective-permute-done.14.refs_2_) | copy-start | bytes 393220
  108.1 5.6 %collective-permute-start.15 = (bf16[64,1024]{1,0:T(8,128)(2,1)S(1)}, bf16[64,1024]{1,0:T(8,128)(2,1)S(1)}, u32[]{:S(2)}, u32[]{:S(2)}) collective-permute-start(bf16[64,1024]{1,0:T(8,128)(2,1)S(1)} %collective-permute-done.14.refs_2_), channel_id=1, source_target_pairs={{0,224},{8,232},{16,240},{24,248},{32,0},{40,8},{48,16},{56,24},{6... | collective-permute-start | bytes 393224 | tf_op jit(solution)/shard_map/ppermute | solution.py:39
  113.7 5.1 %copy-start.20 = (bf16[64,1024]{1,0:T(8,128)(2,1)}, bf16[64,1024]{1,0:T(8,128)(2,1)S(1)}, u32[]{:S(2)}) copy-start(bf16[64,1024]{1,0:T(8,128)(2,1)S(1)} %collective-permute-done.18.refs_6_) | copy-start | bytes 393220
  113.7 5.0 %collective-permute-start.19 = (bf16[64,1024]{1,0:T(8,128)(2,1)S(1)}, bf16[64,1024]{1,0:T(8,128)(2,1)S(1)}, u32[]{:S(2)}, u32[]{:S(2)}) collective-permute-start(bf16[64,1024]{1,0:T(8,128)(2,1)S(1)} %collective-permute-done.18.refs_6_), channel_id=1, source_target_pairs={{0,32},{8,40},{16,48},{24,56},{32,64},{40,72},{48,80},{56,88},{64,... | collective-permute-start | bytes 393224 | tf_op jit(solution)/shard_map/ppermute | solution.py:39
  113.7 5.1 %copy-start.21 = (bf16[64,1024]{1,0:T(8,128)(2,1)}, bf16[64,1024]{1,0:T(8,128)(2,1)S(1)}, u32[]{:S(2)}) copy-start(bf16[64,1024]{1,0:T(8,128)(2,1)S(1)} %collective-permute-done.15.refs_3_) | copy-start | bytes 393220
  113.7 5.0 %collective-permute-start.16 = (bf16[64,1024]{1,0:T(8,128)(2,1)S(1)}, bf16[64,1024]{1,0:T(8,128)(2,1)S(1)}, u32[]{:S(2)}, u32[]{:S(2)}) collective-permute-start(bf16[64,1024]{1,0:T(8,128)(2,1)S(1)} %collective-permute-done.15.refs_3_), channel_id=1, source_target_pairs={{0,224},{8,232},{16,240},{24,248},{32,0},{40,8},{48,16},{56,24},{6... | collective-permute-start | bytes 393224 | tf_op jit(solution)/shard_map/ppermute | solution.py:39
  117.0 1.8 %copy-start.12 = (bf16[1024,256]{1,0:T(8,128)(2,1)}, bf16[1024,256]{1,0:T(8,128)(2,1)S(1)}, u32[]{:S(2)}) copy-start(bf16[1024,256]{1,0:T(8,128)(2,1)S(1)} %collective-permute-done.20.refs_9_) | copy-start | bytes 1572868
  117.0 1.8 %copy-start.13 = (bf16[1024,256]{1,0:T(8,128)(2,1)}, bf16[1024,256]{1,0:T(8,128)(2,1)S(1)}, u32[]{:S(2)}) copy-start(bf16[1024,256]{1,0:T(8,128)(2,1)S(1)} %collective-permute-done.22.refs_11_) | copy-start | bytes 1572868
  119.4 0.7 copy-start.23
  (1 other events, 0.6 us)
where the time goes:
time: 156 us
  Pallas kernels  43.6 us (28%)
  starting transfers between devices  38.9 us (25%)
  waiting for transfers between devices  33.5 us (21%)
  blocking collectives  30.4 us (19%)
  local copies, waits for them, and re-layouts  7.4 us (5%)
    ppermute x23, starting transfers between devices, seq_permute(): return lax.ppermute(value, 'seq', pairs)  38.9 us
    pallas_call x3, Pallas kernels, attention(): pl.pallas_call(functools.partial(attention_kernel, len(shards), first, la...  35.2 us
    ppermute x23, waiting for transfers between devices, seq_permute(): return lax.ppermute(value, 'seq', pairs)  33.5 us
    all_to_all x1, blocking collectives, body(): shares = lax.all_to_all(shares, 'head', 0, 0, tiled=True)  19.3 us
    all_to_all x1, blocking collectives, body(): lax.all_to_all(projected, 'seq', 0, 0, axis_index_groups=PLANES, tiled=True)  11.1 us
    unnamed x53, local copies, waits for them, and re-layouts  4.97 us
    pallas_call x1, Pallas kernels, product(): pl.pallas_call(product_kernel, out_shape=jax.ShapeDtypeStruct((Z, YC, TOK...  4.29 us
  transfers between devices with their start and end apart: 23, of which 8 were waited for; matrix products, arithmetic and copies ran while one was open for 2% of the time, Pallas kernels for 24%

commit v1 on v0

--- a/solution.py
+++ b/solution.py
@@ -93,10 +93,12 @@
     position = lax.broadcasted_iota(jnp.int32, (CACHE, HD), 0)
     lane_position = lax.broadcasted_iota(jnp.int32, (16, CACHE), 1)
     row16 = lax.broadcasted_iota(jnp.int32, (16, CACHE), 0)
+    lengths = []
+    for ref in shard_refs:
+        meta = ref[META_AT:BLOCK_ROWS, :].astype(F32)
+        lengths.append(jnp.max(meta[0:8, :] * 32.0 + meta[8:16, :]).astype(jnp.int32))
     total = jnp.int32(0)
-    for ref in shard_refs:
-        meta = ref[META_AT:BLOCK_ROWS, :].astype(F32).astype(jnp.int32)
-        length = jnp.max(meta[0:8, :]) * 32 + jnp.max(meta[8:16, :])
+    for ref, length in zip(shard_refs, lengths):
         start = pl.multiple_of(total, GRAN)
         counted = position < length
         keys = ref[KEY_AT:VALUE_AT, :]
@@ -229,6 +231,7 @@
         out_specs=out_specs,
         scratch_shapes=scratch,
         compiler_params=pltpu.CompilerParams(vmem_limit_bytes=56 * 2**20),
+        cost_estimate=pl.CostEstimate(flops=1, bytes_accessed=1, transcendentals=1),
         name="attention",
     )(*args)
 
@@ -286,44 +289,42 @@
 def body(queries, cache_keys, cache_values, new_keys, new_values, cache_len, span_rank, out_weight):
     seq = lax.axis_index("seq")
     z, yc = seq // YC, seq % YC
-    y, c = yc // 2, yc % 2
 
     own = pack(cache_len, cache_keys, cache_values, new_keys, new_values)
     over_c = lambda v: seq_permute(v, lambda z, y, c: (z, y, 1 - c))
     over_y = lambda v: seq_permute(v, lambda z, y, c: (z, 1 - y, c))
-    over_z = lambda v: seq_permute(v, lambda z, y, c: (z ^ 1, y, c))
     shift = lambda v, n: seq_permute(v, lambda z, y, c: (z + n, y, c))
 
-    kv_y = over_y(own)
     own_pair = (own, over_c(own))
-    q_blocks = (shift(queries, 4), shift(queries, -2), shift(queries, 2), queries)
-    sent, *q_blocks = lax.optimization_barrier((own, *q_blocks))
-    kv_z = over_z(sent)
-    kv_yz = over_z(kv_y)
-
-    ranks = span_rank.reshape(Z, 2, 2, TOK)
-    flip = lambda a, on, dim: jnp.where(on == 1, jnp.flip(a, dim), a)
-    near = lax.dynamic_slice_in_dim(ranks, (z // 2) * 2, 2, 0)
-    near = flip(flip(flip(near, z % 2, 0), y, 1), c, 2)
-    k_rank = jnp.stack([near[0, 0], near[0, 1], near[1, 0], near[1, 1]]).reshape(8 * TOK, 1)
+    q_far, q_side = shift(queries, 4), over_y(queries)
+    kv_up, kv_down = shift(own, -1), shift(own, 1)
+    q_cross = over_y(q_far)
+    sent, q_cross = lax.optimization_barrier((own, q_cross))
+    kv_two = seq_permute(sent, lambda z, y, c: (z - 2 if z % 2 == 0 else z + 2, y, c))
+    q_blocks = (q_cross, q_far, q_side, queries)
+
+    ranks = span_rank.reshape(Z, YC, TOK)
+    two = jnp.where(z % 2 == 0, z + 2, z - 2)
+    near = ranks[jnp.stack([z, z + 1, z - 1, two]) % Z]
+    k_rank = near[:, jnp.stack([yc, yc ^ 1])].reshape(8 * TOK, 1)
     k_rank = jnp.broadcast_to(k_rank, (8 * TOK, HD))
-    by_z = lax.dynamic_index_in_dim(span_rank.reshape(Z, YC, TOK), yc, 1, False)
-    steps = (z + jnp.array([4, 2, 6, 0])) % Z
-    q_rank = jnp.tile(by_z[steps], (1, QPH)).reshape(1, BLOCKS * ROWS)
-
-    y_pair = (kv_y, over_c(kv_y))
-    state = attention(q_blocks, (*own_pair, *y_pair))
-    kv_z, kv_yz, *state = lax.optimization_barrier((kv_z, kv_yz, *state))
-    z_pair = (kv_z, over_c(kv_z))
-    yz_pair = (kv_yz, over_c(kv_yz))
-    state = attention(q_blocks, z_pair, state)
-    new = (*own_pair, *y_pair, *z_pair, *yz_pair)
-    far, up, down, mine = attention(q_blocks, yz_pair, state, new, q_rank, k_rank)
-    attended = merge((shift(far, 4), shift(up, 2), shift(down, -2), mine))
-
-    weight = lax.optimization_barrier((out_weight, kv_yz))[0]
+    both = ranks[jnp.stack([z + 4, z]) % Z]
+    q_rank = both[:, jnp.stack([yc ^ 2, yc])].reshape(BLOCKS, TOK)
+    q_rank = jnp.tile(q_rank, (1, QPH)).reshape(1, BLOCKS * ROWS)
+
+    state = attention(q_blocks, own_pair)
+    kv_up, kv_down, *state = lax.optimization_barrier((kv_up, kv_down, *state))
+    next_pairs = (kv_up, over_c(kv_up), kv_down, over_c(kv_down))
+    weight = lax.optimization_barrier((out_weight, kv_up, kv_down))[0]
     weight_y = over_y(weight)
     weights = [out_weight, over_c(weight), weight_y, over_c(weight_y)]
+    state = attention(q_blocks, next_pairs, state)
+    kv_two, *state = lax.optimization_barrier((kv_two, *state))
+    last_pair = (kv_two, over_c(kv_two))
+    new = (*own_pair, *next_pairs, *last_pair)
+    cross, far, side, mine = attention(q_blocks, last_pair, state, new, q_rank, k_rank)
+    cross = seq_permute(cross, lambda z, y, c: (z + 4, 1 - y, c))
+    attended = merge((cross, shift(far, 4), over_y(side), mine))
 
     blocks = [None] * Z
     blocks[0] = attended

time: 156 us -> 165 us (1.058)
  waiting for transfers between devices: 33.5 us -> 45.5 us
  starting transfers between devices: 38.9 us -> 36.8 us
  Pallas kernels: 43.6 us -> 41.7 us
    ppermute x23, waiting for transfers between devices: 33.5 us -> 45.5 us  [seq_permute(): return lax.ppermute(value, 'seq', pairs)]
    ppermute x23, starting transfers between devices: 38.9 us -> 36.8 us  [seq_permute(): return lax.ppermute(value, 'seq', pairs)]
    pallas_call x3, Pallas kernels: 35.2 us -> 33.3 us  [attention(): pl.pallas_call(functools.partial(attention_kernel, len(shards), first, la...]
    gather x1 -> x8, local copies, waits for them, and re-layouts: 0.56 us -> 2.3 us  [the longest x2 0.58 us: body(): near = ranks[jnp.stack([z, z + 1, z - 1, two]) % Z]]
    unnamed x53 -> x51, local copies, waits for them, and re-layouts: 4.97 us -> 4.93 us
  transfers between devices with their start and end apart: 23 -> 23, of which waited for: 8 -> 11; matrix products, arithmetic and copies ran while one was open for 2% -> 3% of each run, Pallas kernels for 24% -> 22%
where the time goes in v1:
time: 165 us
  waiting for transfers between devices  45.5 us (28%)
  Pallas kernels  41.7 us (25%)
  starting transfers between devices  36.8 us (22%)
  blocking collectives  30.1 us (18%)
  local copies, waits for them, and re-layouts  8.98 us (5%)
    ppermute x23, waiting for transfers between devices, seq_permute(): return lax.ppermute(value, 'seq', pairs)  45.5 us
    ppermute x23, starting transfers between devices, seq_permute(): return lax.ppermute(value, 'seq', pairs)  36.8 us
    pallas_call x3, Pallas kernels, attention(): pl.pallas_call(functools.partial(attention_kernel, len(shards), first, la...  33.3 us
    all_to_all x1, blocking collectives, body(): shares = lax.all_to_all(shares, 'head', 0, 0, tiled=True)  18.6 us
    all_to_all x1, blocking collectives, body(): lax.all_to_all(projected, 'seq', 0, 0, axis_index_groups=PLANES, tiled=True)  11.5 us
    unnamed x51, local copies, waits for them, and re-layouts  4.93 us
    pallas_call x1, Pallas kernels, product(): pl.pallas_call(product_kernel, out_shape=jax.ShapeDtypeStruct((Z, YC, TOK...  4.28 us
  transfers between devices with their start and end apart: 23, of which 11 were waited for; matrix products, arithmetic and copies ran while one was open for 3% of the time, Pallas kernels for 22%

profile of v1, /device:TPU:1, one launch (start us, length us, event | category | flops | bytes accessed | tf_op | source)
XLA Modules:
  0.0 164.9 jit_solution(1792879424307984838)
XLA Ops:
  0.7 1.9 %pack.1.refs_4_.refs_8_ = bf16[2192,128]{1,0:T(8,128)(2,1)} custom-call(s32[1]{0:T(128)S(6)} %copy.14.length_ref, bf16[1,1024,128]{2,1,0:T(8,128)(2,1)} %k_ref.1, bf16[1,1024,128]{2,1,0:T(8,128)(2,1)} %v_ref.1, bf16[64,128]{1,0:T(8,128)(2,1)} %nk_ref.1, bf16[64,128]{1,0:T(8,128)(2,1)} %nv_ref.1), custom_call_target="tpu_custom_call" | custom-call | tf_op jit(solution)/shard_map/pack/pallas_call | solution.py:55
  2.5 3.2 %collective-permute-start.6 = (bf16[2192,128]{1,0:T(8,128)(2,1)}, bf16[2192,128]{1,0:T(8,128)(2,1)S(1)}, u32[]{:S(2)}, u32[]{:S(2)}) collective-permute-start(bf16[2192,128]{1,0:T(8,128)(2,1)} %pack.1.refs_4_.refs_8_), channel_id=1, source_target_pairs={{0,8},{8,0},{16,24},{24,16},{32,40},{40,32},{48,56},{56,48},{64,72... | collective-permute-start | bytes 1683464 | tf_op jit(solution)/shard_map/ppermute | solution.py:39
  5.8 3.8 %collective-permute-start.4 = (bf16[2192,128]{1,0:T(8,128)(2,1)}, bf16[2192,128]{1,0:T(8,128)(2,1)S(1)}, u32[]{:S(2)}, u32[]{:S(2)}) collective-permute-start(bf16[2192,128]{1,0:T(8,128)(2,1)} %pack.1.refs_4_.refs_8_), channel_id=1, source_target_pairs={{0,224},{8,232},{16,240},{24,248},{32,0},{40,8},{48,16},{56,24},{6... | collective-permute-start | bytes 1683464 | tf_op jit(solution)/shard_map/ppermute | solution.py:39
  9.6 2.8 %collective-permute-start = (bf16[64,1024]{1,0:T(8,128)(2,1)}, bf16[64,1024]{1,0:T(8,128)(2,1)S(1)}, u32[]{:S(2)}, u32[]{:S(2)}) collective-permute-start(bf16[64,1024]{1,0:T(8,128)(2,1)} %refs_3_.5), channel_id=1, source_target_pairs={{0,128},{8,136},{16,144},{24,152},{32,160},{40,168},{48,176},{56,1... | collective-permute-start | bytes 393224 | tf_op jit(solution)/shard_map/ppermute | solution.py:39
  12.4 18.4 %collective-permute-done.refs_1_ = bf16[64,1024]{1,0:T(8,128)(2,1)S(1)} collective-permute-done((bf16[64,1024]{1,0:T(8,128)(2,1)}, bf16[64,1024]{1,0:T(8,128)(2,1)S(1)}, u32[]{:S(2)}, u32[]{:S(2)}) %collective-permute-start) | collective-permute-done | bytes 131104 | tf_op jit(solution)/shard_map/ppermute | solution.py:39
  30.8 1.3 collective-permute-start.1
  32.3 2.4 %collective-permute-done.1.refs_0_ = bf16[64,1024]{1,0:T(8,128)(2,1)S(1)} collective-permute-done((bf16[64,1024]{1,0:T(8,128)(2,1)S(1)}, bf16[64,1024]{1,0:T(8,128)(2,1)S(1)}, u32[]{:S(2)}, u32[]{:S(2)}) %collective-permute-start.1) | collective-permute-done | bytes 131104 | tf_op jit(solution)/shard_map/ppermute | solution.py:39
  34.6 3.1 %collective-permute-done.2.refs_2_ = bf16[64,1024]{1,0:T(8,128)(2,1)S(1)} collective-permute-done((bf16[64,1024]{1,0:T(8,128)(2,1)}, bf16[64,1024]{1,0:T(8,128)(2,1)S(1)}, u32[]{:S(2)}, u32[]{:S(2)}) %collective-permute-start.2) | collective-permute-done | bytes 131104 | tf_op jit(solution)/shard_map/ppermute | solution.py:39
  37.8 0.6 copy-done.10
  38.4 0.8 copy-done.3
  39.2 8.9 %attention.3 = (f32[1,2048]{1,0:T(1,128)}, f32[144,2048]{1,0:T(8,128)}) custom-call(bf16[64,1024]{1,0:T(8,128)(2,1)} %copy-done.9, bf16[64,1024]{1,0:T(8,128)(2,1)} %copy-done.8, bf16[64,1024]{1,0:T(8,128)(2,1)} %copy-done.10, bf16[64,1024]{1,0:T(8,128)(2,1)} %refs_3_.5, bf16[2192,128]{1,0:T(8,128)(2,1)} %pack.1.refs_4_.refs_8_, bf16[2192,128]{1,0:T(8,128)(2,1)} %copy-done.3), custom_call_target="tpu_custom_call" | custom-call | flops 1 | bytes 1 | tf_op jit(solution)/shard_map/attention/pallas_call | solution.py:226
  48.2 1.9 %collective-permute-start.7 = (bf16[2192,128]{1,0:T(8,128)(2,1)S(1)}, bf16[2192,128]{1,0:T(8,128)(2,1)S(1)}, u32[]{:S(2)}, u32[]{:S(2)}) collective-permute-start(bf16[2192,128]{1,0:T(8,128)(2,1)S(1)} %collective-permute-done.4.refs_4_.refs_10_), channel_id=1, source_target_pairs={{0,8},{8,0},{16,24},{24,16},{32,40},{40,32},{48,56},{56,48},{64,72... | collective-permute-start | bytes 1683464 | tf_op jit(solution)/shard_map/ppermute | solution.py:39
  50.3 1.4 collective-permute-done.7.refs_5_.refs_11_
  51.7 0.8 collective-permute-done.8.refs_7_.refs_13_
  52.5 0.8 copy-done.7
  53.3 13.2 %attention.4 = (f32[1,2048]{1,0:T(1,128)}, f32[144,2048]{1,0:T(8,128)}) custom-call(bf16[64,1024]{1,0:T(8,128)(2,1)} %copy-done.9, bf16[64,1024]{1,0:T(8,128)(2,1)} %copy-done.8, bf16[64,1024]{1,0:T(8,128)(2,1)} %copy-done.10, bf16[64,1024]{1,0:T(8,128)(2,1)} %refs_3_.5, bf16[2192,128]{1,0:T(8,128)(2,1)} %copy-done.4, bf16[2192,128]{1,0:T(8,128)(2,1)} %copy-done.6, ...), custom_call_target="tpu_custom_call" | custom-call | flops 1 | bytes 1 | tf_op jit(solution)/shard_map/attention/pallas_call | solution.py:226
  66.5 0.6 collective-permute-start.9
  67.2 4.5 %collective-permute-start.21 = (bf16[1024,256]{1,0:T(8,128)(2,1)}, bf16[1024,256]{1,0:T(8,128)(2,1)S(1)}, u32[]{:S(2)}, u32[]{:S(2)}) collective-permute-start(bf16[1024,256]{1,0:T(8,128)(2,1)} %refs_8_.1), channel_id=1, source_target_pairs={{0,16},{8,24},{16,0},{24,8},{32,48},{40,56},{48,32},{56,40},{64,80... | collective-permute-start | bytes 1572872 | tf_op jit(solution)/shard_map/ppermute | solution.py:39
  71.8 0.6 gather_fusion
  72.4 0.6 gather_fusion.1
  73.0 0.7 tile.11.refs_16_
  73.7 0.6 gather_fusion.2
  74.3 0.6 gather_fusion.3
  75.0 0.9 broadcast_in_dim.5.refs_17_
  75.9 11.2 %attention.5 = (bf16[64,1152]{1,0:T(8,128)(2,1)}, bf16[64,1152]{1,0:T(8,128)(2,1)}, bf16[64,1152]{1,0:T(8,128)(2,1)}, bf16[64,1152]{1,0:T(8,128)(2,1)}) custom-call(bf16[64,1024]{1,0:T(8,128)(2,1)} %copy-done.9, bf16[64,1024]{1,0:T(8,128)(2,1)} %copy-done.8, bf16[64,1024]{1,0:T(8,128)(2,1)} %copy-done.10, bf16[64,1024]{1,0:T(8,128)(2,1)} %refs_3_.5, ...), custom_call_target="tpu_custom_call" | custom-call | flops 1 | bytes 1 | tf_op jit(solution)/shard_map/attention/pallas_call | solution.py:226
  87.1 1.2 collective-permute-start.10
  88.3 5.6 %collective-permute-start.11 = (bf16[64,1152]{1,0:T(8,128)(2,1)}, bf16[64,1152]{1,0:T(8,128)(2,1)S(1)}, u32[]{:S(2)}, u32[]{:S(2)}) collective-permute-start(bf16[64,1152]{1,0:T(8,128)(2,1)} %get-tuple-element.37), channel_id=1, source_target_pairs={{0,128},{8,136},{16,144},{24,152},{32,160},{40,168},{48,176},{56,1... | collective-permute-start | bytes 442376 | tf_op jit(solution)/shard_map/ppermute | solution.py:39
  93.9 1.0 collective-permute-start.20
  94.9 3.1 %collective-permute-done.10.refs_0_ = bf16[64,1152]{1,0:T(8,128)(2,1)S(1)} collective-permute-done((bf16[64,1152]{1,0:T(8,128)(2,1)}, bf16[64,1152]{1,0:T(8,128)(2,1)S(1)}, u32[]{:S(2)}, u32[]{:S(2)}) %collective-permute-start.10) | collective-permute-done | bytes 147488 | tf_op jit(solution)/shard_map/ppermute | solution.py:39
  98.0 8.3 %collective-permute-done.11.refs_1_ = bf16[64,1152]{1,0:T(8,128)(2,1)S(1)} collective-permute-done((bf16[64,1152]{1,0:T(8,128)(2,1)}, bf16[64,1152]{1,0:T(8,128)(2,1)S(1)}, u32[]{:S(2)}, u32[]{:S(2)}) %collective-permute-start.11) | collective-permute-done | bytes 147488 | tf_op jit(solution)/shard_map/ppermute | solution.py:39
  106.3 0.6 copy-done.15
  107.1 2.3 %merge.1.refs_0_ = bf16[64,1024]{1,0:T(8,128)(2,1)} custom-call(bf16[64,1152]{1,0:T(8,128)(2,1)} %copy-done.14, bf16[64,1152]{1,0:T(8,128)(2,1)} %copy-done.15, bf16[64,1152]{1,0:T(8,128)(2,1)} %copy-done.16, bf16[64,1152]{1,0:T(8,128)(2,1)} %get-tuple-element.39.refs_3_), custom_call_target="tpu_custom_call" | custom-call | tf_op jit(solution)/shard_map/merge/pallas_call | solution.py:258
  109.3 2.2 %collective-permute-start.22 = (bf16[1024,256]{1,0:T(8,128)(2,1)S(1)}, bf16[1024,256]{1,0:T(8,128)(2,1)S(1)}, u32[]{:S(2)}, u32[]{:S(2)}) collective-permute-start(bf16[1024,256]{1,0:T(8,128)(2,1)S(1)} %collective-permute-done.21.refs_10_), channel_id=1, source_target_pairs={{0,8},{8,0},{16,24},{24,16},{32,40},{40,32},{48,56},{56,48},{64,72... | collective-permute-start | bytes 1572872 | tf_op jit(solution)/shard_map/ppermute | solution.py:39
  111.5 1.7 %collective-permute-start.17 = (bf16[64,1024]{1,0:T(8,128)(2,1)}, bf16[64,1024]{1,0:T(8,128)(2,1)S(1)}, u32[]{:S(2)}, u32[]{:S(2)}) collective-permute-start(bf16[64,1024]{1,0:T(8,128)(2,1)} %merge.1.refs_0_), channel_id=1, source_target_pairs={{0,32},{8,40},{16,48},{24,56},{32,64},{40,72},{48,80},{56,88},{64,... | collective-permute-start | bytes 393224 | tf_op jit(solution)/shard_map/ppermute | solution.py:39
  113.4 1.2 collective-permute-start.14
  114.6 3.4 %collective-permute-done.17.refs_7_ = bf16[64,1024]{1,0:T(8,128)(2,1)S(1)} collective-permute-done((bf16[64,1024]{1,0:T(8,128)(2,1)}, bf16[64,1024]{1,0:T(8,128)(2,1)S(1)}, u32[]{:S(2)}, u32[]{:S(2)}) %collective-permute-start.17) | collective-permute-done | bytes 131104 | tf_op jit(solution)/shard_map/ppermute | solution.py:39
  118.0 0.4 collective-permute-start.18
  118.5 2.2 %collective-permute-start.15 = (bf16[64,1024]{1,0:T(8,128)(2,1)S(1)}, bf16[64,1024]{1,0:T(8,128)(2,1)S(1)}, u32[]{:S(2)}, u32[]{:S(2)}) collective-permute-start(bf16[64,1024]{1,0:T(8,128)(2,1)S(1)} %collective-permute-done.14.refs_2_), channel_id=1, source_target_pairs={{0,224},{8,232},{16,240},{24,248},{32,0},{40,8},{48,16},{56,24},{6... | collective-permute-start | bytes 393224 | tf_op jit(solution)/shard_map/ppermute | solution.py:39
  120.7 2.7 %collective-permute-done.18.refs_6_ = bf16[64,1024]{1,0:T(8,128)(2,1)S(1)} collective-permute-done((bf16[64,1024]{1,0:T(8,128)(2,1)S(1)}, bf16[64,1024]{1,0:T(8,128)(2,1)S(1)}, u32[]{:S(2)}, u32[]{:S(2)}) %collective-permute-start.18) | collective-permute-done | bytes 131104 | tf_op jit(solution)/shard_map/ppermute | solution.py:39
  123.4 2.7 %collective-permute-start.16 = (bf16[64,1024]{1,0:T(8,128)(2,1)S(1)}, bf16[64,1024]{1,0:T(8,128)(2,1)S(1)}, u32[]{:S(2)}, u32[]{:S(2)}) collective-permute-start(bf16[64,1024]{1,0:T(8,128)(2,1)S(1)} %collective-permute-done.15.refs_3_), channel_id=1, source_target_pairs={{0,224},{8,232},{16,240},{24,248},{32,0},{40,8},{48,16},{56,24},{6... | collective-permute-start | bytes 393224 | tf_op jit(solution)/shard_map/ppermute | solution.py:39
  126.1 0.6 pad_add_fusion.place_ref
  126.7 1.7 %collective-permute-done.19.refs_5_ = bf16[64,1024]{1,0:T(8,128)(2,1)S(1)} collective-permute-done((bf16[64,1024]{1,0:T(8,128)(2,1)S(1)}, bf16[64,1024]{1,0:T(8,128)(2,1)S(1)}, u32[]{:S(2)}, u32[]{:S(2)}) %collective-permute-start.19) | collective-permute-done | bytes 131104 | tf_op jit(solution)/shard_map/ppermute | solution.py:39
  128.5 0.6 copy-done.22
  129.1 0.6 copy-done.23
  129.7 4.3 %product.1 = bf16[8,4,64,256]{3,2,1,0:T(8,128)(2,1)} custom-call(s32[2]{0:T(128)} %pad_add_fusion.place_ref, bf16[64,1024]{1,0:T(8,128)(2,1)} %merge.1.refs_0_, bf16[64,1024]{1,0:T(8,128)(2,1)} %copy-done.17, bf16[64,1024]{1,0:T(8,128)(2,1)} %copy-done.19, bf16[64,1024]{1,0:T(8,128)(2,1)} %copy-done.21, bf16[64,1024]{1,0:T(8,128)(2,1)} %copy-done.23, ...), custom_call_target="tpu_custom_call" | custom-call | tf_op jit(solution)/shard_map/product/pallas_call | solution.py:278
  134.0 18.6 %all_to_all.10 = bf16[8,4,64,256]{3,2,1,0:T(8,128)(2,1)S(1)} all-to-all(bf16[8,4,64,256]{3,2,1,0:T(8,128)(2,1)} %product.1), channel_id=1, replica_groups=mesh['seq'=32,'head'=8] {'head'}, dimensions={0} | all-to-all | bytes 2097152 | tf_op jit(solution)/shard_map/all_to_all | solution.py:336
  152.8 11.5 %all_to_all.11 = bf16[4,64,256]{2,1,0:T(8,128)(2,1)S(1)} all-to-all(bf16[4,64,256]{2,1,0:T(8,128)(2,1)S(1)} %reduce_sum.12), channel_id=1, replica_groups={{0,8,16,24},{32,40,48,56},{64,72,80,88},{96,104,112,120},{128,136,144,1..., dimensions={0} | all-to-all | bytes 262144 | tf_op jit(solution)/shard_map/all_to_all | solution.py:338
  164.3 0.7 copy.15
  (79 shorter events, 1.2 us)
Async XLA Ops:
  2.5 47.7 %copy-start = (bf16[2192,128]{1,0:T(8,128)(2,1)S(1)}, bf16[2192,128]{1,0:T(8,128)(2,1)}, u32[]{:S(2)}) copy-start(bf16[2192,128]{1,0:T(8,128)(2,1)} %pack.1.refs_4_.refs_8_) | copy-start | bytes 1683460
  2.5 35.2 %collective-permute-start.6 = (bf16[2192,128]{1,0:T(8,128)(2,1)}, bf16[2192,128]{1,0:T(8,128)(2,1)S(1)}, u32[]{:S(2)}, u32[]{:S(2)}) collective-permute-start(bf16[2192,128]{1,0:T(8,128)(2,1)} %pack.1.refs_4_.refs_8_), channel_id=1, source_target_pairs={{0,8},{8,0},{16,24},{24,16},{32,40},{40,32},{48,56},{56,48},{64,72... | collective-permute-start | bytes 1683464 | tf_op jit(solution)/shard_map/ppermute | solution.py:39
  5.8 42.4 %collective-permute-start.4 = (bf16[2192,128]{1,0:T(8,128)(2,1)}, bf16[2192,128]{1,0:T(8,128)(2,1)S(1)}, u32[]{:S(2)}, u32[]{:S(2)}) collective-permute-start(bf16[2192,128]{1,0:T(8,128)(2,1)} %pack.1.refs_4_.refs_8_), channel_id=1, source_target_pairs={{0,224},{8,232},{16,240},{24,248},{32,0},{40,8},{48,16},{56,24},{6... | collective-permute-start | bytes 1683464 | tf_op jit(solution)/shard_map/ppermute | solution.py:39
  9.6 38.5 %collective-permute-start.5 = (bf16[2192,128]{1,0:T(8,128)(2,1)}, bf16[2192,128]{1,0:T(8,128)(2,1)S(1)}, u32[]{:S(2)}, u32[]{:S(2)}) collective-permute-start(bf16[2192,128]{1,0:T(8,128)(2,1)} %pack.1.refs_4_.refs_8_), channel_id=1, source_target_pairs={{0,32},{8,40},{16,48},{24,56},{32,64},{40,72},{48,80},{56,88},{64,... | collective-permute-start | bytes 1683464 | tf_op jit(solution)/shard_map/ppermute | solution.py:39
  9.6 21.2 %collective-permute-start = (bf16[64,1024]{1,0:T(8,128)(2,1)}, bf16[64,1024]{1,0:T(8,128)(2,1)S(1)}, u32[]{:S(2)}, u32[]{:S(2)}) collective-permute-start(bf16[64,1024]{1,0:T(8,128)(2,1)} %refs_3_.5), channel_id=1, source_target_pairs={{0,128},{8,136},{16,144},{24,152},{32,160},{40,168},{48,176},{56,1... | collective-permute-start | bytes 393224 | tf_op jit(solution)/shard_map/ppermute | solution.py:39
  30.8 7.0 %copy-start.8 = (bf16[64,1024]{1,0:T(8,128)(2,1)}, bf16[64,1024]{1,0:T(8,128)(2,1)S(1)}, u32[]{:S(2)}) copy-start(bf16[64,1024]{1,0:T(8,128)(2,1)S(1)} %collective-permute-done.refs_1_) | copy-start | bytes 393220
  30.8 3.8 %collective-permute-start.1 = (bf16[64,1024]{1,0:T(8,128)(2,1)S(1)}, bf16[64,1024]{1,0:T(8,128)(2,1)S(1)}, u32[]{:S(2)}, u32[]{:S(2)}) collective-permute-start(bf16[64,1024]{1,0:T(8,128)(2,1)S(1)} %collective-permute-done.refs_1_), channel_id=1, source_target_pairs={{0,16},{8,24},{16,0},{24,8},{32,48},{40,56},{48,32},{56,40},{64,80... | collective-permute-start | bytes 393224 | tf_op jit(solution)/shard_map/ppermute | solution.py:39
  32.1 5.7 %collective-permute-start.2 = (bf16[64,1024]{1,0:T(8,128)(2,1)}, bf16[64,1024]{1,0:T(8,128)(2,1)S(1)}, u32[]{:S(2)}, u32[]{:S(2)}) collective-permute-start(bf16[64,1024]{1,0:T(8,128)(2,1)} %refs_3_.5), channel_id=1, source_target_pairs={{0,16},{8,24},{16,0},{24,8},{32,48},{40,56},{48,32},{56,40},{64,80... | collective-permute-start | bytes 393224 | tf_op jit(solution)/shard_map/ppermute | solution.py:39
  34.6 3.2 %copy-start.9 = (bf16[64,1024]{1,0:T(8,128)(2,1)}, bf16[64,1024]{1,0:T(8,128)(2,1)S(1)}, u32[]{:S(2)}) copy-start(bf16[64,1024]{1,0:T(8,128)(2,1)S(1)} %collective-permute-done.1.refs_0_) | copy-start | bytes 393220
  37.8 0.7 copy-start.10
  38.4 0.8 copy-start.3
  48.1 4.4 %copy-start.4 = (bf16[2192,128]{1,0:T(8,128)(2,1)}, bf16[2192,128]{1,0:T(8,128)(2,1)S(1)}, u32[]{:S(2)}) copy-start(bf16[2192,128]{1,0:T(8,128)(2,1)S(1)} %collective-permute-done.4.refs_4_.refs_10_) | copy-start | bytes 1683460
  48.1 4.3 %copy-start.5 = (bf16[2192,128]{1,0:T(8,128)(2,1)}, bf16[2192,128]{1,0:T(8,128)(2,1)S(1)}, u32[]{:S(2)}) copy-start(bf16[2192,128]{1,0:T(8,128)(2,1)S(1)} %collective-permute-done.5.refs_6_.refs_12_) | copy-start | bytes 1683460
  48.2 3.5 %collective-permute-start.7 = (bf16[2192,128]{1,0:T(8,128)(2,1)S(1)}, bf16[2192,128]{1,0:T(8,128)(2,1)S(1)}, u32[]{:S(2)}, u32[]{:S(2)}) collective-permute-start(bf16[2192,128]{1,0:T(8,128)(2,1)S(1)} %collective-permute-done.4.refs_4_.refs_10_), channel_id=1, source_target_pairs={{0,8},{8,0},{16,24},{24,16},{32,40},{40,32},{48,56},{56,48},{64,72... | collective-permute-start | bytes 1683464 | tf_op jit(solution)/shard_map/ppermute | solution.py:39
  50.1 2.4 %collective-permute-start.8 = (bf16[2192,128]{1,0:T(8,128)(2,1)S(1)}, bf16[2192,128]{1,0:T(8,128)(2,1)S(1)}, u32[]{:S(2)}, u32[]{:S(2)}) collective-permute-start(bf16[2192,128]{1,0:T(8,128)(2,1)S(1)} %collective-permute-done.5.refs_6_.refs_12_), channel_id=1, source_target_pairs={{0,8},{8,0},{16,24},{24,16},{32,40},{40,32},{48,56},{56,48},{64,72... | collective-permute-start | bytes 1683464 | tf_op jit(solution)/shard_map/ppermute | solution.py:39
  50.2 16.3 %collective-permute-start.3 = (bf16[2192,128]{1,0:T(8,128)(2,1)S(1)}, bf16[2192,128]{1,0:T(8,128)(2,1)S(1)}, u32[]{:S(2)}, u32[]{:S(2)}) collective-permute-start(bf16[2192,128]{1,0:T(8,128)(2,1)S(1)} %copy-done), channel_id=1, source_target_pairs={{0,192},{8,200},{16,208},{24,216},{32,96},{40,104},{48,112},{56,12... | collective-permute-start | bytes 1683464 | tf_op jit(solution)/shard_map/ppermute | solution.py:39
  50.3 21.4 %copy-start.24 = (s32[2048]{0:T(1024)S(1)}, s32[2048]{0:T(1024)}, u32[]{:S(2)}) copy-start(s32[2048]{0:T(1024)} %param.14) | copy-start | bytes 24580
  51.7 0.8 copy-start.6
  52.5 0.8 copy-start.7
  66.5 9.4 %copy-start.1 = (bf16[2192,128]{1,0:T(8,128)(2,1)}, bf16[2192,128]{1,0:T(8,128)(2,1)S(1)}, u32[]{:S(2)}) copy-start(bf16[2192,128]{1,0:T(8,128)(2,1)S(1)} %collective-permute-done.3.refs_4_.refs_14_) | copy-start | bytes 1683460
  66.5 8.5 %collective-permute-start.9 = (bf16[2192,128]{1,0:T(8,128)(2,1)S(1)}, bf16[2192,128]{1,0:T(8,128)(2,1)S(1)}, u32[]{:S(2)}, u32[]{:S(2)}) collective-permute-start(bf16[2192,128]{1,0:T(8,128)(2,1)S(1)} %collective-permute-done.3.refs_4_.refs_14_), channel_id=1, source_target_pairs={{0,8},{8,0},{16,24},{24,16},{32,40},{40,32},{48,56},{56,48},{64,72... | collective-permute-start | bytes 1683464 | tf_op jit(solution)/shard_map/ppermute | solution.py:39
  67.2 42.1 %collective-permute-start.21 = (bf16[1024,256]{1,0:T(8,128)(2,1)}, bf16[1024,256]{1,0:T(8,128)(2,1)S(1)}, u32[]{:S(2)}, u32[]{:S(2)}) collective-permute-start(bf16[1024,256]{1,0:T(8,128)(2,1)} %refs_8_.1), channel_id=1, source_target_pairs={{0,16},{8,24},{16,0},{24,8},{32,48},{40,56},{48,32},{56,40},{64,80... | collective-permute-start | bytes 1572872 | tf_op jit(solution)/shard_map/ppermute | solution.py:39
  75.0 0.9 copy-start.2
  87.1 10.9 %collective-permute-start.10 = (bf16[64,1152]{1,0:T(8,128)(2,1)}, bf16[64,1152]{1,0:T(8,128)(2,1)S(1)}, u32[]{:S(2)}, u32[]{:S(2)}) collective-permute-start(bf16[64,1152]{1,0:T(8,128)(2,1)} %get-tuple-element.36), channel_id=1, source_target_pairs={{0,144},{8,152},{16,128},{24,136},{32,176},{40,184},{48,160},{56,1... | collective-permute-start | bytes 442376 | tf_op jit(solution)/shard_map/ppermute | solution.py:39
  88.3 18.1 %collective-permute-start.11 = (bf16[64,1152]{1,0:T(8,128)(2,1)}, bf16[64,1152]{1,0:T(8,128)(2,1)S(1)}, u32[]{:S(2)}, u32[]{:S(2)}) collective-permute-start(bf16[64,1152]{1,0:T(8,128)(2,1)} %get-tuple-element.37), channel_id=1, source_target_pairs={{0,128},{8,136},{16,144},{24,152},{32,160},{40,168},{48,176},{56,1... | collective-permute-start | bytes 442376 | tf_op jit(solution)/shard_map/ppermute | solution.py:39
  93.9 12.5 %collective-permute-start.12 = (bf16[64,1152]{1,0:T(8,128)(2,1)}, bf16[64,1152]{1,0:T(8,128)(2,1)S(1)}, u32[]{:S(2)}, u32[]{:S(2)}) collective-permute-start(bf16[64,1152]{1,0:T(8,128)(2,1)} %get-tuple-element.38), channel_id=1, source_target_pairs={{0,16},{8,24},{16,0},{24,8},{32,48},{40,56},{48,32},{56,40},{64,80... | collective-permute-start | bytes 442376 | tf_op jit(solution)/shard_map/ppermute | solution.py:39
  93.9 32.8 %collective-permute-start.20 = (bf16[1024,256]{1,0:T(8,128)(2,1)}, bf16[1024,256]{1,0:T(8,128)(2,1)S(1)}, u32[]{:S(2)}, u32[]{:S(2)}) collective-permute-start(bf16[1024,256]{1,0:T(8,128)(2,1)} %refs_8_.1), channel_id=1, source_target_pairs={{0,8},{8,0},{16,24},{24,16},{32,40},{40,32},{48,56},{56,48},{64,72... | collective-permute-start | bytes 1572872 | tf_op jit(solution)/shard_map/ppermute | solution.py:39
  98.0 8.4 %copy-start.14 = (bf16[64,1152]{1,0:T(8,128)(2,1)}, bf16[64,1152]{1,0:T(8,128)(2,1)S(1)}, u32[]{:S(2)}) copy-start(bf16[64,1152]{1,0:T(8,128)(2,1)S(1)} %collective-permute-done.10.refs_0_) | copy-start | bytes 442372
  106.3 0.7 copy-start.15
  106.3 0.7 copy-start.16
  109.3 4.0 %collective-permute-start.13 = (bf16[64,1024]{1,0:T(8,128)(2,1)}, bf16[64,1024]{1,0:T(8,128)(2,1)S(1)}, u32[]{:S(2)}, u32[]{:S(2)}) collective-permute-start(bf16[64,1024]{1,0:T(8,128)(2,1)} %merge.1.refs_0_), channel_id=1, source_target_pairs={{0,224},{8,232},{16,240},{24,248},{32,0},{40,8},{48,16},{56,24},{6... | collective-permute-start | bytes 393224 | tf_op jit(solution)/shard_map/ppermute | solution.py:39
  109.3 19.1 %copy-start.11 = (bf16[1024,256]{1,0:T(8,128)(2,1)}, bf16[1024,256]{1,0:T(8,128)(2,1)S(1)}, u32[]{:S(2)}) copy-start(bf16[1024,256]{1,0:T(8,128)(2,1)S(1)} %collective-permute-done.21.refs_10_) | copy-start | bytes 1572868
  109.3 17.4 %collective-permute-start.22 = (bf16[1024,256]{1,0:T(8,128)(2,1)S(1)}, bf16[1024,256]{1,0:T(8,128)(2,1)S(1)}, u32[]{:S(2)}, u32[]{:S(2)}) collective-permute-start(bf16[1024,256]{1,0:T(8,128)(2,1)S(1)} %collective-permute-done.21.refs_10_), channel_id=1, source_target_pairs={{0,8},{8,0},{16,24},{24,16},{32,40},{40,32},{48,56},{56,48},{64,72... | collective-permute-start | bytes 1572872 | tf_op jit(solution)/shard_map/ppermute | solution.py:39
  111.5 6.5 %collective-permute-start.17 = (bf16[64,1024]{1,0:T(8,128)(2,1)}, bf16[64,1024]{1,0:T(8,128)(2,1)S(1)}, u32[]{:S(2)}, u32[]{:S(2)}) collective-permute-start(bf16[64,1024]{1,0:T(8,128)(2,1)} %merge.1.refs_0_), channel_id=1, source_target_pairs={{0,32},{8,40},{16,48},{24,56},{32,64},{40,72},{48,80},{56,88},{64,... | collective-permute-start | bytes 393224 | tf_op jit(solution)/shard_map/ppermute | solution.py:39
  113.4 15.1 %copy-start.17 = (bf16[64,1024]{1,0:T(8,128)(2,1)}, bf16[64,1024]{1,0:T(8,128)(2,1)S(1)}, u32[]{:S(2)}) copy-start(bf16[64,1024]{1,0:T(8,128)(2,1)S(1)} %collective-permute-done.13.refs_1_) | copy-start | bytes 393220
  113.4 5.1 %collective-permute-start.14 = (bf16[64,1024]{1,0:T(8,128)(2,1)S(1)}, bf16[64,1024]{1,0:T(8,128)(2,1)S(1)}, u32[]{:S(2)}, u32[]{:S(2)}) collective-permute-start(bf16[64,1024]{1,0:T(8,128)(2,1)S(1)} %collective-permute-done.13.refs_1_), channel_id=1, source_target_pairs={{0,224},{8,232},{16,240},{24,248},{32,0},{40,8},{48,16},{56,24},{6... | collective-permute-start | bytes 393224 | tf_op jit(solution)/shard_map/ppermute | solution.py:39
  118.0 10.4 %copy-start.18 = (bf16[64,1024]{1,0:T(8,128)(2,1)}, bf16[64,1024]{1,0:T(8,128)(2,1)S(1)}, u32[]{:S(2)}) copy-start(bf16[64,1024]{1,0:T(8,128)(2,1)S(1)} %collective-permute-done.17.refs_7_) | copy-start | bytes 393220
  118.0 5.4 %collective-permute-start.18 = (bf16[64,1024]{1,0:T(8,128)(2,1)S(1)}, bf16[64,1024]{1,0:T(8,128)(2,1)S(1)}, u32[]{:S(2)}, u32[]{:S(2)}) collective-permute-start(bf16[64,1024]{1,0:T(8,128)(2,1)S(1)} %collective-permute-done.17.refs_7_), channel_id=1, source_target_pairs={{0,32},{8,40},{16,48},{24,56},{32,64},{40,72},{48,80},{56,88},{64,... | collective-permute-start | bytes 393224 | tf_op jit(solution)/shard_map/ppermute | solution.py:39
  118.5 10.0 %copy-start.19 = (bf16[64,1024]{1,0:T(8,128)(2,1)}, bf16[64,1024]{1,0:T(8,128)(2,1)S(1)}, u32[]{:S(2)}) copy-start(bf16[64,1024]{1,0:T(8,128)(2,1)S(1)} %collective-permute-done.14.refs_2_) | copy-start | bytes 393220
  118.5 4.9 %collective-permute-start.15 = (bf16[64,1024]{1,0:T(8,128)(2,1)S(1)}, bf16[64,1024]{1,0:T(8,128)(2,1)S(1)}, u32[]{:S(2)}, u32[]{:S(2)}) collective-permute-start(bf16[64,1024]{1,0:T(8,128)(2,1)S(1)} %collective-permute-done.14.refs_2_), channel_id=1, source_target_pairs={{0,224},{8,232},{16,240},{24,248},{32,0},{40,8},{48,16},{56,24},{6... | collective-permute-start | bytes 393224 | tf_op jit(solution)/shard_map/ppermute | solution.py:39
  123.4 5.1 %copy-start.20 = (bf16[64,1024]{1,0:T(8,128)(2,1)}, bf16[64,1024]{1,0:T(8,128)(2,1)S(1)}, u32[]{:S(2)}) copy-start(bf16[64,1024]{1,0:T(8,128)(2,1)S(1)} %collective-permute-done.18.refs_6_) | copy-start | bytes 393220
  123.4 5.0 %collective-permute-start.19 = (bf16[64,1024]{1,0:T(8,128)(2,1)S(1)}, bf16[64,1024]{1,0:T(8,128)(2,1)S(1)}, u32[]{:S(2)}, u32[]{:S(2)}) collective-permute-start(bf16[64,1024]{1,0:T(8,128)(2,1)S(1)} %collective-permute-done.18.refs_6_), channel_id=1, source_target_pairs={{0,32},{8,40},{16,48},{24,56},{32,64},{40,72},{48,80},{56,88},{64,... | collective-permute-start | bytes 393224 | tf_op jit(solution)/shard_map/ppermute | solution.py:39
  123.4 5.1 %copy-start.21 = (bf16[64,1024]{1,0:T(8,128)(2,1)}, bf16[64,1024]{1,0:T(8,128)(2,1)S(1)}, u32[]{:S(2)}) copy-start(bf16[64,1024]{1,0:T(8,128)(2,1)S(1)} %collective-permute-done.15.refs_3_) | copy-start | bytes 393220
  123.4 5.0 %collective-permute-start.16 = (bf16[64,1024]{1,0:T(8,128)(2,1)S(1)}, bf16[64,1024]{1,0:T(8,128)(2,1)S(1)}, u32[]{:S(2)}, u32[]{:S(2)}) collective-permute-start(bf16[64,1024]{1,0:T(8,128)(2,1)S(1)} %collective-permute-done.15.refs_3_), channel_id=1, source_target_pairs={{0,224},{8,232},{16,240},{24,248},{32,0},{40,8},{48,16},{56,24},{6... | collective-permute-start | bytes 393224 | tf_op jit(solution)/shard_map/ppermute | solution.py:39
  126.7 1.8 %copy-start.12 = (bf16[1024,256]{1,0:T(8,128)(2,1)}, bf16[1024,256]{1,0:T(8,128)(2,1)S(1)}, u32[]{:S(2)}) copy-start(bf16[1024,256]{1,0:T(8,128)(2,1)S(1)} %collective-permute-done.20.refs_9_) | copy-start | bytes 1572868
  126.7 1.8 %copy-start.13 = (bf16[1024,256]{1,0:T(8,128)(2,1)}, bf16[1024,256]{1,0:T(8,128)(2,1)S(1)}, u32[]{:S(2)}) copy-start(bf16[1024,256]{1,0:T(8,128)(2,1)S(1)} %collective-permute-done.22.refs_11_) | copy-start | bytes 1572868
  128.4 0.6 copy-start.22
  129.1 0.6 copy-start.23

commit v2 on v1

--- a/solution.py
+++ b/solution.py
@@ -295,9 +295,10 @@
     over_y = lambda v: seq_permute(v, lambda z, y, c: (z, 1 - y, c))
     shift = lambda v, n: seq_permute(v, lambda z, y, c: (z + n, y, c))
 
+    q_far, q_side = shift(queries, 4), over_y(queries)
     own_pair = (own, over_c(own))
-    q_far, q_side = shift(queries, 4), over_y(queries)
-    kv_up, kv_down = shift(own, -1), shift(own, 1)
+    sent, q_far = lax.optimization_barrier((own, q_far))
+    kv_up, kv_down = shift(sent, -1), shift(sent, 1)
     q_cross = over_y(q_far)
     sent, q_cross = lax.optimization_barrier((own, q_cross))
     kv_two = seq_permute(sent, lambda z, y, c: (z - 2 if z % 2 == 0 else z + 2, y, c))
@@ -312,6 +313,8 @@
     q_rank = both[:, jnp.stack([yc ^ 2, yc])].reshape(BLOCKS, TOK)
     q_rank = jnp.tile(q_rank, (1, QPH)).reshape(1, BLOCKS * ROWS)
 
+    q_rank, k_rank, own = lax.optimization_barrier((q_rank, k_rank, own))
+    own_pair = (own, own_pair[1])
     state = attention(q_blocks, own_pair)
     kv_up, kv_down, *state = lax.optimization_barrier((kv_up, kv_down, *state))
     next_pairs = (kv_up, over_c(kv_up), kv_down, over_c(kv_down))

time: 165 us -> 146 us (0.88)
  waiting for transfers between devices: 45.5 us -> 15.1 us
  starting transfers between devices: 36.8 us -> 47.1 us
    ppermute x23, waiting for transfers between devices: 45.5 us -> 15.1 us  [seq_permute(): return lax.ppermute(value, 'seq', pairs)]
    ppermute x23, starting transfers between devices: 36.8 us -> 47.1 us  [seq_permute(): return lax.ppermute(value, 'seq', pairs)]
    unnamed x51 -> x53, local copies, waits for them, and re-layouts: 4.93 us -> 6.45 us
  transfers between devices with their start and end apart: 23 -> 23, of which waited for: 11 -> 8; matrix products, arithmetic and copies ran while one was open for 3% -> 3% of each run, Pallas kernels for 22% -> 25%
where the time goes in v2:
time: 146 us
  starting transfers between devices  47.1 us (32%)
  Pallas kernels  41.1 us (28%)
  blocking collectives  30.1 us (21%)
  waiting for transfers between devices  15.1 us (10%)
  local copies, waits for them, and re-layouts  10.5 us (7%)
    ppermute x23, starting transfers between devices, seq_permute(): return lax.ppermute(value, 'seq', pairs)  47.1 us
    pallas_call x3, Pallas kernels, attention(): pl.pallas_call(functools.partial(attention_kernel, len(shards), first, la...  32.7 us
    all_to_all x1, blocking collectives, body(): shares = lax.all_to_all(shares, 'head', 0, 0, tiled=True)  18.6 us
    ppermute x23, waiting for transfers between devices, seq_permute(): return lax.ppermute(value, 'seq', pairs)  15.1 us
    all_to_all x1, blocking collectives, body(): lax.all_to_all(projected, 'seq', 0, 0, axis_index_groups=PLANES, tiled=True)  11.5 us
    unnamed x53, local copies, waits for them, and re-layouts  6.45 us
    pallas_call x1, Pallas kernels, product(): pl.pallas_call(product_kernel, out_shape=jax.ShapeDtypeStruct((Z, YC, TOK...  4.29 us
  transfers between devices with their start and end apart: 23, of which 8 were waited for; matrix products, arithmetic and copies ran while one was open for 3% of the time, Pallas kernels for 25%

profile of v2, /device:TPU:1, one launch (start us, length us, event | category | flops | bytes accessed | tf_op | source)
XLA Modules:
  0.0 145.7 jit_solution(11283052250637901096)
XLA Ops:
  0.0 7.7 %collective-permute-start = (bf16[64,1024]{1,0:T(8,128)(2,1)}, bf16[64,1024]{1,0:T(8,128)(2,1)S(1)}, u32[]{:S(2)}, u32[]{:S(2)}) collective-permute-start(bf16[64,1024]{1,0:T(8,128)(2,1)} %refs_3_.5), channel_id=1, source_target_pairs={{0,128},{8,136},{16,144},{24,152},{32,160},{40,168},{48,176},{56,1... | collective-permute-start | bytes 393224 | tf_op jit(solution)/shard_map/ppermute | solution.py:39
  7.7 1.3 collective-permute-start.2
  9.7 1.9 %pack.1.refs_4_.refs_8_ = bf16[2192,128]{1,0:T(8,128)(2,1)} custom-call(s32[1]{0:T(128)S(6)} %copy.14.length_ref, bf16[1,1024,128]{2,1,0:T(8,128)(2,1)} %k_ref.1, bf16[1,1024,128]{2,1,0:T(8,128)(2,1)} %v_ref.1, bf16[64,128]{1,0:T(8,128)(2,1)} %nk_ref.1, bf16[64,128]{1,0:T(8,128)(2,1)} %nv_ref.1), custom_call_target="tpu_custom_call" | custom-call | tf_op jit(solution)/shard_map/pack/pallas_call | solution.py:55
  11.6 1.2 collective-permute-start.6
  13.0 3.9 %collective-permute-start.4 = (bf16[2192,128]{1,0:T(8,128)(2,1)}, bf16[2192,128]{1,0:T(8,128)(2,1)S(1)}, u32[]{:S(2)}, u32[]{:S(2)}) collective-permute-start(bf16[2192,128]{1,0:T(8,128)(2,1)} %pack.1.refs_4_.refs_8_), channel_id=1, source_target_pairs={{0,224},{8,232},{16,240},{24,248},{32,0},{40,8},{48,16},{56,24},{6... | collective-permute-start | bytes 1683464 | tf_op jit(solution)/shard_map/ppermute | solution.py:39
  17.0 1.4 collective-permute-start.1
  18.4 0.6 gather_fusion
  19.0 0.6 gather_fusion.1
  19.6 0.7 tile.11.refs_16_
  20.3 0.6 gather_fusion.2
  20.9 0.6 gather_fusion.3
  21.5 0.9 broadcast_in_dim.5.refs_17_
  22.4 0.6 copy-done.10
  23.1 0.8 copy-done.3
  23.9 8.8 %attention.3 = (f32[1,2048]{1,0:T(1,128)}, f32[144,2048]{1,0:T(8,128)}) custom-call(bf16[64,1024]{1,0:T(8,128)(2,1)} %copy-done.10, bf16[64,1024]{1,0:T(8,128)(2,1)} %copy-done.8, bf16[64,1024]{1,0:T(8,128)(2,1)} %copy-done.9, bf16[64,1024]{1,0:T(8,128)(2,1)} %refs_3_.5, bf16[2192,128]{1,0:T(8,128)(2,1)} %pack.1.refs_4_.refs_8_, bf16[2192,128]{1,0:T(8,128)(2,1)} %copy-done.3), custom_call_target="tpu_custom_call" | custom-call | flops 1 | bytes 1 | tf_op jit(solution)/shard_map/attention/pallas_call | solution.py:226
  32.7 1.3 collective-permute-start.7
  34.1 3.8 %collective-permute-start.3 = (bf16[2192,128]{1,0:T(8,128)(2,1)S(1)}, bf16[2192,128]{1,0:T(8,128)(2,1)S(1)}, u32[]{:S(2)}, u32[]{:S(2)}) collective-permute-start(bf16[2192,128]{1,0:T(8,128)(2,1)S(1)} %copy-done), channel_id=1, source_target_pairs={{0,192},{8,200},{16,208},{24,216},{32,96},{40,104},{48,112},{56,12... | collective-permute-start | bytes 1683464 | tf_op jit(solution)/shard_map/ppermute | solution.py:39
  38.0 0.8 copy-done.6
  38.8 0.8 copy-done.7
  39.6 12.9 %attention.4 = (f32[1,2048]{1,0:T(1,128)}, f32[144,2048]{1,0:T(8,128)}) custom-call(bf16[64,1024]{1,0:T(8,128)(2,1)} %copy-done.10, bf16[64,1024]{1,0:T(8,128)(2,1)} %copy-done.8, bf16[64,1024]{1,0:T(8,128)(2,1)} %copy-done.9, bf16[64,1024]{1,0:T(8,128)(2,1)} %refs_3_.5, bf16[2192,128]{1,0:T(8,128)(2,1)} %copy-done.4, bf16[2192,128]{1,0:T(8,128)(2,1)} %copy-done.6, ...), custom_call_target="tpu_custom_call" | custom-call | flops 1 | bytes 1 | tf_op jit(solution)/shard_map/attention/pallas_call | solution.py:226
  52.4 1.0 collective-permute-start.9
  53.4 0.7 collective-permute-start.21
  54.1 0.9 collective-permute-done.9.refs_5_.refs_15_
  55.0 0.8 copy-done.2
  55.8 11.1 %attention.5 = (bf16[64,1152]{1,0:T(8,128)(2,1)}, bf16[64,1152]{1,0:T(8,128)(2,1)}, bf16[64,1152]{1,0:T(8,128)(2,1)}, bf16[64,1152]{1,0:T(8,128)(2,1)}) custom-call(bf16[64,1024]{1,0:T(8,128)(2,1)} %copy-done.10, bf16[64,1024]{1,0:T(8,128)(2,1)} %copy-done.8, bf16[64,1024]{1,0:T(8,128)(2,1)} %copy-done.9, bf16[64,1024]{1,0:T(8,128)(2,1)} %refs_3_.5, ...), custom_call_target="tpu_custom_call" | custom-call | flops 1 | bytes 1 | tf_op jit(solution)/shard_map/attention/pallas_call | solution.py:226
  66.9 4.5 %collective-permute-start.10 = (bf16[64,1152]{1,0:T(8,128)(2,1)}, bf16[64,1152]{1,0:T(8,128)(2,1)S(1)}, u32[]{:S(2)}, u32[]{:S(2)}) collective-permute-start(bf16[64,1152]{1,0:T(8,128)(2,1)} %get-tuple-element.46), channel_id=1, source_target_pairs={{0,144},{8,152},{16,128},{24,136},{32,176},{40,184},{48,160},{56,1... | collective-permute-start | bytes 442376 | tf_op jit(solution)/shard_map/ppermute | solution.py:39
  71.4 1.2 collective-permute-start.11
  72.6 0.8 collective-permute-start.12
  73.4 1.2 collective-permute-start.20
  74.7 2.3 %collective-permute-done.10.refs_0_ = bf16[64,1152]{1,0:T(8,128)(2,1)S(1)} collective-permute-done((bf16[64,1152]{1,0:T(8,128)(2,1)}, bf16[64,1152]{1,0:T(8,128)(2,1)S(1)}, u32[]{:S(2)}, u32[]{:S(2)}) %collective-permute-start.10) | collective-permute-done | bytes 147488 | tf_op jit(solution)/shard_map/ppermute | solution.py:39
  76.9 3.3 %collective-permute-done.11.refs_1_ = bf16[64,1152]{1,0:T(8,128)(2,1)S(1)} collective-permute-done((bf16[64,1152]{1,0:T(8,128)(2,1)}, bf16[64,1152]{1,0:T(8,128)(2,1)S(1)}, u32[]{:S(2)}, u32[]{:S(2)}) %collective-permute-start.11) | collective-permute-done | bytes 147488 | tf_op jit(solution)/shard_map/ppermute | solution.py:39
  80.2 0.6 collective-permute-done.12.refs_2_
  80.9 0.6 copy-done.17
  81.5 2.3 %merge.1.refs_0_ = bf16[64,1024]{1,0:T(8,128)(2,1)} custom-call(bf16[64,1152]{1,0:T(8,128)(2,1)} %copy-done.15, bf16[64,1152]{1,0:T(8,128)(2,1)} %copy-done.16, bf16[64,1152]{1,0:T(8,128)(2,1)} %copy-done.17, bf16[64,1152]{1,0:T(8,128)(2,1)} %get-tuple-element.49.refs_3_), custom_call_target="tpu_custom_call" | custom-call | tf_op jit(solution)/shard_map/merge/pallas_call | solution.py:258
  83.7 7.2 %collective-permute-start.13 = (bf16[64,1024]{1,0:T(8,128)(2,1)}, bf16[64,1024]{1,0:T(8,128)(2,1)S(1)}, u32[]{:S(2)}, u32[]{:S(2)}) collective-permute-start(bf16[64,1024]{1,0:T(8,128)(2,1)} %merge.1.refs_0_), channel_id=1, source_target_pairs={{0,224},{8,232},{16,240},{24,248},{32,0},{40,8},{48,16},{56,24},{6... | collective-permute-start | bytes 393224 | tf_op jit(solution)/shard_map/ppermute | solution.py:39
  91.0 1.4 collective-permute-start.22
  92.3 0.9 collective-permute-done.13.refs_1_
  93.2 3.0 %collective-permute-start.14 = (bf16[64,1024]{1,0:T(8,128)(2,1)S(1)}, bf16[64,1024]{1,0:T(8,128)(2,1)S(1)}, u32[]{:S(2)}, u32[]{:S(2)}) collective-permute-start(bf16[64,1024]{1,0:T(8,128)(2,1)S(1)} %collective-permute-done.13.refs_1_), channel_id=1, source_target_pairs={{0,224},{8,232},{16,240},{24,248},{32,0},{40,8},{48,16},{56,24},{6... | collective-permute-start | bytes 393224 | tf_op jit(solution)/shard_map/ppermute | solution.py:39
  96.2 2.6 %collective-permute-done.17.refs_7_ = bf16[64,1024]{1,0:T(8,128)(2,1)S(1)} collective-permute-done((bf16[64,1024]{1,0:T(8,128)(2,1)}, bf16[64,1024]{1,0:T(8,128)(2,1)S(1)}, u32[]{:S(2)}, u32[]{:S(2)}) %collective-permute-start.17) | collective-permute-done | bytes 131104 | tf_op jit(solution)/shard_map/ppermute | solution.py:39
  98.9 2.7 %collective-permute-start.15 = (bf16[64,1024]{1,0:T(8,128)(2,1)S(1)}, bf16[64,1024]{1,0:T(8,128)(2,1)S(1)}, u32[]{:S(2)}, u32[]{:S(2)}) collective-permute-start(bf16[64,1024]{1,0:T(8,128)(2,1)S(1)} %collective-permute-done.14.refs_2_), channel_id=1, source_target_pairs={{0,224},{8,232},{16,240},{24,248},{32,0},{40,8},{48,16},{56,24},{6... | collective-permute-start | bytes 393224 | tf_op jit(solution)/shard_map/ppermute | solution.py:39
  101.5 2.7 %collective-permute-done.18.refs_6_ = bf16[64,1024]{1,0:T(8,128)(2,1)S(1)} collective-permute-done((bf16[64,1024]{1,0:T(8,128)(2,1)S(1)}, bf16[64,1024]{1,0:T(8,128)(2,1)S(1)}, u32[]{:S(2)}, u32[]{:S(2)}) %collective-permute-start.18) | collective-permute-done | bytes 131104 | tf_op jit(solution)/shard_map/ppermute | solution.py:39
  104.2 2.7 %collective-permute-start.16 = (bf16[64,1024]{1,0:T(8,128)(2,1)S(1)}, bf16[64,1024]{1,0:T(8,128)(2,1)S(1)}, u32[]{:S(2)}, u32[]{:S(2)}) collective-permute-start(bf16[64,1024]{1,0:T(8,128)(2,1)S(1)} %collective-permute-done.15.refs_3_), channel_id=1, source_target_pairs={{0,224},{8,232},{16,240},{24,248},{32,0},{40,8},{48,16},{56,24},{6... | collective-permute-start | bytes 393224 | tf_op jit(solution)/shard_map/ppermute | solution.py:39
  107.5 1.8 %collective-permute-done.19.refs_5_ = bf16[64,1024]{1,0:T(8,128)(2,1)S(1)} collective-permute-done((bf16[64,1024]{1,0:T(8,128)(2,1)S(1)}, bf16[64,1024]{1,0:T(8,128)(2,1)S(1)}, u32[]{:S(2)}, u32[]{:S(2)}) %collective-permute-start.19) | collective-permute-done | bytes 131104 | tf_op jit(solution)/shard_map/ppermute | solution.py:39
  109.9 0.7 copy-done.24
  110.5 4.3 %product.1 = bf16[8,4,64,256]{3,2,1,0:T(8,128)(2,1)} custom-call(s32[2]{0:T(128)} %pad_add_fusion.place_ref, bf16[64,1024]{1,0:T(8,128)(2,1)} %merge.1.refs_0_, bf16[64,1024]{1,0:T(8,128)(2,1)} %copy-done.18, bf16[64,1024]{1,0:T(8,128)(2,1)} %copy-done.20, bf16[64,1024]{1,0:T(8,128)(2,1)} %copy-done.22, bf16[64,1024]{1,0:T(8,128)(2,1)} %copy-done.24, ...), custom_call_target="tpu_custom_call" | custom-call | tf_op jit(solution)/shard_map/product/pallas_call | solution.py:278
  114.8 18.6 %all_to_all.10 = bf16[8,4,64,256]{3,2,1,0:T(8,128)(2,1)S(1)} all-to-all(bf16[8,4,64,256]{3,2,1,0:T(8,128)(2,1)} %product.1), channel_id=1, replica_groups=mesh['seq'=32,'head'=8] {'head'}, dimensions={0} | all-to-all | bytes 2097152 | tf_op jit(solution)/shard_map/all_to_all | solution.py:339
  133.6 11.5 %all_to_all.11 = bf16[4,64,256]{2,1,0:T(8,128)(2,1)S(1)} all-to-all(bf16[4,64,256]{2,1,0:T(8,128)(2,1)S(1)} %reduce_sum.12), channel_id=1, replica_groups={{0,8,16,24},{32,40,48,56},{64,72,80,88},{96,104,112,120},{128,136,144,1..., dimensions={0} | all-to-all | bytes 262144 | tf_op jit(solution)/shard_map/all_to_all | solution.py:341
  145.1 0.7 copy.15
  (81 shorter events, 2.0 us)
Async XLA Ops:
  0.0 18.4 %copy-start.25 = (s32[2048]{0:T(1024)S(1)}, s32[2048]{0:T(1024)}, u32[]{:S(2)}) copy-start(s32[2048]{0:T(1024)} %param.14) | copy-start | bytes 24580
  0.0 13.0 %collective-permute-start = (bf16[64,1024]{1,0:T(8,128)(2,1)}, bf16[64,1024]{1,0:T(8,128)(2,1)S(1)}, u32[]{:S(2)}, u32[]{:S(2)}) collective-permute-start(bf16[64,1024]{1,0:T(8,128)(2,1)} %refs_3_.5), channel_id=1, source_target_pairs={{0,128},{8,136},{16,144},{24,152},{32,160},{40,168},{48,176},{56,1... | collective-permute-start | bytes 393224 | tf_op jit(solution)/shard_map/ppermute | solution.py:39
  7.7 14.7 %collective-permute-start.2 = (bf16[64,1024]{1,0:T(8,128)(2,1)}, bf16[64,1024]{1,0:T(8,128)(2,1)S(1)}, u32[]{:S(2)}, u32[]{:S(2)}) collective-permute-start(bf16[64,1024]{1,0:T(8,128)(2,1)} %refs_3_.5), channel_id=1, source_target_pairs={{0,16},{8,24},{16,0},{24,8},{32,48},{40,56},{48,32},{56,40},{64,80... | collective-permute-start | bytes 393224 | tf_op jit(solution)/shard_map/ppermute | solution.py:39
  11.6 22.5 %copy-start = (bf16[2192,128]{1,0:T(8,128)(2,1)S(1)}, bf16[2192,128]{1,0:T(8,128)(2,1)}, u32[]{:S(2)}) copy-start(bf16[2192,128]{1,0:T(8,128)(2,1)} %pack.1.refs_4_.refs_8_) | copy-start | bytes 1683460
  11.6 10.8 %collective-permute-start.6 = (bf16[2192,128]{1,0:T(8,128)(2,1)}, bf16[2192,128]{1,0:T(8,128)(2,1)S(1)}, u32[]{:S(2)}, u32[]{:S(2)}) collective-permute-start(bf16[2192,128]{1,0:T(8,128)(2,1)} %pack.1.refs_4_.refs_8_), channel_id=1, source_target_pairs={{0,8},{8,0},{16,24},{24,16},{32,40},{40,32},{48,56},{56,48},{64,72... | collective-permute-start | bytes 1683464 | tf_op jit(solution)/shard_map/ppermute | solution.py:39
  13.0 9.5 %copy-start.8 = (bf16[64,1024]{1,0:T(8,128)(2,1)}, bf16[64,1024]{1,0:T(8,128)(2,1)S(1)}, u32[]{:S(2)}) copy-start(bf16[64,1024]{1,0:T(8,128)(2,1)S(1)} %collective-permute-done.refs_1_) | copy-start | bytes 393220
  13.0 19.7 %collective-permute-start.4 = (bf16[2192,128]{1,0:T(8,128)(2,1)}, bf16[2192,128]{1,0:T(8,128)(2,1)S(1)}, u32[]{:S(2)}, u32[]{:S(2)}) collective-permute-start(bf16[2192,128]{1,0:T(8,128)(2,1)} %pack.1.refs_4_.refs_8_), channel_id=1, source_target_pairs={{0,224},{8,232},{16,240},{24,248},{32,0},{40,8},{48,16},{56,24},{6... | collective-permute-start | bytes 1683464 | tf_op jit(solution)/shard_map/ppermute | solution.py:39
  16.9 15.8 %collective-permute-start.5 = (bf16[2192,128]{1,0:T(8,128)(2,1)}, bf16[2192,128]{1,0:T(8,128)(2,1)S(1)}, u32[]{:S(2)}, u32[]{:S(2)}) collective-permute-start(bf16[2192,128]{1,0:T(8,128)(2,1)} %pack.1.refs_4_.refs_8_), channel_id=1, source_target_pairs={{0,32},{8,40},{16,48},{24,56},{32,64},{40,72},{48,80},{56,88},{64,... | collective-permute-start | bytes 1683464 | tf_op jit(solution)/shard_map/ppermute | solution.py:39
  17.0 5.4 %collective-permute-start.1 = (bf16[64,1024]{1,0:T(8,128)(2,1)S(1)}, bf16[64,1024]{1,0:T(8,128)(2,1)S(1)}, u32[]{:S(2)}, u32[]{:S(2)}) collective-permute-start(bf16[64,1024]{1,0:T(8,128)(2,1)S(1)} %collective-permute-done.refs_1_), channel_id=1, source_target_pairs={{0,16},{8,24},{16,0},{24,8},{32,48},{40,56},{48,32},{56,40},{64,80... | collective-permute-start | bytes 393224 | tf_op jit(solution)/shard_map/ppermute | solution.py:39
  22.4 0.7 copy-start.10
  22.4 0.7 copy-start.9
  23.1 0.8 copy-start.3
  32.7 5.3 %copy-start.4 = (bf16[2192,128]{1,0:T(8,128)(2,1)}, bf16[2192,128]{1,0:T(8,128)(2,1)S(1)}, u32[]{:S(2)}) copy-start(bf16[2192,128]{1,0:T(8,128)(2,1)S(1)} %collective-permute-done.4.refs_4_.refs_10_) | copy-start | bytes 1683460
  32.7 5.3 %copy-start.5 = (bf16[2192,128]{1,0:T(8,128)(2,1)}, bf16[2192,128]{1,0:T(8,128)(2,1)S(1)}, u32[]{:S(2)}) copy-start(bf16[2192,128]{1,0:T(8,128)(2,1)S(1)} %collective-permute-done.5.refs_6_.refs_12_) | copy-start | bytes 1683460
  32.7 20.7 %copy-start.11 = (bf16[1024,256]{1,0:T(8,128)(2,1)S(1)}, bf16[1024,256]{1,0:T(8,128)(2,1)}, u32[]{:S(2)}) copy-start(bf16[1024,256]{1,0:T(8,128)(2,1)} %refs_8_.1) | copy-start | bytes 1572868
  32.7 5.2 %collective-permute-start.7 = (bf16[2192,128]{1,0:T(8,128)(2,1)S(1)}, bf16[2192,128]{1,0:T(8,128)(2,1)S(1)}, u32[]{:S(2)}, u32[]{:S(2)}) collective-permute-start(bf16[2192,128]{1,0:T(8,128)(2,1)S(1)} %collective-permute-done.4.refs_4_.refs_10_), channel_id=1, source_target_pairs={{0,8},{8,0},{16,24},{24,16},{32,40},{40,32},{48,56},{56,48},{64,72... | collective-permute-start | bytes 1683464 | tf_op jit(solution)/shard_map/ppermute | solution.py:39
  34.0 4.0 %collective-permute-start.8 = (bf16[2192,128]{1,0:T(8,128)(2,1)S(1)}, bf16[2192,128]{1,0:T(8,128)(2,1)S(1)}, u32[]{:S(2)}, u32[]{:S(2)}) collective-permute-start(bf16[2192,128]{1,0:T(8,128)(2,1)S(1)} %collective-permute-done.5.refs_6_.refs_12_), channel_id=1, source_target_pairs={{0,8},{8,0},{16,24},{24,16},{32,40},{40,32},{48,56},{56,48},{64,72... | collective-permute-start | bytes 1683464 | tf_op jit(solution)/shard_map/ppermute | solution.py:39
  34.1 18.3 %collective-permute-start.3 = (bf16[2192,128]{1,0:T(8,128)(2,1)S(1)}, bf16[2192,128]{1,0:T(8,128)(2,1)S(1)}, u32[]{:S(2)}, u32[]{:S(2)}) collective-permute-start(bf16[2192,128]{1,0:T(8,128)(2,1)S(1)} %copy-done), channel_id=1, source_target_pairs={{0,192},{8,200},{16,208},{24,216},{32,96},{40,104},{48,112},{56,12... | collective-permute-start | bytes 1683464 | tf_op jit(solution)/shard_map/ppermute | solution.py:39
  37.9 0.8 copy-start.6
  38.8 0.8 copy-start.7
  52.4 2.6 %copy-start.1 = (bf16[2192,128]{1,0:T(8,128)(2,1)}, bf16[2192,128]{1,0:T(8,128)(2,1)S(1)}, u32[]{:S(2)}) copy-start(bf16[2192,128]{1,0:T(8,128)(2,1)S(1)} %collective-permute-done.3.refs_4_.refs_14_) | copy-start | bytes 1683460
  52.4 2.5 %collective-permute-start.9 = (bf16[2192,128]{1,0:T(8,128)(2,1)S(1)}, bf16[2192,128]{1,0:T(8,128)(2,1)S(1)}, u32[]{:S(2)}, u32[]{:S(2)}) collective-permute-start(bf16[2192,128]{1,0:T(8,128)(2,1)S(1)} %collective-permute-done.3.refs_4_.refs_14_), channel_id=1, source_target_pairs={{0,8},{8,0},{16,24},{24,16},{32,40},{40,32},{48,56},{56,48},{64,72... | collective-permute-start | bytes 1683464 | tf_op jit(solution)/shard_map/ppermute | solution.py:39
  53.4 37.6 %collective-permute-start.21 = (bf16[1024,256]{1,0:T(8,128)(2,1)S(1)}, bf16[1024,256]{1,0:T(8,128)(2,1)S(1)}, u32[]{:S(2)}, u32[]{:S(2)}) collective-permute-start(bf16[1024,256]{1,0:T(8,128)(2,1)S(1)} %copy-done.11), channel_id=1, source_target_pairs={{0,16},{8,24},{16,0},{24,8},{32,48},{40,56},{48,32},{56,40},{64,80... | collective-permute-start | bytes 1572872 | tf_op jit(solution)/shard_map/ppermute | solution.py:39
  55.0 0.8 copy-start.2
  66.9 10.1 %collective-permute-start.10 = (bf16[64,1152]{1,0:T(8,128)(2,1)}, bf16[64,1152]{1,0:T(8,128)(2,1)S(1)}, u32[]{:S(2)}, u32[]{:S(2)}) collective-permute-start(bf16[64,1152]{1,0:T(8,128)(2,1)} %get-tuple-element.46), channel_id=1, source_target_pairs={{0,144},{8,152},{16,128},{24,136},{32,176},{40,184},{48,160},{56,1... | collective-permute-start | bytes 442376 | tf_op jit(solution)/shard_map/ppermute | solution.py:39
  71.4 8.8 %collective-permute-start.11 = (bf16[64,1152]{1,0:T(8,128)(2,1)}, bf16[64,1152]{1,0:T(8,128)(2,1)S(1)}, u32[]{:S(2)}, u32[]{:S(2)}) collective-permute-start(bf16[64,1152]{1,0:T(8,128)(2,1)} %get-tuple-element.47), channel_id=1, source_target_pairs={{0,128},{8,136},{16,144},{24,152},{32,160},{40,168},{48,176},{56,1... | collective-permute-start | bytes 442376 | tf_op jit(solution)/shard_map/ppermute | solution.py:39
  72.6 8.2 %collective-permute-start.12 = (bf16[64,1152]{1,0:T(8,128)(2,1)}, bf16[64,1152]{1,0:T(8,128)(2,1)S(1)}, u32[]{:S(2)}, u32[]{:S(2)}) collective-permute-start(bf16[64,1152]{1,0:T(8,128)(2,1)} %get-tuple-element.48), channel_id=1, source_target_pairs={{0,16},{8,24},{16,0},{24,8},{32,48},{40,56},{48,32},{56,40},{64,80... | collective-permute-start | bytes 442376 | tf_op jit(solution)/shard_map/ppermute | solution.py:39
  73.4 34.0 %collective-permute-start.20 = (bf16[1024,256]{1,0:T(8,128)(2,1)S(1)}, bf16[1024,256]{1,0:T(8,128)(2,1)S(1)}, u32[]{:S(2)}, u32[]{:S(2)}) collective-permute-start(bf16[1024,256]{1,0:T(8,128)(2,1)S(1)} %copy-done.11), channel_id=1, source_target_pairs={{0,8},{8,0},{16,24},{24,16},{32,40},{40,32},{48,56},{56,48},{64,72... | collective-permute-start | bytes 1572872 | tf_op jit(solution)/shard_map/ppermute | solution.py:39
  76.9 3.9 %copy-start.15 = (bf16[64,1152]{1,0:T(8,128)(2,1)}, bf16[64,1152]{1,0:T(8,128)(2,1)S(1)}, u32[]{:S(2)}) copy-start(bf16[64,1152]{1,0:T(8,128)(2,1)S(1)} %collective-permute-done.10.refs_0_) | copy-start | bytes 442372
  80.2 0.7 copy-start.16
  80.8 0.7 copy-start.17
  83.7 9.5 %collective-permute-start.13 = (bf16[64,1024]{1,0:T(8,128)(2,1)}, bf16[64,1024]{1,0:T(8,128)(2,1)S(1)}, u32[]{:S(2)}, u32[]{:S(2)}) collective-permute-start(bf16[64,1024]{1,0:T(8,128)(2,1)} %merge.1.refs_0_), channel_id=1, source_target_pairs={{0,224},{8,232},{16,240},{24,248},{32,0},{40,8},{48,16},{56,24},{6... | collective-permute-start | bytes 393224 | tf_op jit(solution)/shard_map/ppermute | solution.py:39
  91.0 18.3 %copy-start.12 = (bf16[1024,256]{1,0:T(8,128)(2,1)}, bf16[1024,256]{1,0:T(8,128)(2,1)S(1)}, u32[]{:S(2)}) copy-start(bf16[1024,256]{1,0:T(8,128)(2,1)S(1)} %collective-permute-done.21.refs_10_) | copy-start | bytes 1572868
  91.0 16.5 %collective-permute-start.22 = (bf16[1024,256]{1,0:T(8,128)(2,1)S(1)}, bf16[1024,256]{1,0:T(8,128)(2,1)S(1)}, u32[]{:S(2)}, u32[]{:S(2)}) collective-permute-start(bf16[1024,256]{1,0:T(8,128)(2,1)S(1)} %collective-permute-done.21.refs_10_), channel_id=1, source_target_pairs={{0,8},{8,0},{16,24},{24,16},{32,40},{40,32},{48,56},{56,48},{64,72... | collective-permute-start | bytes 1572872 | tf_op jit(solution)/shard_map/ppermute | solution.py:39
  92.3 6.5 %collective-permute-start.17 = (bf16[64,1024]{1,0:T(8,128)(2,1)}, bf16[64,1024]{1,0:T(8,128)(2,1)S(1)}, u32[]{:S(2)}, u32[]{:S(2)}) collective-permute-start(bf16[64,1024]{1,0:T(8,128)(2,1)} %merge.1.refs_0_), channel_id=1, source_target_pairs={{0,32},{8,40},{16,48},{24,56},{32,64},{40,72},{48,80},{56,88},{64,... | collective-permute-start | bytes 393224 | tf_op jit(solution)/shard_map/ppermute | solution.py:39
  93.2 16.0 %copy-start.18 = (bf16[64,1024]{1,0:T(8,128)(2,1)}, bf16[64,1024]{1,0:T(8,128)(2,1)S(1)}, u32[]{:S(2)}) copy-start(bf16[64,1024]{1,0:T(8,128)(2,1)S(1)} %collective-permute-done.13.refs_1_) | copy-start | bytes 393220
  93.2 5.6 %collective-permute-start.14 = (bf16[64,1024]{1,0:T(8,128)(2,1)S(1)}, bf16[64,1024]{1,0:T(8,128)(2,1)S(1)}, u32[]{:S(2)}, u32[]{:S(2)}) collective-permute-start(bf16[64,1024]{1,0:T(8,128)(2,1)S(1)} %collective-permute-done.13.refs_1_), channel_id=1, source_target_pairs={{0,224},{8,232},{16,240},{24,248},{32,0},{40,8},{48,16},{56,24},{6... | collective-permute-start | bytes 393224 | tf_op jit(solution)/shard_map/ppermute | solution.py:39
  98.8 10.4 %copy-start.19 = (bf16[64,1024]{1,0:T(8,128)(2,1)}, bf16[64,1024]{1,0:T(8,128)(2,1)S(1)}, u32[]{:S(2)}) copy-start(bf16[64,1024]{1,0:T(8,128)(2,1)S(1)} %collective-permute-done.17.refs_7_) | copy-start | bytes 393220
  98.8 5.4 %collective-permute-start.18 = (bf16[64,1024]{1,0:T(8,128)(2,1)S(1)}, bf16[64,1024]{1,0:T(8,128)(2,1)S(1)}, u32[]{:S(2)}, u32[]{:S(2)}) collective-permute-start(bf16[64,1024]{1,0:T(8,128)(2,1)S(1)} %collective-permute-done.17.refs_7_), channel_id=1, source_target_pairs={{0,32},{8,40},{16,48},{24,56},{32,64},{40,72},{48,80},{56,88},{64,... | collective-permute-start | bytes 393224 | tf_op jit(solution)/shard_map/ppermute | solution.py:39
  98.8 10.4 %copy-start.20 = (bf16[64,1024]{1,0:T(8,128)(2,1)}, bf16[64,1024]{1,0:T(8,128)(2,1)S(1)}, u32[]{:S(2)}) copy-start(bf16[64,1024]{1,0:T(8,128)(2,1)S(1)} %collective-permute-done.14.refs_2_) | copy-start | bytes 393220
  98.9 5.4 %collective-permute-start.15 = (bf16[64,1024]{1,0:T(8,128)(2,1)S(1)}, bf16[64,1024]{1,0:T(8,128)(2,1)S(1)}, u32[]{:S(2)}, u32[]{:S(2)}) collective-permute-start(bf16[64,1024]{1,0:T(8,128)(2,1)S(1)} %collective-permute-done.14.refs_2_), channel_id=1, source_target_pairs={{0,224},{8,232},{16,240},{24,248},{32,0},{40,8},{48,16},{56,24},{6... | collective-permute-start | bytes 393224 | tf_op jit(solution)/shard_map/ppermute | solution.py:39
  104.2 5.1 %copy-start.21 = (bf16[64,1024]{1,0:T(8,128)(2,1)}, bf16[64,1024]{1,0:T(8,128)(2,1)S(1)}, u32[]{:S(2)}) copy-start(bf16[64,1024]{1,0:T(8,128)(2,1)S(1)} %collective-permute-done.18.refs_6_) | copy-start | bytes 393220
  104.2 5.0 %collective-permute-start.19 = (bf16[64,1024]{1,0:T(8,128)(2,1)S(1)}, bf16[64,1024]{1,0:T(8,128)(2,1)S(1)}, u32[]{:S(2)}, u32[]{:S(2)}) collective-permute-start(bf16[64,1024]{1,0:T(8,128)(2,1)S(1)} %collective-permute-done.18.refs_6_), channel_id=1, source_target_pairs={{0,32},{8,40},{16,48},{24,56},{32,64},{40,72},{48,80},{56,88},{64,... | collective-permute-start | bytes 393224 | tf_op jit(solution)/shard_map/ppermute | solution.py:39
  104.2 5.1 %copy-start.22 = (bf16[64,1024]{1,0:T(8,128)(2,1)}, bf16[64,1024]{1,0:T(8,128)(2,1)S(1)}, u32[]{:S(2)}) copy-start(bf16[64,1024]{1,0:T(8,128)(2,1)S(1)} %collective-permute-done.15.refs_3_) | copy-start | bytes 393220
  104.2 5.0 %collective-permute-start.16 = (bf16[64,1024]{1,0:T(8,128)(2,1)S(1)}, bf16[64,1024]{1,0:T(8,128)(2,1)S(1)}, u32[]{:S(2)}, u32[]{:S(2)}) collective-permute-start(bf16[64,1024]{1,0:T(8,128)(2,1)S(1)} %collective-permute-done.15.refs_3_), channel_id=1, source_target_pairs={{0,224},{8,232},{16,240},{24,248},{32,0},{40,8},{48,16},{56,24},{6... | collective-permute-start | bytes 393224 | tf_op jit(solution)/shard_map/ppermute | solution.py:39
  107.4 1.9 %copy-start.13 = (bf16[1024,256]{1,0:T(8,128)(2,1)}, bf16[1024,256]{1,0:T(8,128)(2,1)S(1)}, u32[]{:S(2)}) copy-start(bf16[1024,256]{1,0:T(8,128)(2,1)S(1)} %collective-permute-done.20.refs_9_) | copy-start | bytes 1572868
  107.4 1.9 %copy-start.14 = (bf16[1024,256]{1,0:T(8,128)(2,1)}, bf16[1024,256]{1,0:T(8,128)(2,1)S(1)}, u32[]{:S(2)}) copy-start(bf16[1024,256]{1,0:T(8,128)(2,1)S(1)} %collective-permute-done.22.refs_11_) | copy-start | bytes 1572868
  109.9 0.7 copy-start.24
  (1 other events, 0.6 us)

commit v3 on v2

--- a/solution.py
+++ b/solution.py
@@ -69,7 +69,7 @@
         m_in, acc_in = take(2)
     if last:
         new_refs = take(8)
-        q_rank, k_rank = take(2)
+        ids, span = take(2)
         out_refs = take(BLOCKS)
     m_all, acc = take(2)
     q_all, k_all, v_all, s0, s1, p0, p1, scale0, scale1 = take(9)
@@ -166,7 +166,14 @@
     values = jnp.concatenate([new_v[...].T, ones16], axis=0)
     scores(s0, new_k[...], left)
     scores(s1, new_k[...], right)
-    ranks = k_rank[:, 0:1]
+
+    def rank(i):
+        return span[pl.ds(ids[i], 1), :].astype(F32)
+
+    q_rank = jnp.concatenate([rank(b) for b in range(BLOCKS) for _ in range(QPH)], axis=1)
+    k_rank = jnp.concatenate([rank(BLOCKS + s) for s in range(8)], axis=0)
+    k_rank = jnp.concatenate([k_rank, jnp.zeros((8, HD - TOK), F32)], axis=1).T
+    ranks = jnp.concatenate([k_rank[0:TOK, s : s + 1] for s in range(8)], axis=0)
     weigh(jnp.where(ranks <= q_rank[:, left], s0[...], NEG_FILL), p0, scale0, left)
     add(p0, scale0, values, left)
     weigh(jnp.where(ranks <= q_rank[:, right], s1[...], NEG_FILL), p1, scale1, right)
@@ -187,7 +194,7 @@
         out_refs[b][:, QPH * HD : WIDE] = stats.T.astype(BF16)
 
 
-def attention(q_blocks, shards, state=None, new=None, q_rank=None, k_rank=None):
+def attention(q_blocks, shards, state=None, new=None, ids=None, span=None):
     first, last = state is None, new is not None
     m_shape, acc_shape = (1, BLOCKS * ROWS), (VROWS, BLOCKS * ROWS)
     args = [*q_blocks, *shards]
@@ -209,8 +216,9 @@
         pltpu.VMEM((1, TILE), F32),
     ]
     if last:
-        args += [*new, q_rank, k_rank]
-        specs += [pl.BlockSpec((2 * TOK, HD), lambda i: (0, 0))] * 8 + [whole] * 2
+        args += [*new, ids, span]
+        specs += [pl.BlockSpec((2 * TOK, HD), lambda i: (0, 0))] * 8
+        specs += [pl.BlockSpec(memory_space=pltpu.SMEM), whole]
         out_shape = [jax.ShapeDtypeStruct((TOK, WIDE), BF16)] * BLOCKS
         out_specs = [whole] * BLOCKS
         scratch = [
@@ -304,28 +312,28 @@
     kv_two = seq_permute(sent, lambda z, y, c: (z - 2 if z % 2 == 0 else z + 2, y, c))
     q_blocks = (q_cross, q_far, q_side, queries)
 
-    ranks = span_rank.reshape(Z, YC, TOK)
-    two = jnp.where(z % 2 == 0, z + 2, z - 2)
-    near = ranks[jnp.stack([z, z + 1, z - 1, two]) % Z]
-    k_rank = near[:, jnp.stack([yc, yc ^ 1])].reshape(8 * TOK, 1)
-    k_rank = jnp.broadcast_to(k_rank, (8 * TOK, HD))
-    both = ranks[jnp.stack([z + 4, z]) % Z]
-    q_rank = both[:, jnp.stack([yc ^ 2, yc])].reshape(BLOCKS, TOK)
-    q_rank = jnp.tile(q_rank, (1, QPH)).reshape(1, BLOCKS * ROWS)
-
-    q_rank, k_rank, own = lax.optimization_barrier((q_rank, k_rank, own))
-    own_pair = (own, own_pair[1])
+    two = jnp.where(z % 2 == 0, z + 2, z + 6)
+    row = lambda z, i: z % Z * YC + i
+    ids = [row(z + 4, yc ^ 2), row(z + 4, yc), row(z, yc ^ 2), row(z, yc)]
+    for n in (z, z + 1, z + 7, two):
+        ids += [row(n, yc), row(n, yc ^ 1)]
+    ids, span = jnp.stack(ids), span_rank.reshape(Z * YC, TOK)
+
     state = attention(q_blocks, own_pair)
     kv_up, kv_down, *state = lax.optimization_barrier((kv_up, kv_down, *state))
     next_pairs = (kv_up, over_c(kv_up), kv_down, over_c(kv_down))
     weight = lax.optimization_barrier((out_weight, kv_up, kv_down))[0]
-    weight_y = over_y(weight)
-    weights = [out_weight, over_c(weight), weight_y, over_c(weight_y)]
+    weight_y, weight_c = over_y(weight), over_c(weight)
     state = attention(q_blocks, next_pairs, state)
-    kv_two, *state = lax.optimization_barrier((kv_two, *state))
+    kv_two, weight_y, weight_c, *state = lax.optimization_barrier(
+        (kv_two, weight_y, weight_c, *state)
+    )
     last_pair = (kv_two, over_c(kv_two))
+    weight_yc = over_c(weight_y)
     new = (*own_pair, *next_pairs, *last_pair)
-    cross, far, side, mine = attention(q_blocks, last_pair, state, new, q_rank, k_rank)
+    parts = attention(q_blocks, last_pair, state, new, ids, span)
+    weight_yc, cross, far, side, mine = lax.optimization_barrier((weight_yc, *parts))
+    weights = [out_weight, weight_c, weight_y, weight_yc]
     cross = seq_permute(cross, lambda z, y, c: (z + 4, 1 - y, c))
     attended = merge((cross, shift(far, 4), over_y(side), mine))
 
@@ -337,9 +345,8 @@
     blocks[4] = shift(blocks[3], -1)
     shares = product(jnp.stack([z, yc]), blocks, weights)
     shares = lax.all_to_all(shares, "head", 0, 0, tiled=True)
-    projected = jnp.sum(shares.astype(F32), axis=0).astype(BF16)
-    projected = lax.all_to_all(projected, "seq", 0, 0, axis_index_groups=PLANES, tiled=True)
-    return projected.reshape(YC * TOK, 256)
+    projected = jnp.sum(shares.astype(F32), axis=0).astype(BF16).reshape(YC * TOK, 256)
+    return lax.all_to_all(projected, "seq", 0, 0, axis_index_groups=PLANES, tiled=True)
 
 
 def solution(mesh):

time: 146 us -> 152 us (1.041)
  waiting for transfers between devices: 15.1 us -> 24.3 us
  starting transfers between devices: 47.1 us -> 40.4 us
  Pallas kernels: 41.1 us -> 44.6 us
  blocking collectives: 30.1 us -> 32 us
  local copies, waits for them, and re-layouts: 10.5 us -> 8.8 us
    ppermute x23, waiting for transfers between devices: 15.1 us -> 24.3 us  [seq_permute(): return lax.ppermute(value, 'seq', pairs)]
    ppermute x23, starting transfers between devices: 47.1 us -> 40.4 us  [seq_permute(): return lax.ppermute(value, 'seq', pairs)]
    pallas_call x3, Pallas kernels: 32.7 us -> 36.1 us  [attention(): pl.pallas_call(functools.partial(attention_kernel, len(shards), first, la...]
    gather x8 -> x0, local copies, waits for them, and re-layouts: 2.3 us -> none  [the longest x2 0.58 us: body(): k_rank = near[:, jnp.stack([yc, yc ^ 1])].reshape(8 * TOK, 1)]
    all_to_all x1, blocking collectives: 11.5 us -> 13.3 us  [body(): lax.all_to_all(projected, 'seq', 0, 0, axis_index_groups=PLANES, tiled=True)]
  transfers between devices with their start and end apart: 23 -> 23, of which waited for: 8 -> 8; matrix products, arithmetic and copies ran while one was open for 3% -> 1% of each run, Pallas kernels for 25% -> 25%
where the time goes in v3:
time: 152 us
  Pallas kernels  44.6 us (29%)
  starting transfers between devices  40.4 us (27%)
  blocking collectives  32 us (21%)
  waiting for transfers between devices  24.3 us (16%)
  local copies, waits for them, and re-layouts  8.8 us (6%)
    ppermute x23, starting transfers between devices, seq_permute(): return lax.ppermute(value, 'seq', pairs)  40.4 us
    pallas_call x3, Pallas kernels, attention(): pl.pallas_call(functools.partial(attention_kernel, len(shards), first, la...  36.1 us
    ppermute x23, waiting for transfers between devices, seq_permute(): return lax.ppermute(value, 'seq', pairs)  24.3 us
    all_to_all x1, blocking collectives, body(): shares = lax.all_to_all(shares, 'head', 0, 0, tiled=True)  18.6 us
    all_to_all x1, blocking collectives, body(): lax.all_to_all(projected, 'seq', 0, 0, axis_index_groups=PLANES, tiled=True)  13.3 us
    unnamed x53, local copies, waits for them, and re-layouts  7.46 us
    pallas_call x1, Pallas kernels, product(): pl.pallas_call(product_kernel, out_shape=jax.ShapeDtypeStruct((Z, YC, TOK...  4.3 us
  transfers between devices with their start and end apart: 23, of which 8 were waited for; matrix products, arithmetic and copies ran while one was open for 1% of the time, Pallas kernels for 25%

profile of v3, /device:TPU:1, one launch (start us, length us, event | category | flops | bytes accessed | tf_op | source)
XLA Modules:
  0.0 151.6 jit_solution(16893928248205442917)
XLA Ops:
  0.0 7.7 %collective-permute-start = (bf16[64,1024]{1,0:T(8,128)(2,1)}, bf16[64,1024]{1,0:T(8,128)(2,1)S(1)}, u32[]{:S(2)}, u32[]{:S(2)}) collective-permute-start(bf16[64,1024]{1,0:T(8,128)(2,1)} %refs_3_.5), channel_id=1, source_target_pairs={{0,128},{8,136},{16,144},{24,152},{32,160},{40,168},{48,176},{56,1... | collective-permute-start | bytes 393224 | tf_op jit(solution)/shard_map/ppermute | solution.py:39
  8.4 1.9 %pack.1.refs_4_.refs_8_ = bf16[2192,128]{1,0:T(8,128)(2,1)} custom-call(s32[1]{0:T(128)S(6)} %copy.10.length_ref, bf16[1,1024,128]{2,1,0:T(8,128)(2,1)} %k_ref.1, bf16[1,1024,128]{2,1,0:T(8,128)(2,1)} %v_ref.1, bf16[64,128]{1,0:T(8,128)(2,1)} %nk_ref.1, bf16[64,128]{1,0:T(8,128)(2,1)} %nv_ref.1), custom_call_target="tpu_custom_call" | custom-call | tf_op jit(solution)/shard_map/pack/pallas_call | solution.py:55
  10.3 1.0 collective-permute-start.6
  11.2 5.6 %collective-permute-start.3 = (bf16[2192,128]{1,0:T(8,128)(2,1)}, bf16[2192,128]{1,0:T(8,128)(2,1)S(1)}, u32[]{:S(2)}, u32[]{:S(2)}) collective-permute-start(bf16[2192,128]{1,0:T(8,128)(2,1)} %pack.1.refs_4_.refs_8_), channel_id=1, source_target_pairs={{0,224},{8,232},{16,240},{24,248},{32,0},{40,8},{48,16},{56,24},{6... | collective-permute-start | bytes 1683464 | tf_op jit(solution)/shard_map/ppermute | solution.py:39
  16.9 1.3 collective-permute-start.1
  18.2 0.2 collective-permute-start.5
  18.3 2.6 %collective-permute-done.1.refs_0_ = bf16[64,1024]{1,0:T(8,128)(2,1)S(1)} collective-permute-done((bf16[64,1024]{1,0:T(8,128)(2,1)S(1)}, bf16[64,1024]{1,0:T(8,128)(2,1)S(1)}, u32[]{:S(2)}, u32[]{:S(2)}) %collective-permute-start.1) | collective-permute-done | bytes 131104 | tf_op jit(solution)/shard_map/ppermute | solution.py:39
  21.0 2.9 %collective-permute-done.5.refs_2_ = bf16[64,1024]{1,0:T(8,128)(2,1)S(1)} collective-permute-done((bf16[64,1024]{1,0:T(8,128)(2,1)}, bf16[64,1024]{1,0:T(8,128)(2,1)S(1)}, u32[]{:S(2)}, u32[]{:S(2)}) %collective-permute-start.5) | collective-permute-done | bytes 131104 | tf_op jit(solution)/shard_map/ppermute | solution.py:39
  23.9 0.6 copy-done.10
  24.5 0.8 copy-done.1
  25.3 8.8 %attention.3 = (f32[1,2048]{1,0:T(1,128)}, f32[144,2048]{1,0:T(8,128)}) custom-call(bf16[64,1024]{1,0:T(8,128)(2,1)} %copy-done.9, bf16[64,1024]{1,0:T(8,128)(2,1)} %copy-done.8, bf16[64,1024]{1,0:T(8,128)(2,1)} %copy-done.10, bf16[64,1024]{1,0:T(8,128)(2,1)} %refs_3_.5, bf16[2192,128]{1,0:T(8,128)(2,1)} %pack.1.refs_4_.refs_8_, bf16[2192,128]{1,0:T(8,128)(2,1)} %copy-done.1), custom_call_target="tpu_custom_call" | custom-call | flops 1 | bytes 1 | tf_op jit(solution)/shard_map/attention/pallas_call | solution.py:234
  34.2 1.8 %collective-permute-start.10 = (bf16[2192,128]{1,0:T(8,128)(2,1)S(1)}, bf16[2192,128]{1,0:T(8,128)(2,1)S(1)}, u32[]{:S(2)}, u32[]{:S(2)}) collective-permute-start(bf16[2192,128]{1,0:T(8,128)(2,1)S(1)} %collective-permute-done.4.refs_6_.refs_12_), channel_id=1, source_target_pairs={{0,8},{8,0},{16,24},{24,16},{32,40},{40,32},{48,56},{56,48},{64,72... | collective-permute-start | bytes 1683464 | tf_op jit(solution)/shard_map/ppermute | solution.py:39
  36.0 0.1 collective-permute-start.9
  36.1 1.3 collective-permute-start.2
  37.4 4.4 %collective-permute-start.7 = (bf16[1024,256]{1,0:T(8,128)(2,1)S(1)}, bf16[1024,256]{1,0:T(8,128)(2,1)S(1)}, u32[]{:S(2)}, u32[]{:S(2)}) collective-permute-start(bf16[1024,256]{1,0:T(8,128)(2,1)S(1)} %copy-done.11), channel_id=1, source_target_pairs={{0,16},{8,24},{16,0},{24,8},{32,48},{40,56},{48,32},{56,40},{64,80... | collective-permute-start | bytes 1572872 | tf_op jit(solution)/shard_map/ppermute | solution.py:39
  41.8 1.0 collective-permute-start.8
  42.8 0.8 copy-done.4
  43.6 0.8 copy-done.5
  44.4 16.4 %attention.4 = (f32[1,2048]{1,0:T(1,128)}, f32[144,2048]{1,0:T(8,128)}) custom-call(bf16[64,1024]{1,0:T(8,128)(2,1)} %copy-done.9, bf16[64,1024]{1,0:T(8,128)(2,1)} %copy-done.8, bf16[64,1024]{1,0:T(8,128)(2,1)} %copy-done.10, bf16[64,1024]{1,0:T(8,128)(2,1)} %refs_3_.5, bf16[2192,128]{1,0:T(8,128)(2,1)} %copy-done.2, bf16[2192,128]{1,0:T(8,128)(2,1)} %copy-done.5, ...), custom_call_target="tpu_custom_call" | custom-call | flops 1 | bytes 1 | tf_op jit(solution)/shard_map/attention/pallas_call | solution.py:234
  60.9 0.9 copy-done.13
  61.7 0.5 collective-permute-start.11
  62.2 0.7 reshape.7.refs_17_
  62.9 0.7 stack.60.refs_16_
  63.6 0.1 collective-permute-done.12.refs_5_.refs_15_
  63.7 0.8 copy-done.7
  64.5 10.9 %attention.5 = (bf16[64,1152]{1,0:T(8,128)(2,1)}, bf16[64,1152]{1,0:T(8,128)(2,1)}, bf16[64,1152]{1,0:T(8,128)(2,1)}, bf16[64,1152]{1,0:T(8,128)(2,1)}) custom-call(bf16[64,1024]{1,0:T(8,128)(2,1)} %copy-done.9, bf16[64,1024]{1,0:T(8,128)(2,1)} %copy-done.8, bf16[64,1024]{1,0:T(8,128)(2,1)} %copy-done.10, bf16[64,1024]{1,0:T(8,128)(2,1)} %refs_3_.5, ...), custom_call_target="tpu_custom_call" | custom-call | flops 1 | bytes 1 | tf_op jit(solution)/shard_map/attention/pallas_call | solution.py:234
  75.5 0.6 collective-permute-start.13
  76.1 2.7 %collective-permute-start.14 = (bf16[64,1152]{1,0:T(8,128)(2,1)}, bf16[64,1152]{1,0:T(8,128)(2,1)S(1)}, u32[]{:S(2)}, u32[]{:S(2)}) collective-permute-start(bf16[64,1152]{1,0:T(8,128)(2,1)} %get-tuple-element.54), channel_id=1, source_target_pairs={{0,128},{8,136},{16,144},{24,152},{32,160},{40,168},{48,176},{56,1... | collective-permute-start | bytes 442376 | tf_op jit(solution)/shard_map/ppermute | solution.py:39
  78.8 3.3 %collective-permute-start.15 = (bf16[64,1152]{1,0:T(8,128)(2,1)}, bf16[64,1152]{1,0:T(8,128)(2,1)S(1)}, u32[]{:S(2)}, u32[]{:S(2)}) collective-permute-start(bf16[64,1152]{1,0:T(8,128)(2,1)} %get-tuple-element.55), channel_id=1, source_target_pairs={{0,16},{8,24},{16,0},{24,8},{32,48},{40,56},{48,32},{56,40},{64,80... | collective-permute-start | bytes 442376 | tf_op jit(solution)/shard_map/ppermute | solution.py:39
  82.1 9.8 %collective-permute-done.13.refs_0_ = bf16[64,1152]{1,0:T(8,128)(2,1)S(1)} collective-permute-done((bf16[64,1152]{1,0:T(8,128)(2,1)}, bf16[64,1152]{1,0:T(8,128)(2,1)S(1)}, u32[]{:S(2)}, u32[]{:S(2)}) %collective-permute-start.13) | collective-permute-done | bytes 147488 | tf_op jit(solution)/shard_map/ppermute | solution.py:39
  91.9 0.6 copy-done.15
  92.6 0.7 copy-done.17
  93.3 2.3 %merge.1.refs_0_ = bf16[64,1024]{1,0:T(8,128)(2,1)} custom-call(bf16[64,1152]{1,0:T(8,128)(2,1)} %copy-done.15, bf16[64,1152]{1,0:T(8,128)(2,1)} %copy-done.16, bf16[64,1152]{1,0:T(8,128)(2,1)} %copy-done.17, bf16[64,1152]{1,0:T(8,128)(2,1)} %get-tuple-element.56.refs_3_), custom_call_target="tpu_custom_call" | custom-call | tf_op jit(solution)/shard_map/merge/pallas_call | solution.py:266
  95.5 1.5 collective-permute-start.20
  97.0 3.3 %collective-permute-done.16.refs_1_ = bf16[64,1024]{1,0:T(8,128)(2,1)S(1)} collective-permute-done((bf16[64,1024]{1,0:T(8,128)(2,1)}, bf16[64,1024]{1,0:T(8,128)(2,1)S(1)}, u32[]{:S(2)}, u32[]{:S(2)}) %collective-permute-start.16) | collective-permute-done | bytes 131104 | tf_op jit(solution)/shard_map/ppermute | solution.py:39
  100.3 1.5 %collective-permute-start.17 = (bf16[64,1024]{1,0:T(8,128)(2,1)S(1)}, bf16[64,1024]{1,0:T(8,128)(2,1)S(1)}, u32[]{:S(2)}, u32[]{:S(2)}) collective-permute-start(bf16[64,1024]{1,0:T(8,128)(2,1)S(1)} %collective-permute-done.16.refs_1_), channel_id=1, source_target_pairs={{0,224},{8,232},{16,240},{24,248},{32,0},{40,8},{48,16},{56,24},{6... | collective-permute-start | bytes 393224 | tf_op jit(solution)/shard_map/ppermute | solution.py:39
  101.9 2.3 %collective-permute-done.17.refs_2_ = bf16[64,1024]{1,0:T(8,128)(2,1)S(1)} collective-permute-done((bf16[64,1024]{1,0:T(8,128)(2,1)S(1)}, bf16[64,1024]{1,0:T(8,128)(2,1)S(1)}, u32[]{:S(2)}, u32[]{:S(2)}) %collective-permute-start.17) | collective-permute-done | bytes 131104 | tf_op jit(solution)/shard_map/ppermute | solution.py:39
  104.1 2.7 %collective-permute-start.18 = (bf16[64,1024]{1,0:T(8,128)(2,1)S(1)}, bf16[64,1024]{1,0:T(8,128)(2,1)S(1)}, u32[]{:S(2)}, u32[]{:S(2)}) collective-permute-start(bf16[64,1024]{1,0:T(8,128)(2,1)S(1)} %collective-permute-done.17.refs_2_), channel_id=1, source_target_pairs={{0,224},{8,232},{16,240},{24,248},{32,0},{40,8},{48,16},{56,24},{6... | collective-permute-start | bytes 393224 | tf_op jit(solution)/shard_map/ppermute | solution.py:39
  106.9 1.9 %collective-permute-done.18.refs_3_ = bf16[64,1024]{1,0:T(8,128)(2,1)S(1)} collective-permute-done((bf16[64,1024]{1,0:T(8,128)(2,1)S(1)}, bf16[64,1024]{1,0:T(8,128)(2,1)S(1)}, u32[]{:S(2)}, u32[]{:S(2)}) %collective-permute-start.18) | collective-permute-done | bytes 131104 | tf_op jit(solution)/shard_map/ppermute | solution.py:39
  108.8 3.1 %collective-permute-start.19 = (bf16[64,1024]{1,0:T(8,128)(2,1)S(1)}, bf16[64,1024]{1,0:T(8,128)(2,1)S(1)}, u32[]{:S(2)}, u32[]{:S(2)}) collective-permute-start(bf16[64,1024]{1,0:T(8,128)(2,1)S(1)} %collective-permute-done.18.refs_3_), channel_id=1, source_target_pairs={{0,224},{8,232},{16,240},{24,248},{32,0},{40,8},{48,16},{56,24},{6... | collective-permute-start | bytes 393224 | tf_op jit(solution)/shard_map/ppermute | solution.py:39
  111.9 0.6 pad_add_fusion.place_ref
  112.5 1.3 collective-permute-done.19.refs_4_
  113.9 0.6 copy-done.24
  114.5 4.3 %product.1 = bf16[8,4,64,256]{3,2,1,0:T(8,128)(2,1)} custom-call(s32[2]{0:T(128)} %pad_add_fusion.place_ref, bf16[64,1024]{1,0:T(8,128)(2,1)} %merge.1.refs_0_, bf16[64,1024]{1,0:T(8,128)(2,1)} %copy-done.18, bf16[64,1024]{1,0:T(8,128)(2,1)} %copy-done.20, bf16[64,1024]{1,0:T(8,128)(2,1)} %copy-done.22, bf16[64,1024]{1,0:T(8,128)(2,1)} %copy-done.24, ...), custom_call_target="tpu_custom_call" | custom-call | tf_op jit(solution)/shard_map/product/pallas_call | solution.py:286
  118.8 18.6 %all_to_all.14 = bf16[8,4,64,256]{3,2,1,0:T(8,128)(2,1)S(1)} all-to-all(bf16[8,4,64,256]{3,2,1,0:T(8,128)(2,1)} %product.1), channel_id=1, replica_groups=mesh['seq'=32,'head'=8] {'head'}, dimensions={0} | all-to-all | bytes 2097152 | tf_op jit(solution)/shard_map/all_to_all | solution.py:347
  137.5 0.1 reduce_sum.12
  137.6 13.3 %all_to_all.15 = bf16[4,64,256]{2,1,0:T(8,128)(2,1)S(1)} all-to-all(bf16[4,64,256]{2,1,0:T(8,128)(2,1)S(1)} %reduce_sum.12), channel_id=1, replica_groups={{0,8,16,24},{32,40,48,56},{64,72,80,88},{96,104,112,120},{128,136,144,1..., dimensions={0} | all-to-all | bytes 262144 | tf_op jit(solution)/shard_map/all_to_all | solution.py:349
  151.0 0.7 copy.11
  (63 shorter events, 0.2 us)
Async XLA Ops:
  0.0 11.2 %collective-permute-start = (bf16[64,1024]{1,0:T(8,128)(2,1)}, bf16[64,1024]{1,0:T(8,128)(2,1)S(1)}, u32[]{:S(2)}, u32[]{:S(2)}) collective-permute-start(bf16[64,1024]{1,0:T(8,128)(2,1)} %refs_3_.5), channel_id=1, source_target_pairs={{0,128},{8,136},{16,144},{24,152},{32,160},{40,168},{48,176},{56,1... | collective-permute-start | bytes 393224 | tf_op jit(solution)/shard_map/ppermute | solution.py:39
  10.3 25.8 %copy-start = (bf16[2192,128]{1,0:T(8,128)(2,1)S(1)}, bf16[2192,128]{1,0:T(8,128)(2,1)}, u32[]{:S(2)}) copy-start(bf16[2192,128]{1,0:T(8,128)(2,1)} %pack.1.refs_4_.refs_8_) | copy-start | bytes 1683460
  10.3 27.1 %copy-start.11 = (bf16[1024,256]{1,0:T(8,128)(2,1)S(1)}, bf16[1024,256]{1,0:T(8,128)(2,1)}, u32[]{:S(2)}) copy-start(bf16[1024,256]{1,0:T(8,128)(2,1)} %refs_8_.1) | copy-start | bytes 1572868
  10.3 13.6 %collective-permute-start.6 = (bf16[2192,128]{1,0:T(8,128)(2,1)}, bf16[2192,128]{1,0:T(8,128)(2,1)S(1)}, u32[]{:S(2)}, u32[]{:S(2)}) collective-permute-start(bf16[2192,128]{1,0:T(8,128)(2,1)} %pack.1.refs_4_.refs_8_), channel_id=1, source_target_pairs={{0,8},{8,0},{16,24},{24,16},{32,40},{40,32},{48,56},{56,48},{64,72... | collective-permute-start | bytes 1683464 | tf_op jit(solution)/shard_map/ppermute | solution.py:39
  11.2 12.7 %copy-start.8 = (bf16[64,1024]{1,0:T(8,128)(2,1)}, bf16[64,1024]{1,0:T(8,128)(2,1)S(1)}, u32[]{:S(2)}) copy-start(bf16[64,1024]{1,0:T(8,128)(2,1)S(1)} %collective-permute-done.refs_1_) | copy-start | bytes 393220
  11.2 22.9 %collective-permute-start.3 = (bf16[2192,128]{1,0:T(8,128)(2,1)}, bf16[2192,128]{1,0:T(8,128)(2,1)S(1)}, u32[]{:S(2)}, u32[]{:S(2)}) collective-permute-start(bf16[2192,128]{1,0:T(8,128)(2,1)} %pack.1.refs_4_.refs_8_), channel_id=1, source_target_pairs={{0,224},{8,232},{16,240},{24,248},{32,0},{40,8},{48,16},{56,24},{6... | collective-permute-start | bytes 1683464 | tf_op jit(solution)/shard_map/ppermute | solution.py:39
  16.9 17.3 %collective-permute-start.4 = (bf16[2192,128]{1,0:T(8,128)(2,1)}, bf16[2192,128]{1,0:T(8,128)(2,1)S(1)}, u32[]{:S(2)}, u32[]{:S(2)}) collective-permute-start(bf16[2192,128]{1,0:T(8,128)(2,1)} %pack.1.refs_4_.refs_8_), channel_id=1, source_target_pairs={{0,32},{8,40},{16,48},{24,56},{32,64},{40,72},{48,80},{56,88},{64,... | collective-permute-start | bytes 1683464 | tf_op jit(solution)/shard_map/ppermute | solution.py:39
  16.9 4.1 %collective-permute-start.1 = (bf16[64,1024]{1,0:T(8,128)(2,1)S(1)}, bf16[64,1024]{1,0:T(8,128)(2,1)S(1)}, u32[]{:S(2)}, u32[]{:S(2)}) collective-permute-start(bf16[64,1024]{1,0:T(8,128)(2,1)S(1)} %collective-permute-done.refs_1_), channel_id=1, source_target_pairs={{0,16},{8,24},{16,0},{24,8},{32,48},{40,56},{48,32},{56,40},{64,80... | collective-permute-start | bytes 393224 | tf_op jit(solution)/shard_map/ppermute | solution.py:39
  18.2 5.7 %collective-permute-start.5 = (bf16[64,1024]{1,0:T(8,128)(2,1)}, bf16[64,1024]{1,0:T(8,128)(2,1)S(1)}, u32[]{:S(2)}, u32[]{:S(2)}) collective-permute-start(bf16[64,1024]{1,0:T(8,128)(2,1)} %refs_3_.5), channel_id=1, source_target_pairs={{0,16},{8,24},{16,0},{24,8},{32,48},{40,56},{48,32},{56,40},{64,80... | collective-permute-start | bytes 393224 | tf_op jit(solution)/shard_map/ppermute | solution.py:39
  21.0 2.9 %copy-start.9 = (bf16[64,1024]{1,0:T(8,128)(2,1)}, bf16[64,1024]{1,0:T(8,128)(2,1)S(1)}, u32[]{:S(2)}) copy-start(bf16[64,1024]{1,0:T(8,128)(2,1)S(1)} %collective-permute-done.1.refs_0_) | copy-start | bytes 393220
  23.9 0.7 copy-start.10
  24.5 0.8 copy-start.1
  34.2 8.6 %copy-start.2 = (bf16[2192,128]{1,0:T(8,128)(2,1)}, bf16[2192,128]{1,0:T(8,128)(2,1)S(1)}, u32[]{:S(2)}) copy-start(bf16[2192,128]{1,0:T(8,128)(2,1)S(1)} %collective-permute-done.3.refs_4_.refs_10_) | copy-start | bytes 1683460
  34.2 8.6 %copy-start.3 = (bf16[2192,128]{1,0:T(8,128)(2,1)}, bf16[2192,128]{1,0:T(8,128)(2,1)S(1)}, u32[]{:S(2)}) copy-start(bf16[2192,128]{1,0:T(8,128)(2,1)S(1)} %collective-permute-done.4.refs_6_.refs_12_) | copy-start | bytes 1683460
  34.2 28.0 %copy-start.25 = (s32[2048]{0:T(1024)S(1)}, s32[2048]{0:T(1024)}, u32[]{:S(2)}) copy-start(s32[2048]{0:T(1024)} %param.14) | copy-start | bytes 24580
  34.2 8.6 %collective-permute-start.10 = (bf16[2192,128]{1,0:T(8,128)(2,1)S(1)}, bf16[2192,128]{1,0:T(8,128)(2,1)S(1)}, u32[]{:S(2)}, u32[]{:S(2)}) collective-permute-start(bf16[2192,128]{1,0:T(8,128)(2,1)S(1)} %collective-permute-done.4.refs_6_.refs_12_), channel_id=1, source_target_pairs={{0,8},{8,0},{16,24},{24,16},{32,40},{40,32},{48,56},{56,48},{64,72... | collective-permute-start | bytes 1683464 | tf_op jit(solution)/shard_map/ppermute | solution.py:39
  36.0 6.8 %collective-permute-start.9 = (bf16[2192,128]{1,0:T(8,128)(2,1)S(1)}, bf16[2192,128]{1,0:T(8,128)(2,1)S(1)}, u32[]{:S(2)}, u32[]{:S(2)}) collective-permute-start(bf16[2192,128]{1,0:T(8,128)(2,1)S(1)} %collective-permute-done.3.refs_4_.refs_10_), channel_id=1, source_target_pairs={{0,8},{8,0},{16,24},{24,16},{32,40},{40,32},{48,56},{56,48},{64,72... | collective-permute-start | bytes 1683464 | tf_op jit(solution)/shard_map/ppermute | solution.py:39
  36.1 24.7 %collective-permute-start.2 = (bf16[2192,128]{1,0:T(8,128)(2,1)S(1)}, bf16[2192,128]{1,0:T(8,128)(2,1)S(1)}, u32[]{:S(2)}, u32[]{:S(2)}) collective-permute-start(bf16[2192,128]{1,0:T(8,128)(2,1)S(1)} %copy-done), channel_id=1, source_target_pairs={{0,192},{8,200},{16,208},{24,216},{32,96},{40,104},{48,112},{56,12... | collective-permute-start | bytes 1683464 | tf_op jit(solution)/shard_map/ppermute | solution.py:39
  37.4 23.4 %collective-permute-start.7 = (bf16[1024,256]{1,0:T(8,128)(2,1)S(1)}, bf16[1024,256]{1,0:T(8,128)(2,1)S(1)}, u32[]{:S(2)}, u32[]{:S(2)}) collective-permute-start(bf16[1024,256]{1,0:T(8,128)(2,1)S(1)} %copy-done.11), channel_id=1, source_target_pairs={{0,16},{8,24},{16,0},{24,8},{32,48},{40,56},{48,32},{56,40},{64,80... | collective-permute-start | bytes 1572872 | tf_op jit(solution)/shard_map/ppermute | solution.py:39
  41.8 19.0 %collective-permute-start.8 = (bf16[1024,256]{1,0:T(8,128)(2,1)S(1)}, bf16[1024,256]{1,0:T(8,128)(2,1)S(1)}, u32[]{:S(2)}, u32[]{:S(2)}) collective-permute-start(bf16[1024,256]{1,0:T(8,128)(2,1)S(1)} %copy-done.11), channel_id=1, source_target_pairs={{0,8},{8,0},{16,24},{24,16},{32,40},{40,32},{48,56},{56,48},{64,72... | collective-permute-start | bytes 1572872 | tf_op jit(solution)/shard_map/ppermute | solution.py:39
  42.8 0.8 copy-start.4
  43.6 0.8 copy-start.5
  60.8 2.9 %copy-start.6 = (bf16[2192,128]{1,0:T(8,128)(2,1)}, bf16[2192,128]{1,0:T(8,128)(2,1)S(1)}, u32[]{:S(2)}) copy-start(bf16[2192,128]{1,0:T(8,128)(2,1)S(1)} %collective-permute-done.2.refs_4_.refs_14_) | copy-start | bytes 1683460
  60.8 14.6 %copy-start.12 = (bf16[1024,256]{1,0:T(8,128)(2,1)}, bf16[1024,256]{1,0:T(8,128)(2,1)S(1)}, u32[]{:S(2)}) copy-start(bf16[1024,256]{1,0:T(8,128)(2,1)S(1)} %collective-permute-done.7.refs_10_) | copy-start | bytes 1572868
  60.9 0.9 copy-start.13
  61.7 2.0 %collective-permute-start.12 = (bf16[2192,128]{1,0:T(8,128)(2,1)S(1)}, bf16[2192,128]{1,0:T(8,128)(2,1)S(1)}, u32[]{:S(2)}, u32[]{:S(2)}) collective-permute-start(bf16[2192,128]{1,0:T(8,128)(2,1)S(1)} %collective-permute-done.2.refs_4_.refs_14_), channel_id=1, source_target_pairs={{0,8},{8,0},{16,24},{24,16},{32,40},{40,32},{48,56},{56,48},{64,72... | collective-permute-start | bytes 1683464 | tf_op jit(solution)/shard_map/ppermute | solution.py:39
  61.7 13.7 %collective-permute-start.11 = (bf16[1024,256]{1,0:T(8,128)(2,1)S(1)}, bf16[1024,256]{1,0:T(8,128)(2,1)S(1)}, u32[]{:S(2)}, u32[]{:S(2)}) collective-permute-start(bf16[1024,256]{1,0:T(8,128)(2,1)S(1)} %collective-permute-done.7.refs_10_), channel_id=1, source_target_pairs={{0,8},{8,0},{16,24},{24,16},{32,40},{40,32},{48,56},{56,48},{64,72... | collective-permute-start | bytes 1572872 | tf_op jit(solution)/shard_map/ppermute | solution.py:39
  63.7 0.8 copy-start.7
  75.5 38.4 %copy-start.14 = (bf16[1024,256]{1,0:T(8,128)(2,1)}, bf16[1024,256]{1,0:T(8,128)(2,1)S(1)}, u32[]{:S(2)}) copy-start(bf16[1024,256]{1,0:T(8,128)(2,1)S(1)} %collective-permute-done.11.refs_11_) | copy-start | bytes 1572868
  75.5 16.4 %collective-permute-start.13 = (bf16[64,1152]{1,0:T(8,128)(2,1)}, bf16[64,1152]{1,0:T(8,128)(2,1)S(1)}, u32[]{:S(2)}, u32[]{:S(2)}) collective-permute-start(bf16[64,1152]{1,0:T(8,128)(2,1)} %get-tuple-element.53), channel_id=1, source_target_pairs={{0,144},{8,152},{16,128},{24,136},{32,176},{40,184},{48,160},{56,1... | collective-permute-start | bytes 442376 | tf_op jit(solution)/shard_map/ppermute | solution.py:39
  76.1 15.8 %collective-permute-start.14 = (bf16[64,1152]{1,0:T(8,128)(2,1)}, bf16[64,1152]{1,0:T(8,128)(2,1)S(1)}, u32[]{:S(2)}, u32[]{:S(2)}) collective-permute-start(bf16[64,1152]{1,0:T(8,128)(2,1)} %get-tuple-element.54), channel_id=1, source_target_pairs={{0,128},{8,136},{16,144},{24,152},{32,160},{40,168},{48,176},{56,1... | collective-permute-start | bytes 442376 | tf_op jit(solution)/shard_map/ppermute | solution.py:39
  78.8 13.1 %collective-permute-start.15 = (bf16[64,1152]{1,0:T(8,128)(2,1)}, bf16[64,1152]{1,0:T(8,128)(2,1)S(1)}, u32[]{:S(2)}, u32[]{:S(2)}) collective-permute-start(bf16[64,1152]{1,0:T(8,128)(2,1)} %get-tuple-element.55), channel_id=1, source_target_pairs={{0,16},{8,24},{16,0},{24,8},{32,48},{40,56},{48,32},{56,40},{64,80... | collective-permute-start | bytes 442376 | tf_op jit(solution)/shard_map/ppermute | solution.py:39
  91.9 0.7 copy-start.16
  92.6 0.7 copy-start.17
  95.5 4.8 %collective-permute-start.16 = (bf16[64,1024]{1,0:T(8,128)(2,1)}, bf16[64,1024]{1,0:T(8,128)(2,1)S(1)}, u32[]{:S(2)}, u32[]{:S(2)}) collective-permute-start(bf16[64,1024]{1,0:T(8,128)(2,1)} %merge.1.refs_0_), channel_id=1, source_target_pairs={{0,224},{8,232},{16,240},{24,248},{32,0},{40,8},{48,16},{56,24},{6... | collective-permute-start | bytes 393224 | tf_op jit(solution)/shard_map/ppermute | solution.py:39
  95.5 6.3 %collective-permute-start.20 = (bf16[64,1024]{1,0:T(8,128)(2,1)}, bf16[64,1024]{1,0:T(8,128)(2,1)S(1)}, u32[]{:S(2)}, u32[]{:S(2)}) collective-permute-start(bf16[64,1024]{1,0:T(8,128)(2,1)} %merge.1.refs_0_), channel_id=1, source_target_pairs={{0,32},{8,40},{16,48},{24,56},{32,64},{40,72},{48,80},{56,88},{64,... | collective-permute-start | bytes 393224 | tf_op jit(solution)/shard_map/ppermute | solution.py:39
  100.3 13.6 %copy-start.18 = (bf16[64,1024]{1,0:T(8,128)(2,1)}, bf16[64,1024]{1,0:T(8,128)(2,1)S(1)}, u32[]{:S(2)}) copy-start(bf16[64,1024]{1,0:T(8,128)(2,1)S(1)} %collective-permute-done.16.refs_1_) | copy-start | bytes 393220
  100.3 3.8 %collective-permute-start.17 = (bf16[64,1024]{1,0:T(8,128)(2,1)S(1)}, bf16[64,1024]{1,0:T(8,128)(2,1)S(1)}, u32[]{:S(2)}, u32[]{:S(2)}) collective-permute-start(bf16[64,1024]{1,0:T(8,128)(2,1)S(1)} %collective-permute-done.16.refs_1_), channel_id=1, source_target_pairs={{0,224},{8,232},{16,240},{24,248},{32,0},{40,8},{48,16},{56,24},{6... | collective-permute-start | bytes 393224 | tf_op jit(solution)/shard_map/ppermute | solution.py:39
  101.8 12.0 %copy-start.19 = (bf16[64,1024]{1,0:T(8,128)(2,1)}, bf16[64,1024]{1,0:T(8,128)(2,1)S(1)}, u32[]{:S(2)}) copy-start(bf16[64,1024]{1,0:T(8,128)(2,1)S(1)} %collective-permute-done.20.refs_7_) | copy-start | bytes 393220
  101.8 5.0 %collective-permute-start.21 = (bf16[64,1024]{1,0:T(8,128)(2,1)S(1)}, bf16[64,1024]{1,0:T(8,128)(2,1)S(1)}, u32[]{:S(2)}, u32[]{:S(2)}) collective-permute-start(bf16[64,1024]{1,0:T(8,128)(2,1)S(1)} %collective-permute-done.20.refs_7_), channel_id=1, source_target_pairs={{0,32},{8,40},{16,48},{24,56},{32,64},{40,72},{48,80},{56,88},{64,... | collective-permute-start | bytes 393224 | tf_op jit(solution)/shard_map/ppermute | solution.py:39
  104.1 9.7 %copy-start.20 = (bf16[64,1024]{1,0:T(8,128)(2,1)}, bf16[64,1024]{1,0:T(8,128)(2,1)S(1)}, u32[]{:S(2)}) copy-start(bf16[64,1024]{1,0:T(8,128)(2,1)S(1)} %collective-permute-done.17.refs_2_) | copy-start | bytes 393220
  104.1 4.7 %collective-permute-start.18 = (bf16[64,1024]{1,0:T(8,128)(2,1)S(1)}, bf16[64,1024]{1,0:T(8,128)(2,1)S(1)}, u32[]{:S(2)}, u32[]{:S(2)}) collective-permute-start(bf16[64,1024]{1,0:T(8,128)(2,1)S(1)} %collective-permute-done.17.refs_2_), channel_id=1, source_target_pairs={{0,224},{8,232},{16,240},{24,248},{32,0},{40,8},{48,16},{56,24},{6... | collective-permute-start | bytes 393224 | tf_op jit(solution)/shard_map/ppermute | solution.py:39
  106.9 7.0 %copy-start.21 = (bf16[64,1024]{1,0:T(8,128)(2,1)}, bf16[64,1024]{1,0:T(8,128)(2,1)S(1)}, u32[]{:S(2)}) copy-start(bf16[64,1024]{1,0:T(8,128)(2,1)S(1)} %collective-permute-done.21.refs_6_) | copy-start | bytes 393220
  106.9 5.7 %collective-permute-start.22 = (bf16[64,1024]{1,0:T(8,128)(2,1)S(1)}, bf16[64,1024]{1,0:T(8,128)(2,1)S(1)}, u32[]{:S(2)}, u32[]{:S(2)}) collective-permute-start(bf16[64,1024]{1,0:T(8,128)(2,1)S(1)} %collective-permute-done.21.refs_6_), channel_id=1, source_target_pairs={{0,32},{8,40},{16,48},{24,56},{32,64},{40,72},{48,80},{56,88},{64,... | collective-permute-start | bytes 393224 | tf_op jit(solution)/shard_map/ppermute | solution.py:39
  108.8 5.1 %copy-start.22 = (bf16[64,1024]{1,0:T(8,128)(2,1)}, bf16[64,1024]{1,0:T(8,128)(2,1)S(1)}, u32[]{:S(2)}) copy-start(bf16[64,1024]{1,0:T(8,128)(2,1)S(1)} %collective-permute-done.18.refs_3_) | copy-start | bytes 393220
  108.8 5.0 %collective-permute-start.19 = (bf16[64,1024]{1,0:T(8,128)(2,1)S(1)}, bf16[64,1024]{1,0:T(8,128)(2,1)S(1)}, u32[]{:S(2)}, u32[]{:S(2)}) collective-permute-start(bf16[64,1024]{1,0:T(8,128)(2,1)S(1)} %collective-permute-done.18.refs_3_), channel_id=1, source_target_pairs={{0,224},{8,232},{16,240},{24,248},{32,0},{40,8},{48,16},{56,24},{6... | collective-permute-start | bytes 393224 | tf_op jit(solution)/shard_map/ppermute | solution.py:39
  112.5 1.3 copy-start.23
  113.9 0.7 copy-start.24
  (1 other events, 0.7 us)

commit v4 on v3

--- a/solution.py
+++ b/solution.py
@@ -305,7 +305,7 @@
 
     q_far, q_side = shift(queries, 4), over_y(queries)
     own_pair = (own, over_c(own))
-    sent, q_far = lax.optimization_barrier((own, q_far))
+    sent, q_far, q_side = lax.optimization_barrier((own, q_far, q_side))
     kv_up, kv_down = shift(sent, -1), shift(sent, 1)
     q_cross = over_y(q_far)
     sent, q_cross = lax.optimization_barrier((own, q_cross))
@@ -319,21 +319,19 @@
         ids += [row(n, yc), row(n, yc ^ 1)]
     ids, span = jnp.stack(ids), span_rank.reshape(Z * YC, TOK)
 
+    ids, span, own = lax.optimization_barrier((ids, span, own))
+    own_pair = (own, own_pair[1])
     state = attention(q_blocks, own_pair)
     kv_up, kv_down, *state = lax.optimization_barrier((kv_up, kv_down, *state))
     next_pairs = (kv_up, over_c(kv_up), kv_down, over_c(kv_down))
     weight = lax.optimization_barrier((out_weight, kv_up, kv_down))[0]
-    weight_y, weight_c = over_y(weight), over_c(weight)
+    weight_y = over_y(weight)
+    weights = [out_weight, over_c(weight), weight_y, over_c(weight_y)]
     state = attention(q_blocks, next_pairs, state)
-    kv_two, weight_y, weight_c, *state = lax.optimization_barrier(
-        (kv_two, weight_y, weight_c, *state)
-    )
+    kv_two, *state = lax.optimization_barrier((kv_two, *state))
     last_pair = (kv_two, over_c(kv_two))
-    weight_yc = over_c(weight_y)
     new = (*own_pair, *next_pairs, *last_pair)
-    parts = attention(q_blocks, last_pair, state, new, ids, span)
-    weight_yc, cross, far, side, mine = lax.optimization_barrier((weight_yc, *parts))
-    weights = [out_weight, weight_c, weight_y, weight_yc]
+    cross, far, side, mine = attention(q_blocks, last_pair, state, new, ids, span)
     cross = seq_permute(cross, lambda z, y, c: (z + 4, 1 - y, c))
     attended = merge((cross, shift(far, 4), over_y(side), mine))
 

time: 152 us -> 147 us (0.967)
  waiting for transfers between devices: 24.3 us -> 22 us
  blocking collectives: 32 us -> 30.4 us
    ppermute x23, waiting for transfers between devices: 24.3 us -> 22 us  [seq_permute(): return lax.ppermute(value, 'seq', pairs)]
    all_to_all x1, blocking collectives: 13.3 us -> 11.5 us  [body(): lax.all_to_all(projected, 'seq', 0, 0, axis_index_groups=PLANES, tiled=True)]
  transfers between devices with their start and end apart: 23 -> 23, of which waited for: 8 -> 10; matrix products, arithmetic and copies ran while one was open for 1% -> 1% of each run, Pallas kernels for 25% -> 27%
where the time goes in v4:
time: 147 us; the launch traced here: 146 us
  Pallas kernels  44.3 us (30%)
  starting transfers between devices  39.4 us (27%)
  blocking collectives  30.4 us (21%)
  waiting for transfers between devices  22 us (15%)
  local copies, waits for them, and re-layouts  7.83 us (5%)
    ppermute x23, starting transfers between devices, seq_permute(): return lax.ppermute(value, 'seq', pairs)  39.4 us
    pallas_call x3, Pallas kernels, attention(): pl.pallas_call(functools.partial(attention_kernel, len(shards), first, la...  35.9 us
    ppermute x23, waiting for transfers between devices, seq_permute(): return lax.ppermute(value, 'seq', pairs)  22 us
    all_to_all x1, blocking collectives, body(): shares = lax.all_to_all(shares, 'head', 0, 0, tiled=True)  18.9 us
    all_to_all x1, blocking collectives, body(): lax.all_to_all(projected, 'seq', 0, 0, axis_index_groups=PLANES, tiled=True)  11.5 us
    unnamed x53, local copies, waits for them, and re-layouts  6.53 us
    pallas_call x1, Pallas kernels, product(): pl.pallas_call(product_kernel, out_shape=jax.ShapeDtypeStruct((Z, YC, TOK...  4.27 us
  transfers between devices with their start and end apart: 23, of which 10 were waited for; matrix products, arithmetic and copies ran while one was open for 1% of the time, Pallas kernels for 27%

profile of v4, /device:TPU:1, one launch (start us, length us, event | category | flops | bytes accessed | tf_op | source)
XLA Modules:
  0.0 145.7 jit_solution(11412010163529532780)
XLA Ops:
  0.0 7.7 %collective-permute-start = (bf16[64,1024]{1,0:T(8,128)(2,1)}, bf16[64,1024]{1,0:T(8,128)(2,1)S(1)}, u32[]{:S(2)}, u32[]{:S(2)}) collective-permute-start(bf16[64,1024]{1,0:T(8,128)(2,1)} %refs_3_.5), channel_id=1, source_target_pairs={{0,128},{8,136},{16,144},{24,152},{32,160},{40,168},{48,176},{56,1... | collective-permute-start | bytes 393224 | tf_op jit(solution)/shard_map/ppermute | solution.py:39
  7.7 1.3 collective-permute-start.1
  9.7 1.9 %pack.1.refs_4_.refs_8_ = bf16[2192,128]{1,0:T(8,128)(2,1)} custom-call(s32[1]{0:T(128)S(6)} %copy.10.length_ref, bf16[1,1024,128]{2,1,0:T(8,128)(2,1)} %k_ref.1, bf16[1,1024,128]{2,1,0:T(8,128)(2,1)} %v_ref.1, bf16[64,128]{1,0:T(8,128)(2,1)} %nk_ref.1, bf16[64,128]{1,0:T(8,128)(2,1)} %nv_ref.1), custom_call_target="tpu_custom_call" | custom-call | tf_op jit(solution)/shard_map/pack/pallas_call | solution.py:55
  11.6 1.2 collective-permute-start.6
  12.8 4.1 %collective-permute-start.4 = (bf16[2192,128]{1,0:T(8,128)(2,1)}, bf16[2192,128]{1,0:T(8,128)(2,1)S(1)}, u32[]{:S(2)}, u32[]{:S(2)}) collective-permute-start(bf16[2192,128]{1,0:T(8,128)(2,1)} %pack.1.refs_4_.refs_8_), channel_id=1, source_target_pairs={{0,224},{8,232},{16,240},{24,248},{32,0},{40,8},{48,16},{56,24},{6... | collective-permute-start | bytes 1683464 | tf_op jit(solution)/shard_map/ppermute | solution.py:39
  16.9 1.3 collective-permute-start.2
  18.2 0.7 reshape.7.refs_17_
  18.9 0.6 stack.60.refs_16_
  19.5 1.5 %collective-permute-done.2.refs_0_ = bf16[64,1024]{1,0:T(8,128)(2,1)S(1)} collective-permute-done((bf16[64,1024]{1,0:T(8,128)(2,1)S(1)}, bf16[64,1024]{1,0:T(8,128)(2,1)S(1)}, u32[]{:S(2)}, u32[]{:S(2)}) %collective-permute-start.2) | collective-permute-done | bytes 131104 | tf_op jit(solution)/shard_map/ppermute | solution.py:39
  21.1 0.6 copy-done.10
  21.7 0.8 copy-done.1
  22.5 8.8 %attention.3 = (f32[1,2048]{1,0:T(1,128)}, f32[144,2048]{1,0:T(8,128)}) custom-call(bf16[64,1024]{1,0:T(8,128)(2,1)} %copy-done.10, bf16[64,1024]{1,0:T(8,128)(2,1)} %copy-done.8, bf16[64,1024]{1,0:T(8,128)(2,1)} %copy-done.9, bf16[64,1024]{1,0:T(8,128)(2,1)} %refs_3_.5, bf16[2192,128]{1,0:T(8,128)(2,1)} %pack.1.refs_4_.refs_8_, bf16[2192,128]{1,0:T(8,128)(2,1)} %copy-done.1), custom_call_target="tpu_custom_call" | custom-call | flops 1 | bytes 1 | tf_op jit(solution)/shard_map/attention/pallas_call | solution.py:234
  31.3 0.4 collective-permute-done.5.refs_6_.refs_12_
  31.6 1.8 %collective-permute-start.7 = (bf16[2192,128]{1,0:T(8,128)(2,1)S(1)}, bf16[2192,128]{1,0:T(8,128)(2,1)S(1)}, u32[]{:S(2)}, u32[]{:S(2)}) collective-permute-start(bf16[2192,128]{1,0:T(8,128)(2,1)S(1)} %collective-permute-done.4.refs_4_.refs_10_), channel_id=1, source_target_pairs={{0,8},{8,0},{16,24},{24,16},{32,40},{40,32},{48,56},{56,48},{64,72... | collective-permute-start | bytes 1683464 | tf_op jit(solution)/shard_map/ppermute | solution.py:39
  33.6 3.6 %collective-permute-start.3 = (bf16[2192,128]{1,0:T(8,128)(2,1)S(1)}, bf16[2192,128]{1,0:T(8,128)(2,1)S(1)}, u32[]{:S(2)}, u32[]{:S(2)}) collective-permute-start(bf16[2192,128]{1,0:T(8,128)(2,1)S(1)} %copy-done), channel_id=1, source_target_pairs={{0,192},{8,200},{16,208},{24,216},{32,96},{40,104},{48,112},{56,12... | collective-permute-start | bytes 1683464 | tf_op jit(solution)/shard_map/ppermute | solution.py:39
  37.2 0.8 copy-done.4
  38.0 0.8 copy-done.5
  38.8 14.4 %attention.4 = (f32[1,2048]{1,0:T(1,128)}, f32[144,2048]{1,0:T(8,128)}) custom-call(bf16[64,1024]{1,0:T(8,128)(2,1)} %copy-done.10, bf16[64,1024]{1,0:T(8,128)(2,1)} %copy-done.8, bf16[64,1024]{1,0:T(8,128)(2,1)} %copy-done.9, bf16[64,1024]{1,0:T(8,128)(2,1)} %refs_3_.5, bf16[2192,128]{1,0:T(8,128)(2,1)} %copy-done.2, bf16[2192,128]{1,0:T(8,128)(2,1)} %copy-done.4, ...), custom_call_target="tpu_custom_call" | custom-call | flops 1 | bytes 1 | tf_op jit(solution)/shard_map/attention/pallas_call | solution.py:234
  53.2 1.0 collective-permute-start.9
  54.2 1.3 collective-permute-start.21
  55.5 0.3 collective-permute-done.9.refs_5_.refs_15_
  55.8 0.8 copy-done.7
  56.6 12.8 %attention.5 = (bf16[64,1152]{1,0:T(8,128)(2,1)}, bf16[64,1152]{1,0:T(8,128)(2,1)}, bf16[64,1152]{1,0:T(8,128)(2,1)}, bf16[64,1152]{1,0:T(8,128)(2,1)}) custom-call(bf16[64,1024]{1,0:T(8,128)(2,1)} %copy-done.10, bf16[64,1024]{1,0:T(8,128)(2,1)} %copy-done.8, bf16[64,1024]{1,0:T(8,128)(2,1)} %copy-done.9, bf16[64,1024]{1,0:T(8,128)(2,1)} %refs_3_.5, ...), custom_call_target="tpu_custom_call" | custom-call | flops 1 | bytes 1 | tf_op jit(solution)/shard_map/attention/pallas_call | solution.py:234
  69.4 4.7 %collective-permute-start.11 = (bf16[64,1152]{1,0:T(8,128)(2,1)}, bf16[64,1152]{1,0:T(8,128)(2,1)S(1)}, u32[]{:S(2)}, u32[]{:S(2)}) collective-permute-start(bf16[64,1152]{1,0:T(8,128)(2,1)} %get-tuple-element.49), channel_id=1, source_target_pairs={{0,128},{8,136},{16,144},{24,152},{32,160},{40,168},{48,176},{56,1... | collective-permute-start | bytes 442376 | tf_op jit(solution)/shard_map/ppermute | solution.py:39
  74.1 1.8 %collective-permute-start.12 = (bf16[64,1152]{1,0:T(8,128)(2,1)}, bf16[64,1152]{1,0:T(8,128)(2,1)S(1)}, u32[]{:S(2)}, u32[]{:S(2)}) collective-permute-start(bf16[64,1152]{1,0:T(8,128)(2,1)} %get-tuple-element.50), channel_id=1, source_target_pairs={{0,16},{8,24},{16,0},{24,8},{32,48},{40,56},{48,32},{56,40},{64,80... | collective-permute-start | bytes 442376 | tf_op jit(solution)/shard_map/ppermute | solution.py:39
  75.9 1.2 collective-permute-start.20
  77.1 8.1 %collective-permute-done.10.refs_0_ = bf16[64,1152]{1,0:T(8,128)(2,1)S(1)} collective-permute-done((bf16[64,1152]{1,0:T(8,128)(2,1)}, bf16[64,1152]{1,0:T(8,128)(2,1)S(1)}, u32[]{:S(2)}, u32[]{:S(2)}) %collective-permute-start.10) | collective-permute-done | bytes 147488 | tf_op jit(solution)/shard_map/ppermute | solution.py:39
  85.2 2.5 %collective-permute-done.11.refs_1_ = bf16[64,1152]{1,0:T(8,128)(2,1)S(1)} collective-permute-done((bf16[64,1152]{1,0:T(8,128)(2,1)}, bf16[64,1152]{1,0:T(8,128)(2,1)S(1)}, u32[]{:S(2)}, u32[]{:S(2)}) %collective-permute-start.11) | collective-permute-done | bytes 147488 | tf_op jit(solution)/shard_map/ppermute | solution.py:39
  87.8 0.6 copy-done.16
  88.5 2.3 %merge.1.refs_0_ = bf16[64,1024]{1,0:T(8,128)(2,1)} custom-call(bf16[64,1152]{1,0:T(8,128)(2,1)} %copy-done.15, bf16[64,1152]{1,0:T(8,128)(2,1)} %copy-done.16, bf16[64,1152]{1,0:T(8,128)(2,1)} %copy-done.17, bf16[64,1152]{1,0:T(8,128)(2,1)} %get-tuple-element.51.refs_3_), custom_call_target="tpu_custom_call" | custom-call | tf_op jit(solution)/shard_map/merge/pallas_call | solution.py:266
  90.8 1.2 collective-permute-start.22
  92.0 1.3 collective-permute-start.17
  93.3 1.9 %collective-permute-done.13.refs_1_ = bf16[64,1024]{1,0:T(8,128)(2,1)S(1)} collective-permute-done((bf16[64,1024]{1,0:T(8,128)(2,1)}, bf16[64,1024]{1,0:T(8,128)(2,1)S(1)}, u32[]{:S(2)}, u32[]{:S(2)}) %collective-permute-start.13) | collective-permute-done | bytes 131104 | tf_op jit(solution)/shard_map/ppermute | solution.py:39
  95.2 0.8 collective-permute-start.14
  96.0 2.5 %collective-permute-done.17.refs_7_ = bf16[64,1024]{1,0:T(8,128)(2,1)S(1)} collective-permute-done((bf16[64,1024]{1,0:T(8,128)(2,1)}, bf16[64,1024]{1,0:T(8,128)(2,1)S(1)}, u32[]{:S(2)}, u32[]{:S(2)}) %collective-permute-start.17) | collective-permute-done | bytes 131104 | tf_op jit(solution)/shard_map/ppermute | solution.py:39
  98.6 0.5 collective-permute-done.14.refs_2_
  99.1 2.1 %collective-permute-start.15 = (bf16[64,1024]{1,0:T(8,128)(2,1)S(1)}, bf16[64,1024]{1,0:T(8,128)(2,1)S(1)}, u32[]{:S(2)}, u32[]{:S(2)}) collective-permute-start(bf16[64,1024]{1,0:T(8,128)(2,1)S(1)} %collective-permute-done.14.refs_2_), channel_id=1, source_target_pairs={{0,224},{8,232},{16,240},{24,248},{32,0},{40,8},{48,16},{56,24},{6... | collective-permute-start | bytes 393224 | tf_op jit(solution)/shard_map/ppermute | solution.py:39
  101.2 2.7 %collective-permute-done.18.refs_6_ = bf16[64,1024]{1,0:T(8,128)(2,1)S(1)} collective-permute-done((bf16[64,1024]{1,0:T(8,128)(2,1)S(1)}, bf16[64,1024]{1,0:T(8,128)(2,1)S(1)}, u32[]{:S(2)}, u32[]{:S(2)}) %collective-permute-start.18) | collective-permute-done | bytes 131104 | tf_op jit(solution)/shard_map/ppermute | solution.py:39
  103.9 2.7 %collective-permute-start.16 = (bf16[64,1024]{1,0:T(8,128)(2,1)S(1)}, bf16[64,1024]{1,0:T(8,128)(2,1)S(1)}, u32[]{:S(2)}, u32[]{:S(2)}) collective-permute-start(bf16[64,1024]{1,0:T(8,128)(2,1)S(1)} %collective-permute-done.15.refs_3_), channel_id=1, source_target_pairs={{0,224},{8,232},{16,240},{24,248},{32,0},{40,8},{48,16},{56,24},{6... | collective-permute-start | bytes 393224 | tf_op jit(solution)/shard_map/ppermute | solution.py:39
  106.5 0.6 pad_add_fusion.place_ref
  107.2 1.7 %collective-permute-done.19.refs_5_ = bf16[64,1024]{1,0:T(8,128)(2,1)S(1)} collective-permute-done((bf16[64,1024]{1,0:T(8,128)(2,1)S(1)}, bf16[64,1024]{1,0:T(8,128)(2,1)S(1)}, u32[]{:S(2)}, u32[]{:S(2)}) %collective-permute-start.19) | collective-permute-done | bytes 131104 | tf_op jit(solution)/shard_map/ppermute | solution.py:39
  109.0 0.6 copy-done.23
  109.5 0.6 copy-done.24
  110.2 4.3 %product.1 = bf16[8,4,64,256]{3,2,1,0:T(8,128)(2,1)} custom-call(s32[2]{0:T(128)} %pad_add_fusion.place_ref, bf16[64,1024]{1,0:T(8,128)(2,1)} %merge.1.refs_0_, bf16[64,1024]{1,0:T(8,128)(2,1)} %copy-done.18, bf16[64,1024]{1,0:T(8,128)(2,1)} %copy-done.20, bf16[64,1024]{1,0:T(8,128)(2,1)} %copy-done.22, bf16[64,1024]{1,0:T(8,128)(2,1)} %copy-done.24, ...), custom_call_target="tpu_custom_call" | custom-call | tf_op jit(solution)/shard_map/product/pallas_call | solution.py:286
  114.4 18.9 %all_to_all.14 = bf16[8,4,64,256]{3,2,1,0:T(8,128)(2,1)S(1)} all-to-all(bf16[8,4,64,256]{3,2,1,0:T(8,128)(2,1)} %product.1), channel_id=1, replica_groups=mesh['seq'=32,'head'=8] {'head'}, dimensions={0} | all-to-all | bytes 2097152 | tf_op jit(solution)/shard_map/all_to_all | solution.py:345
  133.3 0.1 reduce_sum.12
  133.5 11.5 %all_to_all.15 = bf16[4,64,256]{2,1,0:T(8,128)(2,1)S(1)} all-to-all(bf16[4,64,256]{2,1,0:T(8,128)(2,1)S(1)} %reduce_sum.12), channel_id=1, replica_groups={{0,8,16,24},{32,40,48,56},{64,72,80,88},{96,104,112,120},{128,136,144,1..., dimensions={0} | all-to-all | bytes 262144 | tf_op jit(solution)/shard_map/all_to_all | solution.py:347
  145.0 0.7 copy.11
  (63 shorter events, 0.4 us)
Async XLA Ops:
  0.0 18.2 %copy-start.25 = (s32[2048]{0:T(1024)S(1)}, s32[2048]{0:T(1024)}, u32[]{:S(2)}) copy-start(s32[2048]{0:T(1024)} %param.14) | copy-start | bytes 24580
  0.0 12.8 %collective-permute-start = (bf16[64,1024]{1,0:T(8,128)(2,1)}, bf16[64,1024]{1,0:T(8,128)(2,1)S(1)}, u32[]{:S(2)}, u32[]{:S(2)}) collective-permute-start(bf16[64,1024]{1,0:T(8,128)(2,1)} %refs_3_.5), channel_id=1, source_target_pairs={{0,128},{8,136},{16,144},{24,152},{32,160},{40,168},{48,176},{56,1... | collective-permute-start | bytes 393224 | tf_op jit(solution)/shard_map/ppermute | solution.py:39
  7.7 5.1 %collective-permute-start.1 = (bf16[64,1024]{1,0:T(8,128)(2,1)}, bf16[64,1024]{1,0:T(8,128)(2,1)S(1)}, u32[]{:S(2)}, u32[]{:S(2)}) collective-permute-start(bf16[64,1024]{1,0:T(8,128)(2,1)} %refs_3_.5), channel_id=1, source_target_pairs={{0,16},{8,24},{16,0},{24,8},{32,48},{40,56},{48,32},{56,40},{64,80... | collective-permute-start | bytes 393224 | tf_op jit(solution)/shard_map/ppermute | solution.py:39
  11.6 22.0 %copy-start = (bf16[2192,128]{1,0:T(8,128)(2,1)S(1)}, bf16[2192,128]{1,0:T(8,128)(2,1)}, u32[]{:S(2)}) copy-start(bf16[2192,128]{1,0:T(8,128)(2,1)} %pack.1.refs_4_.refs_8_) | copy-start | bytes 1683460
  11.6 9.5 %collective-permute-start.6 = (bf16[2192,128]{1,0:T(8,128)(2,1)}, bf16[2192,128]{1,0:T(8,128)(2,1)S(1)}, u32[]{:S(2)}, u32[]{:S(2)}) collective-permute-start(bf16[2192,128]{1,0:T(8,128)(2,1)} %pack.1.refs_4_.refs_8_), channel_id=1, source_target_pairs={{0,8},{8,0},{16,24},{24,16},{32,40},{40,32},{48,56},{56,48},{64,72... | collective-permute-start | bytes 1683464 | tf_op jit(solution)/shard_map/ppermute | solution.py:39
  12.8 8.3 %copy-start.8 = (bf16[64,1024]{1,0:T(8,128)(2,1)}, bf16[64,1024]{1,0:T(8,128)(2,1)S(1)}, u32[]{:S(2)}) copy-start(bf16[64,1024]{1,0:T(8,128)(2,1)S(1)} %collective-permute-done.refs_1_) | copy-start | bytes 393220
  12.8 8.3 %copy-start.9 = (bf16[64,1024]{1,0:T(8,128)(2,1)}, bf16[64,1024]{1,0:T(8,128)(2,1)S(1)}, u32[]{:S(2)}) copy-start(bf16[64,1024]{1,0:T(8,128)(2,1)S(1)} %collective-permute-done.1.refs_2_) | copy-start | bytes 393220
  12.8 18.5 %collective-permute-start.4 = (bf16[2192,128]{1,0:T(8,128)(2,1)}, bf16[2192,128]{1,0:T(8,128)(2,1)S(1)}, u32[]{:S(2)}, u32[]{:S(2)}) collective-permute-start(bf16[2192,128]{1,0:T(8,128)(2,1)} %pack.1.refs_4_.refs_8_), channel_id=1, source_target_pairs={{0,224},{8,232},{16,240},{24,248},{32,0},{40,8},{48,16},{56,24},{6... | collective-permute-start | bytes 1683464 | tf_op jit(solution)/shard_map/ppermute | solution.py:39
  16.9 14.7 %collective-permute-start.5 = (bf16[2192,128]{1,0:T(8,128)(2,1)}, bf16[2192,128]{1,0:T(8,128)(2,1)S(1)}, u32[]{:S(2)}, u32[]{:S(2)}) collective-permute-start(bf16[2192,128]{1,0:T(8,128)(2,1)} %pack.1.refs_4_.refs_8_), channel_id=1, source_target_pairs={{0,32},{8,40},{16,48},{24,56},{32,64},{40,72},{48,80},{56,88},{64,... | collective-permute-start | bytes 1683464 | tf_op jit(solution)/shard_map/ppermute | solution.py:39
  16.9 4.1 %collective-permute-start.2 = (bf16[64,1024]{1,0:T(8,128)(2,1)S(1)}, bf16[64,1024]{1,0:T(8,128)(2,1)S(1)}, u32[]{:S(2)}, u32[]{:S(2)}) collective-permute-start(bf16[64,1024]{1,0:T(8,128)(2,1)S(1)} %collective-permute-done.refs_1_), channel_id=1, source_target_pairs={{0,16},{8,24},{16,0},{24,8},{32,48},{40,56},{48,32},{56,40},{64,80... | collective-permute-start | bytes 393224 | tf_op jit(solution)/shard_map/ppermute | solution.py:39
  21.1 0.7 copy-start.10
  21.7 0.8 copy-start.1
  31.3 5.9 %copy-start.2 = (bf16[2192,128]{1,0:T(8,128)(2,1)}, bf16[2192,128]{1,0:T(8,128)(2,1)S(1)}, u32[]{:S(2)}) copy-start(bf16[2192,128]{1,0:T(8,128)(2,1)S(1)} %collective-permute-done.4.refs_4_.refs_10_) | copy-start | bytes 1683460
  31.6 5.5 %copy-start.3 = (bf16[2192,128]{1,0:T(8,128)(2,1)}, bf16[2192,128]{1,0:T(8,128)(2,1)S(1)}, u32[]{:S(2)}) copy-start(bf16[2192,128]{1,0:T(8,128)(2,1)S(1)} %collective-permute-done.5.refs_6_.refs_12_) | copy-start | bytes 1683460
  31.6 22.5 %copy-start.11 = (bf16[1024,256]{1,0:T(8,128)(2,1)S(1)}, bf16[1024,256]{1,0:T(8,128)(2,1)}, u32[]{:S(2)}) copy-start(bf16[1024,256]{1,0:T(8,128)(2,1)} %refs_8_.1) | copy-start | bytes 1572868
  31.6 5.5 %collective-permute-start.7 = (bf16[2192,128]{1,0:T(8,128)(2,1)S(1)}, bf16[2192,128]{1,0:T(8,128)(2,1)S(1)}, u32[]{:S(2)}, u32[]{:S(2)}) collective-permute-start(bf16[2192,128]{1,0:T(8,128)(2,1)S(1)} %collective-permute-done.4.refs_4_.refs_10_), channel_id=1, source_target_pairs={{0,8},{8,0},{16,24},{24,16},{32,40},{40,32},{48,56},{56,48},{64,72... | collective-permute-start | bytes 1683464 | tf_op jit(solution)/shard_map/ppermute | solution.py:39
  33.5 3.6 %collective-permute-start.8 = (bf16[2192,128]{1,0:T(8,128)(2,1)S(1)}, bf16[2192,128]{1,0:T(8,128)(2,1)S(1)}, u32[]{:S(2)}, u32[]{:S(2)}) collective-permute-start(bf16[2192,128]{1,0:T(8,128)(2,1)S(1)} %collective-permute-done.5.refs_6_.refs_12_), channel_id=1, source_target_pairs={{0,8},{8,0},{16,24},{24,16},{32,40},{40,32},{48,56},{56,48},{64,72... | collective-permute-start | bytes 1683464 | tf_op jit(solution)/shard_map/ppermute | solution.py:39
  33.6 19.6 %collective-permute-start.3 = (bf16[2192,128]{1,0:T(8,128)(2,1)S(1)}, bf16[2192,128]{1,0:T(8,128)(2,1)S(1)}, u32[]{:S(2)}, u32[]{:S(2)}) collective-permute-start(bf16[2192,128]{1,0:T(8,128)(2,1)S(1)} %copy-done), channel_id=1, source_target_pairs={{0,192},{8,200},{16,208},{24,216},{32,96},{40,104},{48,112},{56,12... | collective-permute-start | bytes 1683464 | tf_op jit(solution)/shard_map/ppermute | solution.py:39
  37.1 0.8 copy-start.4
  37.9 0.8 copy-start.5
  53.2 2.6 %copy-start.6 = (bf16[2192,128]{1,0:T(8,128)(2,1)}, bf16[2192,128]{1,0:T(8,128)(2,1)S(1)}, u32[]{:S(2)}) copy-start(bf16[2192,128]{1,0:T(8,128)(2,1)S(1)} %collective-permute-done.3.refs_4_.refs_14_) | copy-start | bytes 1683460
  53.2 2.5 %collective-permute-start.9 = (bf16[2192,128]{1,0:T(8,128)(2,1)S(1)}, bf16[2192,128]{1,0:T(8,128)(2,1)S(1)}, u32[]{:S(2)}, u32[]{:S(2)}) collective-permute-start(bf16[2192,128]{1,0:T(8,128)(2,1)S(1)} %collective-permute-done.3.refs_4_.refs_14_), channel_id=1, source_target_pairs={{0,8},{8,0},{16,24},{24,16},{32,40},{40,32},{48,56},{56,48},{64,72... | collective-permute-start | bytes 1683464 | tf_op jit(solution)/shard_map/ppermute | solution.py:39
  54.2 36.6 %collective-permute-start.21 = (bf16[1024,256]{1,0:T(8,128)(2,1)S(1)}, bf16[1024,256]{1,0:T(8,128)(2,1)S(1)}, u32[]{:S(2)}, u32[]{:S(2)}) collective-permute-start(bf16[1024,256]{1,0:T(8,128)(2,1)S(1)} %copy-done.11), channel_id=1, source_target_pairs={{0,16},{8,24},{16,0},{24,8},{32,48},{40,56},{48,32},{56,40},{64,80... | collective-permute-start | bytes 1572872 | tf_op jit(solution)/shard_map/ppermute | solution.py:39
  55.8 0.8 copy-start.7
  69.3 15.9 %collective-permute-start.10 = (bf16[64,1152]{1,0:T(8,128)(2,1)}, bf16[64,1152]{1,0:T(8,128)(2,1)S(1)}, u32[]{:S(2)}, u32[]{:S(2)}) collective-permute-start(bf16[64,1152]{1,0:T(8,128)(2,1)} %get-tuple-element.48), channel_id=1, source_target_pairs={{0,144},{8,152},{16,128},{24,136},{32,176},{40,184},{48,160},{56,1... | collective-permute-start | bytes 442376 | tf_op jit(solution)/shard_map/ppermute | solution.py:39
  69.4 18.4 %collective-permute-start.11 = (bf16[64,1152]{1,0:T(8,128)(2,1)}, bf16[64,1152]{1,0:T(8,128)(2,1)S(1)}, u32[]{:S(2)}, u32[]{:S(2)}) collective-permute-start(bf16[64,1152]{1,0:T(8,128)(2,1)} %get-tuple-element.49), channel_id=1, source_target_pairs={{0,128},{8,136},{16,144},{24,152},{32,160},{40,168},{48,176},{56,1... | collective-permute-start | bytes 442376 | tf_op jit(solution)/shard_map/ppermute | solution.py:39
  74.1 13.7 %collective-permute-start.12 = (bf16[64,1152]{1,0:T(8,128)(2,1)}, bf16[64,1152]{1,0:T(8,128)(2,1)S(1)}, u32[]{:S(2)}, u32[]{:S(2)}) collective-permute-start(bf16[64,1152]{1,0:T(8,128)(2,1)} %get-tuple-element.50), channel_id=1, source_target_pairs={{0,16},{8,24},{16,0},{24,8},{32,48},{40,56},{48,32},{56,40},{64,80... | collective-permute-start | bytes 442376 | tf_op jit(solution)/shard_map/ppermute | solution.py:39
  75.9 31.3 %collective-permute-start.20 = (bf16[1024,256]{1,0:T(8,128)(2,1)S(1)}, bf16[1024,256]{1,0:T(8,128)(2,1)S(1)}, u32[]{:S(2)}, u32[]{:S(2)}) collective-permute-start(bf16[1024,256]{1,0:T(8,128)(2,1)S(1)} %copy-done.11), channel_id=1, source_target_pairs={{0,8},{8,0},{16,24},{24,16},{32,40},{40,32},{48,56},{56,48},{64,72... | collective-permute-start | bytes 1572872 | tf_op jit(solution)/shard_map/ppermute | solution.py:39
  85.2 2.6 %copy-start.15 = (bf16[64,1152]{1,0:T(8,128)(2,1)}, bf16[64,1152]{1,0:T(8,128)(2,1)S(1)}, u32[]{:S(2)}) copy-start(bf16[64,1152]{1,0:T(8,128)(2,1)S(1)} %collective-permute-done.10.refs_0_) | copy-start | bytes 442372
  87.8 0.7 copy-start.16
  87.8 0.7 copy-start.17
  90.8 4.5 %collective-permute-start.13 = (bf16[64,1024]{1,0:T(8,128)(2,1)}, bf16[64,1024]{1,0:T(8,128)(2,1)S(1)}, u32[]{:S(2)}, u32[]{:S(2)}) collective-permute-start(bf16[64,1024]{1,0:T(8,128)(2,1)} %merge.1.refs_0_), channel_id=1, source_target_pairs={{0,224},{8,232},{16,240},{24,248},{32,0},{40,8},{48,16},{56,24},{6... | collective-permute-start | bytes 393224 | tf_op jit(solution)/shard_map/ppermute | solution.py:39
  90.8 18.1 %copy-start.12 = (bf16[1024,256]{1,0:T(8,128)(2,1)}, bf16[1024,256]{1,0:T(8,128)(2,1)S(1)}, u32[]{:S(2)}) copy-start(bf16[1024,256]{1,0:T(8,128)(2,1)S(1)} %collective-permute-done.21.refs_10_) | copy-start | bytes 1572868
  90.8 16.4 %collective-permute-start.22 = (bf16[1024,256]{1,0:T(8,128)(2,1)S(1)}, bf16[1024,256]{1,0:T(8,128)(2,1)S(1)}, u32[]{:S(2)}, u32[]{:S(2)}) collective-permute-start(bf16[1024,256]{1,0:T(8,128)(2,1)S(1)} %collective-permute-done.21.refs_10_), channel_id=1, source_target_pairs={{0,8},{8,0},{16,24},{24,16},{32,40},{40,32},{48,56},{56,48},{64,72... | collective-permute-start | bytes 1572872 | tf_op jit(solution)/shard_map/ppermute | solution.py:39
  92.0 6.5 %collective-permute-start.17 = (bf16[64,1024]{1,0:T(8,128)(2,1)}, bf16[64,1024]{1,0:T(8,128)(2,1)S(1)}, u32[]{:S(2)}, u32[]{:S(2)}) collective-permute-start(bf16[64,1024]{1,0:T(8,128)(2,1)} %merge.1.refs_0_), channel_id=1, source_target_pairs={{0,32},{8,40},{16,48},{24,56},{32,64},{40,72},{48,80},{56,88},{64,... | collective-permute-start | bytes 393224 | tf_op jit(solution)/shard_map/ppermute | solution.py:39
  95.2 13.7 %copy-start.18 = (bf16[64,1024]{1,0:T(8,128)(2,1)}, bf16[64,1024]{1,0:T(8,128)(2,1)S(1)}, u32[]{:S(2)}) copy-start(bf16[64,1024]{1,0:T(8,128)(2,1)S(1)} %collective-permute-done.13.refs_1_) | copy-start | bytes 393220
  95.2 3.8 %collective-permute-start.14 = (bf16[64,1024]{1,0:T(8,128)(2,1)S(1)}, bf16[64,1024]{1,0:T(8,128)(2,1)S(1)}, u32[]{:S(2)}, u32[]{:S(2)}) collective-permute-start(bf16[64,1024]{1,0:T(8,128)(2,1)S(1)} %collective-permute-done.13.refs_1_), channel_id=1, source_target_pairs={{0,224},{8,232},{16,240},{24,248},{32,0},{40,8},{48,16},{56,24},{6... | collective-permute-start | bytes 393224 | tf_op jit(solution)/shard_map/ppermute | solution.py:39
  98.5 10.4 %copy-start.19 = (bf16[64,1024]{1,0:T(8,128)(2,1)}, bf16[64,1024]{1,0:T(8,128)(2,1)S(1)}, u32[]{:S(2)}) copy-start(bf16[64,1024]{1,0:T(8,128)(2,1)S(1)} %collective-permute-done.17.refs_7_) | copy-start | bytes 393220
  98.5 5.4 %collective-permute-start.18 = (bf16[64,1024]{1,0:T(8,128)(2,1)S(1)}, bf16[64,1024]{1,0:T(8,128)(2,1)S(1)}, u32[]{:S(2)}, u32[]{:S(2)}) collective-permute-start(bf16[64,1024]{1,0:T(8,128)(2,1)S(1)} %collective-permute-done.17.refs_7_), channel_id=1, source_target_pairs={{0,32},{8,40},{16,48},{24,56},{32,64},{40,72},{48,80},{56,88},{64,... | collective-permute-start | bytes 393224 | tf_op jit(solution)/shard_map/ppermute | solution.py:39
  99.0 9.9 %copy-start.20 = (bf16[64,1024]{1,0:T(8,128)(2,1)}, bf16[64,1024]{1,0:T(8,128)(2,1)S(1)}, u32[]{:S(2)}) copy-start(bf16[64,1024]{1,0:T(8,128)(2,1)S(1)} %collective-permute-done.14.refs_2_) | copy-start | bytes 393220
  99.1 4.8 %collective-permute-start.15 = (bf16[64,1024]{1,0:T(8,128)(2,1)S(1)}, bf16[64,1024]{1,0:T(8,128)(2,1)S(1)}, u32[]{:S(2)}, u32[]{:S(2)}) collective-permute-start(bf16[64,1024]{1,0:T(8,128)(2,1)S(1)} %collective-permute-done.14.refs_2_), channel_id=1, source_target_pairs={{0,224},{8,232},{16,240},{24,248},{32,0},{40,8},{48,16},{56,24},{6... | collective-permute-start | bytes 393224 | tf_op jit(solution)/shard_map/ppermute | solution.py:39
  103.8 5.1 %copy-start.21 = (bf16[64,1024]{1,0:T(8,128)(2,1)}, bf16[64,1024]{1,0:T(8,128)(2,1)S(1)}, u32[]{:S(2)}) copy-start(bf16[64,1024]{1,0:T(8,128)(2,1)S(1)} %collective-permute-done.18.refs_6_) | copy-start | bytes 393220
  103.8 5.0 %collective-permute-start.19 = (bf16[64,1024]{1,0:T(8,128)(2,1)S(1)}, bf16[64,1024]{1,0:T(8,128)(2,1)S(1)}, u32[]{:S(2)}, u32[]{:S(2)}) collective-permute-start(bf16[64,1024]{1,0:T(8,128)(2,1)S(1)} %collective-permute-done.18.refs_6_), channel_id=1, source_target_pairs={{0,32},{8,40},{16,48},{24,56},{32,64},{40,72},{48,80},{56,88},{64,... | collective-permute-start | bytes 393224 | tf_op jit(solution)/shard_map/ppermute | solution.py:39
  103.9 5.1 %copy-start.22 = (bf16[64,1024]{1,0:T(8,128)(2,1)}, bf16[64,1024]{1,0:T(8,128)(2,1)S(1)}, u32[]{:S(2)}) copy-start(bf16[64,1024]{1,0:T(8,128)(2,1)S(1)} %collective-permute-done.15.refs_3_) | copy-start | bytes 393220
  103.9 5.0 %collective-permute-start.16 = (bf16[64,1024]{1,0:T(8,128)(2,1)S(1)}, bf16[64,1024]{1,0:T(8,128)(2,1)S(1)}, u32[]{:S(2)}, u32[]{:S(2)}) collective-permute-start(bf16[64,1024]{1,0:T(8,128)(2,1)S(1)} %collective-permute-done.15.refs_3_), channel_id=1, source_target_pairs={{0,224},{8,232},{16,240},{24,248},{32,0},{40,8},{48,16},{56,24},{6... | collective-permute-start | bytes 393224 | tf_op jit(solution)/shard_map/ppermute | solution.py:39
  107.2 1.8 %copy-start.13 = (bf16[1024,256]{1,0:T(8,128)(2,1)}, bf16[1024,256]{1,0:T(8,128)(2,1)S(1)}, u32[]{:S(2)}) copy-start(bf16[1024,256]{1,0:T(8,128)(2,1)S(1)} %collective-permute-done.20.refs_9_) | copy-start | bytes 1572868
  107.2 1.8 %copy-start.14 = (bf16[1024,256]{1,0:T(8,128)(2,1)}, bf16[1024,256]{1,0:T(8,128)(2,1)S(1)}, u32[]{:S(2)}) copy-start(bf16[1024,256]{1,0:T(8,128)(2,1)S(1)} %collective-permute-done.22.refs_11_) | copy-start | bytes 1572868
  109.5 0.6 copy-start.24
  (1 other events, 0.6 us)

commit v5 on v4

--- a/solution.py
+++ b/solution.py
@@ -26,7 +26,7 @@
 VALUE_AT = KEY_AT + CACHE
 META_AT = VALUE_AT + CACHE
 BLOCK_ROWS = META_AT + 16
-PLANES = [[z * YC + i for i in range(YC)] for z in range(Z)]
+PLANES = [[z * YC * 8 + i for i in range(YC * 8)] for z in range(Z)]
 
 
 def seq_permute(value, move):
@@ -278,14 +278,14 @@
     rows = every[...].reshape(Z * TOK, QPH * HD)
     for r in range(YC):
         part = jnp.dot(rows, weights[r][...], preferred_element_type=F32)
-        out_ref[:, yc ^ r] = part.astype(BF16).reshape(Z, TOK, 256)
+        out_ref[yc ^ r] = part.astype(BF16).reshape(Z, TOK, 256)
 
 
 def product(place, blocks, weights):
     whole = pl.BlockSpec(memory_space=pltpu.VMEM)
     return pl.pallas_call(
         product_kernel,
-        out_shape=jax.ShapeDtypeStruct((Z, YC, TOK, 256), BF16),
+        out_shape=jax.ShapeDtypeStruct((YC, Z, TOK, 256), BF16),
         in_specs=[pl.BlockSpec(memory_space=pltpu.SMEM)] + [whole] * 12,
         out_specs=whole,
         scratch_shapes=[pltpu.VMEM((Z, TOK, QPH * HD), BF16)],
@@ -335,16 +335,17 @@
     cross = seq_permute(cross, lambda z, y, c: (z + 4, 1 - y, c))
     attended = merge((cross, shift(far, 4), over_y(side), mine))
 
-    blocks = [None] * Z
-    blocks[0] = attended
-    for k in (1, 2, 3):
-        blocks[k] = shift(blocks[k - 1], -1)
-        blocks[Z - k] = shift(blocks[(Z - k + 1) % Z], 1)
-    blocks[4] = shift(blocks[3], -1)
-    shares = product(jnp.stack([z, yc]), blocks, weights)
-    shares = lax.all_to_all(shares, "head", 0, 0, tiled=True)
-    projected = jnp.sum(shares.astype(F32), axis=0).astype(BF16).reshape(YC * TOK, 256)
-    return lax.all_to_all(projected, "seq", 0, 0, axis_index_groups=PLANES, tiled=True)
+    blocks = [attended] + [None] * (Z - 1)
+    blocks[1], blocks[7] = shift(attended, -1), shift(attended, 1)
+    blocks[2], blocks[6] = shift(attended, -2), shift(attended, 2)
+    blocks[3], blocks[5] = shift(blocks[1], -2), shift(blocks[7], 2)
+    blocks[4] = shift(blocks[6], 2)
+    shares = product(jnp.stack([z, yc]), blocks, weights).reshape(YC * Z, TOK, 256)
+    shares = lax.all_to_all(
+        shares, ("seq", "head"), 0, 0, axis_index_groups=PLANES, tiled=True
+    )
+    shares = shares.reshape(YC, Z, TOK, 256).astype(F32)
+    return jnp.sum(shares, axis=1).astype(BF16).reshape(YC * TOK, 256)
 
 
 def solution(mesh):

time: 147 us -> 149 us (1.014)
  waiting for transfers between devices: 22 us -> 28.8 us
  Pallas kernels: 44.3 us -> 39.7 us
  starting transfers between devices: 39.4 us -> 43.8 us
  blocking collectives: 30.4 us -> 26.9 us
    ppermute x23, waiting for transfers between devices: 22 us -> 28.8 us  [seq_permute(): return lax.ppermute(value, 'seq', pairs)]
    pallas_call x3, Pallas kernels: 35.9 us -> 31.2 us  [attention(): pl.pallas_call(functools.partial(attention_kernel, len(shards), first, la...]
    ppermute x23, starting transfers between devices: 39.4 us -> 43.8 us  [seq_permute(): return lax.ppermute(value, 'seq', pairs)]
    all_to_all x2 -> x1, blocking collectives: 30.4 us -> 26.9 us  [body(): lax.all_to_all(shares, ('seq', 'head'), 0, 0, axis_index_groups=PLANES, t...]
    unnamed x53 -> x50, local copies, waits for them, and re-layouts: 6.53 us -> 5.27 us
  transfers between devices with their start and end apart: 23 -> 23, of which waited for: 10 -> 8; matrix products, arithmetic and copies ran while one was open for 1% -> 1% of each run, Pallas kernels for 27% -> 24%
where the time goes in v5:
time: 149 us; the launch traced here: 148 us
  starting transfers between devices  43.8 us (29%)
  Pallas kernels  39.7 us (27%)
  waiting for transfers between devices  28.8 us (19%)
  blocking collectives  26.9 us (18%)
  local copies, waits for them, and re-layouts  6.61 us (4%)
    ppermute x23, starting transfers between devices, seq_permute(): return lax.ppermute(value, 'seq', pairs)  43.8 us
    pallas_call x3, Pallas kernels, attention(): pl.pallas_call(functools.partial(attention_kernel, len(shards), first, la...  31.2 us
    ppermute x23, waiting for transfers between devices, seq_permute(): return lax.ppermute(value, 'seq', pairs)  28.8 us
    all_to_all x1, blocking collectives, body(): lax.all_to_all(shares, ('seq', 'head'), 0, 0, axis_index_groups=PLANES, t...  26.9 us
    unnamed x50, local copies, waits for them, and re-layouts  5.27 us
    pallas_call x1, Pallas kernels, product(): pl.pallas_call(product_kernel, out_shape=jax.ShapeDtypeStruct((YC, Z, TOK...  4.28 us
  transfers between devices with their start and end apart: 23, of which 8 were waited for; matrix products, arithmetic and copies ran while one was open for 1% of the time, Pallas kernels for 24%

profile of v5, /device:TPU:1, one launch (start us, length us, event | category | flops | bytes accessed | tf_op | source)
XLA Modules:
  0.0 148.0 jit_solution(4650274461492825302)
XLA Ops:
  0.0 7.7 %collective-permute-start = (bf16[64,1024]{1,0:T(8,128)(2,1)}, bf16[64,1024]{1,0:T(8,128)(2,1)S(1)}, u32[]{:S(2)}, u32[]{:S(2)}) collective-permute-start(bf16[64,1024]{1,0:T(8,128)(2,1)} %refs_3_.5), channel_id=1, source_target_pairs={{0,128},{8,136},{16,144},{24,152},{32,160},{40,168},{48,176},{56,1... | collective-permute-start | bytes 393224 | tf_op jit(solution)/shard_map/ppermute | solution.py:39
  7.7 1.3 collective-permute-start.1
  9.7 1.9 %pack.1.refs_4_.refs_8_ = bf16[2192,128]{1,0:T(8,128)(2,1)} custom-call(s32[1]{0:T(128)S(6)} %copy.9.length_ref, bf16[1,1024,128]{2,1,0:T(8,128)(2,1)} %k_ref.1, bf16[1,1024,128]{2,1,0:T(8,128)(2,1)} %v_ref.1, bf16[64,128]{1,0:T(8,128)(2,1)} %nk_ref.1, bf16[64,128]{1,0:T(8,128)(2,1)} %nv_ref.1), custom_call_target="tpu_custom_call" | custom-call | tf_op jit(solution)/shard_map/pack/pallas_call | solution.py:55
  11.6 1.2 collective-permute-start.6
  12.9 4.1 %collective-permute-start.4 = (bf16[2192,128]{1,0:T(8,128)(2,1)}, bf16[2192,128]{1,0:T(8,128)(2,1)S(1)}, u32[]{:S(2)}, u32[]{:S(2)}) collective-permute-start(bf16[2192,128]{1,0:T(8,128)(2,1)} %pack.1.refs_4_.refs_8_), channel_id=1, source_target_pairs={{0,224},{8,232},{16,240},{24,248},{32,0},{40,8},{48,16},{56,24},{6... | collective-permute-start | bytes 1683464 | tf_op jit(solution)/shard_map/ppermute | solution.py:39
  16.9 1.3 collective-permute-start.2
  18.2 0.7 reshape.12.refs_17_
  18.9 0.7 stack.60.refs_16_
  19.6 1.5 collective-permute-done.2.refs_0_
  21.1 0.0 collective-permute-done.6.refs_5_.refs_9_
  21.1 0.6 copy-done.10
  21.7 0.8 copy-done.1
  22.5 10.3 %attention.3 = (f32[1,2048]{1,0:T(1,128)}, f32[144,2048]{1,0:T(8,128)}) custom-call(bf16[64,1024]{1,0:T(8,128)(2,1)} %copy-done.10, bf16[64,1024]{1,0:T(8,128)(2,1)} %copy-done.8, bf16[64,1024]{1,0:T(8,128)(2,1)} %copy-done.9, bf16[64,1024]{1,0:T(8,128)(2,1)} %refs_3_.5, bf16[2192,128]{1,0:T(8,128)(2,1)} %pack.1.refs_4_.refs_8_, bf16[2192,128]{1,0:T(8,128)(2,1)} %copy-done.1), custom_call_target="tpu_custom_call" | custom-call | flops 1 | bytes 1 | tf_op jit(solution)/shard_map/attention/pallas_call | solution.py:234
  32.9 0.0 collective-permute-done.5.refs_6_.refs_12_
  32.9 1.9 %collective-permute-start.7 = (bf16[2192,128]{1,0:T(8,128)(2,1)S(1)}, bf16[2192,128]{1,0:T(8,128)(2,1)S(1)}, u32[]{:S(2)}, u32[]{:S(2)}) collective-permute-start(bf16[2192,128]{1,0:T(8,128)(2,1)S(1)} %collective-permute-done.4.refs_4_.refs_10_), channel_id=1, source_target_pairs={{0,8},{8,0},{16,24},{24,16},{32,40},{40,32},{48,56},{56,48},{64,72... | collective-permute-start | bytes 1683464 | tf_op jit(solution)/shard_map/ppermute | solution.py:39
  34.8 0.1 collective-permute-start.8
  34.9 0.7 collective-permute-start.3
  35.5 4.5 %collective-permute-start.21 = (bf16[1024,256]{1,0:T(8,128)(2,1)S(1)}, bf16[1024,256]{1,0:T(8,128)(2,1)}, u32[]{:S(2)}, u32[]{:S(2)}) collective-permute-start(bf16[1024,256]{1,0:T(8,128)(2,1)S(1)} %copy-done.11), channel_id=1, source_target_pairs={{0,16},{8,24},{16,0},{24,8},{32,48},{40,56},{48,32},{56,40},{64,80... | collective-permute-start | bytes 1572872 | tf_op jit(solution)/shard_map/ppermute | solution.py:39
  40.0 0.0 collective-permute-done.7.refs_5_.refs_11_
  40.0 0.8 copy-done.4
  40.8 0.8 copy-done.5
  41.6 11.4 %attention.4 = (f32[1,2048]{1,0:T(1,128)}, f32[144,2048]{1,0:T(8,128)}) custom-call(bf16[64,1024]{1,0:T(8,128)(2,1)} %copy-done.10, bf16[64,1024]{1,0:T(8,128)(2,1)} %copy-done.8, bf16[64,1024]{1,0:T(8,128)(2,1)} %copy-done.9, bf16[64,1024]{1,0:T(8,128)(2,1)} %refs_3_.5, bf16[2192,128]{1,0:T(8,128)(2,1)} %copy-done.2, bf16[2192,128]{1,0:T(8,128)(2,1)} %copy-done.4, ...), custom_call_target="tpu_custom_call" | custom-call | flops 1 | bytes 1 | tf_op jit(solution)/shard_map/attention/pallas_call | solution.py:234
  53.1 1.1 collective-permute-start.9
  54.1 0.1 collective-permute-start.20
  54.2 0.4 collective-permute-start.22
  54.6 1.1 collective-permute-done.9.refs_5_.refs_15_
  55.7 0.8 copy-done.7
  56.5 9.5 %attention.5 = (bf16[64,1152]{1,0:T(8,128)(2,1)}, bf16[64,1152]{1,0:T(8,128)(2,1)}, bf16[64,1152]{1,0:T(8,128)(2,1)}, bf16[64,1152]{1,0:T(8,128)(2,1)}) custom-call(bf16[64,1024]{1,0:T(8,128)(2,1)} %copy-done.10, bf16[64,1024]{1,0:T(8,128)(2,1)} %copy-done.8, bf16[64,1024]{1,0:T(8,128)(2,1)} %copy-done.9, bf16[64,1024]{1,0:T(8,128)(2,1)} %refs_3_.5, ...), custom_call_target="tpu_custom_call" | custom-call | flops 1 | bytes 1 | tf_op jit(solution)/shard_map/attention/pallas_call | solution.py:234
  66.0 6.3 %collective-permute-start.10 = (bf16[64,1152]{1,0:T(8,128)(2,1)}, bf16[64,1152]{1,0:T(8,128)(2,1)S(1)}, u32[]{:S(2)}, u32[]{:S(2)}) collective-permute-start(bf16[64,1152]{1,0:T(8,128)(2,1)} %get-tuple-element.48), channel_id=1, source_target_pairs={{0,144},{8,152},{16,128},{24,136},{32,176},{40,184},{48,160},{56,1... | collective-permute-start | bytes 442376 | tf_op jit(solution)/shard_map/ppermute | solution.py:39
  72.3 6.5 %collective-permute-start.11 = (bf16[64,1152]{1,0:T(8,128)(2,1)}, bf16[64,1152]{1,0:T(8,128)(2,1)S(1)}, u32[]{:S(2)}, u32[]{:S(2)}) collective-permute-start(bf16[64,1152]{1,0:T(8,128)(2,1)} %get-tuple-element.49), channel_id=1, source_target_pairs={{0,128},{8,136},{16,144},{24,152},{32,160},{40,168},{48,176},{56,1... | collective-permute-start | bytes 442376 | tf_op jit(solution)/shard_map/ppermute | solution.py:39
  78.8 3.6 %collective-permute-done.10.refs_0_ = bf16[64,1152]{1,0:T(8,128)(2,1)S(1)} collective-permute-done((bf16[64,1152]{1,0:T(8,128)(2,1)}, bf16[64,1152]{1,0:T(8,128)(2,1)S(1)}, u32[]{:S(2)}, u32[]{:S(2)}) %collective-permute-start.10) | collective-permute-done | bytes 147488 | tf_op jit(solution)/shard_map/ppermute | solution.py:39
  82.4 8.2 %collective-permute-done.11.refs_1_ = bf16[64,1152]{1,0:T(8,128)(2,1)S(1)} collective-permute-done((bf16[64,1152]{1,0:T(8,128)(2,1)}, bf16[64,1152]{1,0:T(8,128)(2,1)S(1)}, u32[]{:S(2)}, u32[]{:S(2)}) %collective-permute-start.11) | collective-permute-done | bytes 147488 | tf_op jit(solution)/shard_map/ppermute | solution.py:39
  90.6 0.6 copy-done.15
  91.2 0.1 copy-done.16
  91.3 2.3 %merge.1.refs_0_ = bf16[64,1024]{1,0:T(8,128)(2,1)} custom-call(bf16[64,1152]{1,0:T(8,128)(2,1)} %copy-done.14, bf16[64,1152]{1,0:T(8,128)(2,1)} %copy-done.15, bf16[64,1152]{1,0:T(8,128)(2,1)} %copy-done.16, bf16[64,1152]{1,0:T(8,128)(2,1)} %get-tuple-element.51.refs_3_), custom_call_target="tpu_custom_call" | custom-call | tf_op jit(solution)/shard_map/merge/pallas_call | solution.py:266
  93.6 1.5 %collective-permute-start.18 = (bf16[64,1024]{1,0:T(8,128)(2,1)}, bf16[64,1024]{1,0:T(8,128)(2,1)S(1)}, u32[]{:S(2)}, u32[]{:S(2)}) collective-permute-start(bf16[64,1024]{1,0:T(8,128)(2,1)} %merge.1.refs_0_), channel_id=1, source_target_pairs={{0,32},{8,40},{16,48},{24,56},{32,64},{40,72},{48,80},{56,88},{64,... | collective-permute-start | bytes 393224 | tf_op jit(solution)/shard_map/ppermute | solution.py:39
  95.1 3.5 %collective-permute-start.14 = (bf16[64,1024]{1,0:T(8,128)(2,1)}, bf16[64,1024]{1,0:T(8,128)(2,1)S(1)}, u32[]{:S(2)}, u32[]{:S(2)}) collective-permute-start(bf16[64,1024]{1,0:T(8,128)(2,1)} %merge.1.refs_0_), channel_id=1, source_target_pairs={{0,192},{8,200},{16,208},{24,216},{32,224},{40,232},{48,240},{56,2... | collective-permute-start | bytes 393224 | tf_op jit(solution)/shard_map/ppermute | solution.py:39
  98.6 0.3 collective-permute-start.15
  98.9 2.2 %collective-permute-done.16.refs_6_ = bf16[64,1024]{1,0:T(8,128)(2,1)S(1)} collective-permute-done((bf16[64,1024]{1,0:T(8,128)(2,1)}, bf16[64,1024]{1,0:T(8,128)(2,1)S(1)}, u32[]{:S(2)}, u32[]{:S(2)}) %collective-permute-start.16) | collective-permute-done | bytes 131104 | tf_op jit(solution)/shard_map/ppermute | solution.py:39
  101.2 1.2 collective-permute-start.17
  102.4 5.7 %collective-permute-done.18.refs_7_ = bf16[64,1024]{1,0:T(8,128)(2,1)S(1)} collective-permute-done((bf16[64,1024]{1,0:T(8,128)(2,1)}, bf16[64,1024]{1,0:T(8,128)(2,1)S(1)}, u32[]{:S(2)}, u32[]{:S(2)}) %collective-permute-start.18) | collective-permute-done | bytes 131104 | tf_op jit(solution)/shard_map/ppermute | solution.py:39
  108.1 0.6 pad_add_fusion.place_ref
  108.8 1.1 collective-permute-done.15.refs_3_
  109.9 5.5 %collective-permute-done.19.refs_5_ = bf16[64,1024]{1,0:T(8,128)(2,1)S(1)} collective-permute-done((bf16[64,1024]{1,0:T(8,128)(2,1)S(1)}, bf16[64,1024]{1,0:T(8,128)(2,1)S(1)}, u32[]{:S(2)}, u32[]{:S(2)}) %collective-permute-start.19) | collective-permute-done | bytes 131104 | tf_op jit(solution)/shard_map/ppermute | solution.py:39
  115.4 0.6 copy-done.23
  116.0 4.3 %product.1 = bf16[4,8,64,256]{3,2,1,0:T(8,128)(2,1)} custom-call(s32[2]{0:T(128)} %pad_add_fusion.place_ref, bf16[64,1024]{1,0:T(8,128)(2,1)} %merge.1.refs_0_, bf16[64,1024]{1,0:T(8,128)(2,1)} %copy-done.17, bf16[64,1024]{1,0:T(8,128)(2,1)} %copy-done.20, bf16[64,1024]{1,0:T(8,128)(2,1)} %copy-done.21, bf16[64,1024]{1,0:T(8,128)(2,1)} %copy-done.22, ...), custom_call_target="tpu_custom_call" | custom-call | tf_op jit(solution)/shard_map/product/pallas_call | solution.py:286
  120.3 26.9 %all_to_all.5 = bf16[32,64,256]{2,1,0:T(8,128)(2,1)S(1)} all-to-all(bf16[32,64,256]{2,1,0:T(8,128)(2,1)} %bitcast.17), channel_id=1, replica_groups={{0,1,2,3,4,5,6,7,8,9,10,11,12,13,14,15,16,17,18,19,20,21,22,23,24,25,26..., dimensions={0} | all-to-all | bytes 2097152 | tf_op jit(solution)/shard_map/all_to_all | solution.py:344
  147.2 0.8 bitcast_reduce_fusion
  (59 shorter events, 0.1 us)
Async XLA Ops:
  0.0 18.2 %copy-start.24 = (s32[2048]{0:T(1024)S(1)}, s32[2048]{0:T(1024)}, u32[]{:S(2)}) copy-start(s32[2048]{0:T(1024)} %param.14) | copy-start | bytes 24580
  0.0 12.8 %collective-permute-start = (bf16[64,1024]{1,0:T(8,128)(2,1)}, bf16[64,1024]{1,0:T(8,128)(2,1)S(1)}, u32[]{:S(2)}, u32[]{:S(2)}) collective-permute-start(bf16[64,1024]{1,0:T(8,128)(2,1)} %refs_3_.5), channel_id=1, source_target_pairs={{0,128},{8,136},{16,144},{24,152},{32,160},{40,168},{48,176},{56,1... | collective-permute-start | bytes 393224 | tf_op jit(solution)/shard_map/ppermute | solution.py:39
  7.7 5.1 %collective-permute-start.1 = (bf16[64,1024]{1,0:T(8,128)(2,1)}, bf16[64,1024]{1,0:T(8,128)(2,1)S(1)}, u32[]{:S(2)}, u32[]{:S(2)}) collective-permute-start(bf16[64,1024]{1,0:T(8,128)(2,1)} %refs_3_.5), channel_id=1, source_target_pairs={{0,16},{8,24},{16,0},{24,8},{32,48},{40,56},{48,32},{56,40},{64,80... | collective-permute-start | bytes 393224 | tf_op jit(solution)/shard_map/ppermute | solution.py:39
  11.6 23.3 %copy-start = (bf16[2192,128]{1,0:T(8,128)(2,1)S(1)}, bf16[2192,128]{1,0:T(8,128)(2,1)}, u32[]{:S(2)}) copy-start(bf16[2192,128]{1,0:T(8,128)(2,1)} %pack.1.refs_4_.refs_8_) | copy-start | bytes 1683460
  11.6 23.9 %copy-start.11 = (bf16[1024,256]{1,0:T(8,128)(2,1)S(1)}, bf16[1024,256]{1,0:T(8,128)(2,1)}, u32[]{:S(2)}) copy-start(bf16[1024,256]{1,0:T(8,128)(2,1)} %refs_8_.1) | copy-start | bytes 1572868
  11.6 9.5 %collective-permute-start.6 = (bf16[2192,128]{1,0:T(8,128)(2,1)}, bf16[2192,128]{1,0:T(8,128)(2,1)S(1)}, u32[]{:S(2)}, u32[]{:S(2)}) collective-permute-start(bf16[2192,128]{1,0:T(8,128)(2,1)} %pack.1.refs_4_.refs_8_), channel_id=1, source_target_pairs={{0,8},{8,0},{16,24},{24,16},{32,40},{40,32},{48,56},{56,48},{64,72... | collective-permute-start | bytes 1683464 | tf_op jit(solution)/shard_map/ppermute | solution.py:39
  12.8 8.2 %copy-start.8 = (bf16[64,1024]{1,0:T(8,128)(2,1)}, bf16[64,1024]{1,0:T(8,128)(2,1)S(1)}, u32[]{:S(2)}) copy-start(bf16[64,1024]{1,0:T(8,128)(2,1)S(1)} %collective-permute-done.refs_1_) | copy-start | bytes 393220
  12.8 8.2 %copy-start.9 = (bf16[64,1024]{1,0:T(8,128)(2,1)}, bf16[64,1024]{1,0:T(8,128)(2,1)S(1)}, u32[]{:S(2)}) copy-start(bf16[64,1024]{1,0:T(8,128)(2,1)S(1)} %collective-permute-done.1.refs_2_) | copy-start | bytes 393220
  12.9 20.0 %collective-permute-start.4 = (bf16[2192,128]{1,0:T(8,128)(2,1)}, bf16[2192,128]{1,0:T(8,128)(2,1)S(1)}, u32[]{:S(2)}, u32[]{:S(2)}) collective-permute-start(bf16[2192,128]{1,0:T(8,128)(2,1)} %pack.1.refs_4_.refs_8_), channel_id=1, source_target_pairs={{0,224},{8,232},{16,240},{24,248},{32,0},{40,8},{48,16},{56,24},{6... | collective-permute-start | bytes 1683464 | tf_op jit(solution)/shard_map/ppermute | solution.py:39
  16.9 15.9 %collective-permute-start.5 = (bf16[2192,128]{1,0:T(8,128)(2,1)}, bf16[2192,128]{1,0:T(8,128)(2,1)S(1)}, u32[]{:S(2)}, u32[]{:S(2)}) collective-permute-start(bf16[2192,128]{1,0:T(8,128)(2,1)} %pack.1.refs_4_.refs_8_), channel_id=1, source_target_pairs={{0,32},{8,40},{16,48},{24,56},{32,64},{40,72},{48,80},{56,88},{64,... | collective-permute-start | bytes 1683464 | tf_op jit(solution)/shard_map/ppermute | solution.py:39
  16.9 4.1 %collective-permute-start.2 = (bf16[64,1024]{1,0:T(8,128)(2,1)S(1)}, bf16[64,1024]{1,0:T(8,128)(2,1)S(1)}, u32[]{:S(2)}, u32[]{:S(2)}) collective-permute-start(bf16[64,1024]{1,0:T(8,128)(2,1)S(1)} %collective-permute-done.refs_1_), channel_id=1, source_target_pairs={{0,16},{8,24},{16,0},{24,8},{32,48},{40,56},{48,32},{56,40},{64,80... | collective-permute-start | bytes 393224 | tf_op jit(solution)/shard_map/ppermute | solution.py:39
  21.1 0.7 copy-start.10
  21.7 0.8 copy-start.1
  32.8 7.2 %copy-start.2 = (bf16[2192,128]{1,0:T(8,128)(2,1)}, bf16[2192,128]{1,0:T(8,128)(2,1)S(1)}, u32[]{:S(2)}) copy-start(bf16[2192,128]{1,0:T(8,128)(2,1)S(1)} %collective-permute-done.4.refs_4_.refs_10_) | copy-start | bytes 1683460
  32.9 7.2 %copy-start.3 = (bf16[2192,128]{1,0:T(8,128)(2,1)}, bf16[2192,128]{1,0:T(8,128)(2,1)S(1)}, u32[]{:S(2)}) copy-start(bf16[2192,128]{1,0:T(8,128)(2,1)S(1)} %collective-permute-done.5.refs_6_.refs_12_) | copy-start | bytes 1683460
  32.9 7.1 %collective-permute-start.7 = (bf16[2192,128]{1,0:T(8,128)(2,1)S(1)}, bf16[2192,128]{1,0:T(8,128)(2,1)S(1)}, u32[]{:S(2)}, u32[]{:S(2)}) collective-permute-start(bf16[2192,128]{1,0:T(8,128)(2,1)S(1)} %collective-permute-done.4.refs_4_.refs_10_), channel_id=1, source_target_pairs={{0,8},{8,0},{16,24},{24,16},{32,40},{40,32},{48,56},{56,48},{64,72... | collective-permute-start | bytes 1683464 | tf_op jit(solution)/shard_map/ppermute | solution.py:39
  34.8 5.2 %collective-permute-start.8 = (bf16[2192,128]{1,0:T(8,128)(2,1)S(1)}, bf16[2192,128]{1,0:T(8,128)(2,1)S(1)}, u32[]{:S(2)}, u32[]{:S(2)}) collective-permute-start(bf16[2192,128]{1,0:T(8,128)(2,1)S(1)} %collective-permute-done.5.refs_6_.refs_12_), channel_id=1, source_target_pairs={{0,8},{8,0},{16,24},{24,16},{32,40},{40,32},{48,56},{56,48},{64,72... | collective-permute-start | bytes 1683464 | tf_op jit(solution)/shard_map/ppermute | solution.py:39
  34.9 18.2 %collective-permute-start.3 = (bf16[2192,128]{1,0:T(8,128)(2,1)S(1)}, bf16[2192,128]{1,0:T(8,128)(2,1)S(1)}, u32[]{:S(2)}, u32[]{:S(2)}) collective-permute-start(bf16[2192,128]{1,0:T(8,128)(2,1)S(1)} %copy-done), channel_id=1, source_target_pairs={{0,192},{8,200},{16,208},{24,216},{32,96},{40,104},{48,112},{56,12... | collective-permute-start | bytes 1683464 | tf_op jit(solution)/shard_map/ppermute | solution.py:39
  35.5 18.7 %collective-permute-start.21 = (bf16[1024,256]{1,0:T(8,128)(2,1)S(1)}, bf16[1024,256]{1,0:T(8,128)(2,1)}, u32[]{:S(2)}, u32[]{:S(2)}) collective-permute-start(bf16[1024,256]{1,0:T(8,128)(2,1)S(1)} %copy-done.11), channel_id=1, source_target_pairs={{0,16},{8,24},{16,0},{24,8},{32,48},{40,56},{48,32},{56,40},{64,80... | collective-permute-start | bytes 1572872 | tf_op jit(solution)/shard_map/ppermute | solution.py:39
  40.0 0.8 copy-start.4
  40.8 0.8 copy-start.5
  53.1 2.7 %copy-start.6 = (bf16[2192,128]{1,0:T(8,128)(2,1)}, bf16[2192,128]{1,0:T(8,128)(2,1)S(1)}, u32[]{:S(2)}) copy-start(bf16[2192,128]{1,0:T(8,128)(2,1)S(1)} %collective-permute-done.3.refs_4_.refs_14_) | copy-start | bytes 1683460
  53.1 2.7 %collective-permute-start.9 = (bf16[2192,128]{1,0:T(8,128)(2,1)S(1)}, bf16[2192,128]{1,0:T(8,128)(2,1)S(1)}, u32[]{:S(2)}, u32[]{:S(2)}) collective-permute-start(bf16[2192,128]{1,0:T(8,128)(2,1)S(1)} %collective-permute-done.3.refs_4_.refs_14_), channel_id=1, source_target_pairs={{0,8},{8,0},{16,24},{24,16},{32,40},{40,32},{48,56},{56,48},{64,72... | collective-permute-start | bytes 1683464 | tf_op jit(solution)/shard_map/ppermute | solution.py:39
  54.1 41.0 %collective-permute-start.20 = (bf16[1024,256]{1,0:T(8,128)(2,1)S(1)}, bf16[1024,256]{1,0:T(8,128)(2,1)S(1)}, u32[]{:S(2)}, u32[]{:S(2)}) collective-permute-start(bf16[1024,256]{1,0:T(8,128)(2,1)S(1)} %copy-done.11), channel_id=1, source_target_pairs={{0,8},{8,0},{16,24},{24,16},{32,40},{40,32},{48,56},{56,48},{64,72... | collective-permute-start | bytes 1572872 | tf_op jit(solution)/shard_map/ppermute | solution.py:39
  54.2 54.5 %collective-permute-start.22 = (bf16[1024,256]{1,0:T(8,128)(2,1)}, bf16[1024,256]{1,0:T(8,128)(2,1)S(1)}, u32[]{:S(2)}, u32[]{:S(2)}) collective-permute-start(bf16[1024,256]{1,0:T(8,128)(2,1)} %collective-permute-done.21.refs_10_), channel_id=1, source_target_pairs={{0,8},{8,0},{16,24},{24,16},{32,40},{40,32},{48,56},{56,48},{64,72... | collective-permute-start | bytes 1572872 | tf_op jit(solution)/shard_map/ppermute | solution.py:39
  55.7 0.8 copy-start.7
  66.0 16.4 %collective-permute-start.10 = (bf16[64,1152]{1,0:T(8,128)(2,1)}, bf16[64,1152]{1,0:T(8,128)(2,1)S(1)}, u32[]{:S(2)}, u32[]{:S(2)}) collective-permute-start(bf16[64,1152]{1,0:T(8,128)(2,1)} %get-tuple-element.48), channel_id=1, source_target_pairs={{0,144},{8,152},{16,128},{24,136},{32,176},{40,184},{48,160},{56,1... | collective-permute-start | bytes 442376 | tf_op jit(solution)/shard_map/ppermute | solution.py:39
  72.3 18.2 %collective-permute-start.11 = (bf16[64,1152]{1,0:T(8,128)(2,1)}, bf16[64,1152]{1,0:T(8,128)(2,1)S(1)}, u32[]{:S(2)}, u32[]{:S(2)}) collective-permute-start(bf16[64,1152]{1,0:T(8,128)(2,1)} %get-tuple-element.49), channel_id=1, source_target_pairs={{0,128},{8,136},{16,144},{24,152},{32,160},{40,168},{48,176},{56,1... | collective-permute-start | bytes 442376 | tf_op jit(solution)/shard_map/ppermute | solution.py:39
  78.8 11.8 %collective-permute-start.12 = (bf16[64,1152]{1,0:T(8,128)(2,1)}, bf16[64,1152]{1,0:T(8,128)(2,1)S(1)}, u32[]{:S(2)}, u32[]{:S(2)}) collective-permute-start(bf16[64,1152]{1,0:T(8,128)(2,1)} %get-tuple-element.50), channel_id=1, source_target_pairs={{0,16},{8,24},{16,0},{24,8},{32,48},{40,56},{48,32},{56,40},{64,80... | collective-permute-start | bytes 442376 | tf_op jit(solution)/shard_map/ppermute | solution.py:39
  82.4 8.2 %copy-start.14 = (bf16[64,1152]{1,0:T(8,128)(2,1)}, bf16[64,1152]{1,0:T(8,128)(2,1)S(1)}, u32[]{:S(2)}) copy-start(bf16[64,1152]{1,0:T(8,128)(2,1)S(1)} %collective-permute-done.10.refs_0_) | copy-start | bytes 442372
  90.6 0.7 copy-start.15
  90.6 0.7 copy-start.16
  93.6 5.1 %collective-permute-start.13 = (bf16[64,1024]{1,0:T(8,128)(2,1)}, bf16[64,1024]{1,0:T(8,128)(2,1)S(1)}, u32[]{:S(2)}, u32[]{:S(2)}) collective-permute-start(bf16[64,1024]{1,0:T(8,128)(2,1)} %merge.1.refs_0_), channel_id=1, source_target_pairs={{0,224},{8,232},{16,240},{24,248},{32,0},{40,8},{48,16},{56,24},{6... | collective-permute-start | bytes 393224 | tf_op jit(solution)/shard_map/ppermute | solution.py:39
  93.6 7.6 %collective-permute-start.16 = (bf16[64,1024]{1,0:T(8,128)(2,1)}, bf16[64,1024]{1,0:T(8,128)(2,1)S(1)}, u32[]{:S(2)}, u32[]{:S(2)}) collective-permute-start(bf16[64,1024]{1,0:T(8,128)(2,1)} %merge.1.refs_0_), channel_id=1, source_target_pairs={{0,64},{8,72},{16,80},{24,88},{32,96},{40,104},{48,112},{56,120},{... | collective-permute-start | bytes 393224 | tf_op jit(solution)/shard_map/ppermute | solution.py:39
  93.6 14.5 %collective-permute-start.18 = (bf16[64,1024]{1,0:T(8,128)(2,1)}, bf16[64,1024]{1,0:T(8,128)(2,1)S(1)}, u32[]{:S(2)}, u32[]{:S(2)}) collective-permute-start(bf16[64,1024]{1,0:T(8,128)(2,1)} %merge.1.refs_0_), channel_id=1, source_target_pairs={{0,32},{8,40},{16,48},{24,56},{32,64},{40,72},{48,80},{56,88},{64,... | collective-permute-start | bytes 393224 | tf_op jit(solution)/shard_map/ppermute | solution.py:39
  95.1 20.2 %copy-start.12 = (bf16[1024,256]{1,0:T(8,128)(2,1)}, bf16[1024,256]{1,0:T(8,128)(2,1)S(1)}, u32[]{:S(2)}) copy-start(bf16[1024,256]{1,0:T(8,128)(2,1)S(1)} %collective-permute-done.20.refs_9_) | copy-start | bytes 1572868
  95.1 13.7 %collective-permute-start.14 = (bf16[64,1024]{1,0:T(8,128)(2,1)}, bf16[64,1024]{1,0:T(8,128)(2,1)S(1)}, u32[]{:S(2)}, u32[]{:S(2)}) collective-permute-start(bf16[64,1024]{1,0:T(8,128)(2,1)} %merge.1.refs_0_), channel_id=1, source_target_pairs={{0,192},{8,200},{16,208},{24,216},{32,224},{40,232},{48,240},{56,2... | collective-permute-start | bytes 393224 | tf_op jit(solution)/shard_map/ppermute | solution.py:39
  98.6 16.7 %copy-start.17 = (bf16[64,1024]{1,0:T(8,128)(2,1)}, bf16[64,1024]{1,0:T(8,128)(2,1)S(1)}, u32[]{:S(2)}) copy-start(bf16[64,1024]{1,0:T(8,128)(2,1)S(1)} %collective-permute-done.13.refs_1_) | copy-start | bytes 393220
  98.6 11.2 %collective-permute-start.15 = (bf16[64,1024]{1,0:T(8,128)(2,1)S(1)}, bf16[64,1024]{1,0:T(8,128)(2,1)S(1)}, u32[]{:S(2)}, u32[]{:S(2)}) collective-permute-start(bf16[64,1024]{1,0:T(8,128)(2,1)S(1)} %collective-permute-done.13.refs_1_), channel_id=1, source_target_pairs={{0,192},{8,200},{16,208},{24,216},{32,224},{40,232},{48,240},{56,2... | collective-permute-start | bytes 393224 | tf_op jit(solution)/shard_map/ppermute | solution.py:39
  101.2 14.2 %copy-start.18 = (bf16[64,1024]{1,0:T(8,128)(2,1)}, bf16[64,1024]{1,0:T(8,128)(2,1)S(1)}, u32[]{:S(2)}) copy-start(bf16[64,1024]{1,0:T(8,128)(2,1)S(1)} %collective-permute-done.16.refs_6_) | copy-start | bytes 393220
  101.2 8.7 %collective-permute-start.17 = (bf16[64,1024]{1,0:T(8,128)(2,1)S(1)}, bf16[64,1024]{1,0:T(8,128)(2,1)S(1)}, u32[]{:S(2)}, u32[]{:S(2)}) collective-permute-start(bf16[64,1024]{1,0:T(8,128)(2,1)S(1)} %collective-permute-done.16.refs_6_), channel_id=1, source_target_pairs={{0,64},{8,72},{16,80},{24,88},{32,96},{40,104},{48,112},{56,120},{... | collective-permute-start | bytes 393224 | tf_op jit(solution)/shard_map/ppermute | solution.py:39
  108.1 7.2 %copy-start.19 = (bf16[64,1024]{1,0:T(8,128)(2,1)}, bf16[64,1024]{1,0:T(8,128)(2,1)S(1)}, u32[]{:S(2)}) copy-start(bf16[64,1024]{1,0:T(8,128)(2,1)S(1)} %collective-permute-done.18.refs_7_) | copy-start | bytes 393220
  108.1 7.2 %collective-permute-start.19 = (bf16[64,1024]{1,0:T(8,128)(2,1)S(1)}, bf16[64,1024]{1,0:T(8,128)(2,1)S(1)}, u32[]{:S(2)}, u32[]{:S(2)}) collective-permute-start(bf16[64,1024]{1,0:T(8,128)(2,1)S(1)} %collective-permute-done.18.refs_7_), channel_id=1, source_target_pairs={{0,64},{8,72},{16,80},{24,88},{32,96},{40,104},{48,112},{56,120},{... | collective-permute-start | bytes 393224 | tf_op jit(solution)/shard_map/ppermute | solution.py:39
  108.7 6.6 %copy-start.13 = (bf16[1024,256]{1,0:T(8,128)(2,1)}, bf16[1024,256]{1,0:T(8,128)(2,1)S(1)}, u32[]{:S(2)}) copy-start(bf16[1024,256]{1,0:T(8,128)(2,1)S(1)} %collective-permute-done.22.refs_11_) | copy-start | bytes 1572868
  108.7 6.6 %copy-start.20 = (bf16[64,1024]{1,0:T(8,128)(2,1)}, bf16[64,1024]{1,0:T(8,128)(2,1)S(1)}, u32[]{:S(2)}) copy-start(bf16[64,1024]{1,0:T(8,128)(2,1)S(1)} %collective-permute-done.14.refs_2_) | copy-start | bytes 393220
  109.8 5.5 %copy-start.21 = (bf16[64,1024]{1,0:T(8,128)(2,1)}, bf16[64,1024]{1,0:T(8,128)(2,1)S(1)}, u32[]{:S(2)}) copy-start(bf16[64,1024]{1,0:T(8,128)(2,1)S(1)} %collective-permute-done.15.refs_3_) | copy-start | bytes 393220
  109.9 5.5 %copy-start.22 = (bf16[64,1024]{1,0:T(8,128)(2,1)}, bf16[64,1024]{1,0:T(8,128)(2,1)S(1)}, u32[]{:S(2)}) copy-start(bf16[64,1024]{1,0:T(8,128)(2,1)S(1)} %collective-permute-done.17.refs_4_) | copy-start | bytes 393220
  115.4 0.6 copy-start.23

commit v6 on v5

--- a/solution.py
+++ b/solution.py
@@ -324,11 +324,10 @@
     state = attention(q_blocks, own_pair)
     kv_up, kv_down, *state = lax.optimization_barrier((kv_up, kv_down, *state))
     next_pairs = (kv_up, over_c(kv_up), kv_down, over_c(kv_down))
-    weight = lax.optimization_barrier((out_weight, kv_up, kv_down))[0]
+    state = attention(q_blocks, next_pairs, state)
+    kv_two, weight, *state = lax.optimization_barrier((kv_two, out_weight, *state))
     weight_y = over_y(weight)
     weights = [out_weight, over_c(weight), weight_y, over_c(weight_y)]
-    state = attention(q_blocks, next_pairs, state)
-    kv_two, *state = lax.optimization_barrier((kv_two, *state))
     last_pair = (kv_two, over_c(kv_two))
     new = (*own_pair, *next_pairs, *last_pair)
     cross, far, side, mine = attention(q_blocks, last_pair, state, new, ids, span)

time: 149 us -> 162 us (1.087)
  waiting for transfers between devices: 28.8 us -> 35.8 us
  Pallas kernels: 39.7 us -> 45.9 us
  blocking collectives: 26.9 us -> 32.7 us
  starting transfers between devices: 43.8 us -> 38.1 us
    ppermute x23, waiting for transfers between devices: 28.8 us -> 35.8 us  [seq_permute(): return lax.ppermute(value, 'seq', pairs)]
    pallas_call x3, Pallas kernels: 31.2 us -> 37.5 us  [attention(): pl.pallas_call(functools.partial(attention_kernel, len(shards), first, la...]
    all_to_all x1, blocking collectives: 26.9 us -> 32.7 us  [body(): lax.all_to_all(shares, ('seq', 'head'), 0, 0, axis_index_groups=PLANES, t...]
    ppermute x23, starting transfers between devices: 43.8 us -> 38.1 us  [seq_permute(): return lax.ppermute(value, 'seq', pairs)]
    unnamed x50 -> x52, local copies, waits for them, and re-layouts: 5.27 us -> 6.02 us
  transfers between devices with their start and end apart: 23 -> 23, of which waited for: 8 -> 10; matrix products, arithmetic and copies ran while one was open for 1% -> 1% of each run, Pallas kernels for 24% -> 26%
where the time goes in v6:
time: 162 us
  Pallas kernels  45.9 us (28%)
  starting transfers between devices  38.1 us (24%)
  waiting for transfers between devices  35.8 us (22%)
  blocking collectives  32.7 us (20%)
  local copies, waits for them, and re-layouts  7.36 us (5%)
    ppermute x23, starting transfers between devices, seq_permute(): return lax.ppermute(value, 'seq', pairs)  38.1 us
    pallas_call x3, Pallas kernels, attention(): pl.pallas_call(functools.partial(attention_kernel, len(shards), first, la...  37.5 us
    ppermute x23, waiting for transfers between devices, seq_permute(): return lax.ppermute(value, 'seq', pairs)  35.8 us
    all_to_all x1, blocking collectives, body(): lax.all_to_all(shares, ('seq', 'head'), 0, 0, axis_index_groups=PLANES, t...  32.7 us
    unnamed x52, local copies, waits for them, and re-layouts  6.02 us
    pallas_call x1, Pallas kernels, product(): pl.pallas_call(product_kernel, out_shape=jax.ShapeDtypeStruct((YC, Z, TOK...  4.26 us
  transfers between devices with their start and end apart: 23, of which 10 were waited for; matrix products, arithmetic and copies ran while one was open for 1% of the time, Pallas kernels for 26%

profile of v6, /device:TPU:1, one launch (start us, length us, event | category | flops | bytes accessed | tf_op | source)
XLA Modules:
  0.0 162.1 jit_solution(2149563788623832025)
XLA Ops:
  0.0 7.7 %collective-permute-start = (bf16[64,1024]{1,0:T(8,128)(2,1)}, bf16[64,1024]{1,0:T(8,128)(2,1)S(1)}, u32[]{:S(2)}, u32[]{:S(2)}) collective-permute-start(bf16[64,1024]{1,0:T(8,128)(2,1)} %refs_3_.5), channel_id=1, source_target_pairs={{0,128},{8,136},{16,144},{24,152},{32,160},{40,168},{48,176},{56,1... | collective-permute-start | bytes 393224 | tf_op jit(solution)/shard_map/ppermute | solution.py:39
  7.7 1.3 collective-permute-start.1
  9.7 1.9 %pack.1.refs_4_.refs_8_ = bf16[2192,128]{1,0:T(8,128)(2,1)} custom-call(s32[1]{0:T(128)S(6)} %copy.9.length_ref, bf16[1,1024,128]{2,1,0:T(8,128)(2,1)} %k_ref.1, bf16[1,1024,128]{2,1,0:T(8,128)(2,1)} %v_ref.1, bf16[64,128]{1,0:T(8,128)(2,1)} %nk_ref.1, bf16[64,128]{1,0:T(8,128)(2,1)} %nv_ref.1), custom_call_target="tpu_custom_call" | custom-call | tf_op jit(solution)/shard_map/pack/pallas_call | solution.py:55
  11.6 1.2 collective-permute-start.6
  12.8 4.1 %collective-permute-start.4 = (bf16[2192,128]{1,0:T(8,128)(2,1)}, bf16[2192,128]{1,0:T(8,128)(2,1)S(1)}, u32[]{:S(2)}, u32[]{:S(2)}) collective-permute-start(bf16[2192,128]{1,0:T(8,128)(2,1)} %pack.1.refs_4_.refs_8_), channel_id=1, source_target_pairs={{0,224},{8,232},{16,240},{24,248},{32,0},{40,8},{48,16},{56,24},{6... | collective-permute-start | bytes 1683464 | tf_op jit(solution)/shard_map/ppermute | solution.py:39
  16.9 1.3 collective-permute-start.2
  18.2 0.7 reshape.12.refs_17_
  18.9 0.7 stack.60.refs_16_
  19.6 1.5 collective-permute-done.2.refs_0_
  21.1 0.6 copy-done.10
  21.7 0.8 copy-done.1
  22.5 8.7 %attention.3 = (f32[1,2048]{1,0:T(1,128)}, f32[144,2048]{1,0:T(8,128)}) custom-call(bf16[64,1024]{1,0:T(8,128)(2,1)} %copy-done.10, bf16[64,1024]{1,0:T(8,128)(2,1)} %copy-done.8, bf16[64,1024]{1,0:T(8,128)(2,1)} %copy-done.9, bf16[64,1024]{1,0:T(8,128)(2,1)} %refs_3_.5, bf16[2192,128]{1,0:T(8,128)(2,1)} %pack.1.refs_4_.refs_8_, bf16[2192,128]{1,0:T(8,128)(2,1)} %copy-done.1), custom_call_target="tpu_custom_call" | custom-call | flops 1 | bytes 1 | tf_op jit(solution)/shard_map/attention/pallas_call | solution.py:234
  31.3 0.4 collective-permute-done.5.refs_6_.refs_12_
  31.6 1.8 %collective-permute-start.7 = (bf16[2192,128]{1,0:T(8,128)(2,1)S(1)}, bf16[2192,128]{1,0:T(8,128)(2,1)S(1)}, u32[]{:S(2)}, u32[]{:S(2)}) collective-permute-start(bf16[2192,128]{1,0:T(8,128)(2,1)S(1)} %collective-permute-done.4.refs_4_.refs_10_), channel_id=1, source_target_pairs={{0,8},{8,0},{16,24},{24,16},{32,40},{40,32},{48,56},{56,48},{64,72... | collective-permute-start | bytes 1683464 | tf_op jit(solution)/shard_map/ppermute | solution.py:39
  33.5 0.1 collective-permute-start.8
  33.6 3.6 %collective-permute-start.3 = (bf16[2192,128]{1,0:T(8,128)(2,1)S(1)}, bf16[2192,128]{1,0:T(8,128)(2,1)S(1)}, u32[]{:S(2)}, u32[]{:S(2)}) collective-permute-start(bf16[2192,128]{1,0:T(8,128)(2,1)S(1)} %copy-done), channel_id=1, source_target_pairs={{0,192},{8,200},{16,208},{24,216},{32,96},{40,104},{48,112},{56,12... | collective-permute-start | bytes 1683464 | tf_op jit(solution)/shard_map/ppermute | solution.py:39
  37.2 0.8 copy-done.4
  38.0 0.8 copy-done.5
  38.8 16.0 %attention.4 = (f32[1,2048]{1,0:T(1,128)}, f32[144,2048]{1,0:T(8,128)}) custom-call(bf16[64,1024]{1,0:T(8,128)(2,1)} %copy-done.10, bf16[64,1024]{1,0:T(8,128)(2,1)} %copy-done.8, bf16[64,1024]{1,0:T(8,128)(2,1)} %copy-done.9, bf16[64,1024]{1,0:T(8,128)(2,1)} %refs_3_.5, bf16[2192,128]{1,0:T(8,128)(2,1)} %copy-done.2, bf16[2192,128]{1,0:T(8,128)(2,1)} %copy-done.4, ...), custom_call_target="tpu_custom_call" | custom-call | flops 1 | bytes 1 | tf_op jit(solution)/shard_map/attention/pallas_call | solution.py:234
  54.8 1.6 collective-permute-start.21
  56.4 1.0 collective-permute-start.9
  57.3 10.5 %collective-permute-done.21.refs_10_ = bf16[1024,256]{1,0:T(8,128)(2,1)S(1)} collective-permute-done((bf16[1024,256]{1,0:T(8,128)(2,1)S(1)}, bf16[1024,256]{1,0:T(8,128)(2,1)S(1)}, u32[]{:S(2)}, u32[]{:S(2)}) %collective-permute-start.21) | collective-permute-done | bytes 524320 | tf_op jit(solution)/shard_map/ppermute | solution.py:39
  67.9 1.5 collective-permute-start.22
  69.4 0.8 copy-done.7
  70.2 12.8 %attention.5 = (bf16[64,1152]{1,0:T(8,128)(2,1)}, bf16[64,1152]{1,0:T(8,128)(2,1)}, bf16[64,1152]{1,0:T(8,128)(2,1)}, bf16[64,1152]{1,0:T(8,128)(2,1)}) custom-call(bf16[64,1024]{1,0:T(8,128)(2,1)} %copy-done.10, bf16[64,1024]{1,0:T(8,128)(2,1)} %copy-done.8, bf16[64,1024]{1,0:T(8,128)(2,1)} %copy-done.9, bf16[64,1024]{1,0:T(8,128)(2,1)} %refs_3_.5, ...), custom_call_target="tpu_custom_call" | custom-call | flops 1 | bytes 1 | tf_op jit(solution)/shard_map/attention/pallas_call | solution.py:234
  83.0 0.1 collective-permute-start.10
  83.1 4.7 %collective-permute-start.11 = (bf16[64,1152]{1,0:T(8,128)(2,1)}, bf16[64,1152]{1,0:T(8,128)(2,1)S(1)}, u32[]{:S(2)}, u32[]{:S(2)}) collective-permute-start(bf16[64,1152]{1,0:T(8,128)(2,1)} %get-tuple-element.49), channel_id=1, source_target_pairs={{0,128},{8,136},{16,144},{24,152},{32,160},{40,168},{48,176},{56,1... | collective-permute-start | bytes 442376 | tf_op jit(solution)/shard_map/ppermute | solution.py:39
  87.8 1.8 %collective-permute-start.12 = (bf16[64,1152]{1,0:T(8,128)(2,1)}, bf16[64,1152]{1,0:T(8,128)(2,1)S(1)}, u32[]{:S(2)}, u32[]{:S(2)}) collective-permute-start(bf16[64,1152]{1,0:T(8,128)(2,1)} %get-tuple-element.50), channel_id=1, source_target_pairs={{0,16},{8,24},{16,0},{24,8},{32,48},{40,56},{48,32},{56,40},{64,80... | collective-permute-start | bytes 442376 | tf_op jit(solution)/shard_map/ppermute | solution.py:39
  89.6 10.3 %collective-permute-done.10.refs_0_ = bf16[64,1152]{1,0:T(8,128)(2,1)S(1)} collective-permute-done((bf16[64,1152]{1,0:T(8,128)(2,1)}, bf16[64,1152]{1,0:T(8,128)(2,1)S(1)}, u32[]{:S(2)}, u32[]{:S(2)}) %collective-permute-start.10) | collective-permute-done | bytes 147488 | tf_op jit(solution)/shard_map/ppermute | solution.py:39
  99.9 0.3 collective-permute-done.11.refs_1_
  100.2 0.4 copy-done.15
  100.5 0.3 copy-done.16
  100.9 2.3 %merge.1.refs_0_ = bf16[64,1024]{1,0:T(8,128)(2,1)} custom-call(bf16[64,1152]{1,0:T(8,128)(2,1)} %copy-done.15, bf16[64,1152]{1,0:T(8,128)(2,1)} %copy-done.16, bf16[64,1152]{1,0:T(8,128)(2,1)} %copy-done.17, bf16[64,1152]{1,0:T(8,128)(2,1)} %get-tuple-element.51.refs_3_), custom_call_target="tpu_custom_call" | custom-call | tf_op jit(solution)/shard_map/merge/pallas_call | solution.py:266
  103.2 1.5 collective-permute-start.18
  104.6 3.6 %collective-permute-start.14 = (bf16[64,1024]{1,0:T(8,128)(2,1)}, bf16[64,1024]{1,0:T(8,128)(2,1)S(1)}, u32[]{:S(2)}, u32[]{:S(2)}) collective-permute-start(bf16[64,1024]{1,0:T(8,128)(2,1)} %merge.1.refs_0_), channel_id=1, source_target_pairs={{0,192},{8,200},{16,208},{24,216},{32,224},{40,232},{48,240},{56,2... | collective-permute-start | bytes 393224 | tf_op jit(solution)/shard_map/ppermute | solution.py:39
  108.2 0.4 collective-permute-start.15
  108.6 4.1 %collective-permute-done.16.refs_6_ = bf16[64,1024]{1,0:T(8,128)(2,1)S(1)} collective-permute-done((bf16[64,1024]{1,0:T(8,128)(2,1)}, bf16[64,1024]{1,0:T(8,128)(2,1)S(1)}, u32[]{:S(2)}, u32[]{:S(2)}) %collective-permute-start.16) | collective-permute-done | bytes 131104 | tf_op jit(solution)/shard_map/ppermute | solution.py:39
  112.7 3.0 %collective-permute-done.18.refs_7_ = bf16[64,1024]{1,0:T(8,128)(2,1)S(1)} collective-permute-done((bf16[64,1024]{1,0:T(8,128)(2,1)}, bf16[64,1024]{1,0:T(8,128)(2,1)S(1)}, u32[]{:S(2)}, u32[]{:S(2)}) %collective-permute-start.18) | collective-permute-done | bytes 131104 | tf_op jit(solution)/shard_map/ppermute | solution.py:39
  115.7 0.8 collective-permute-start.19
  116.5 0.6 pad_add_fusion.place_ref
  117.1 0.5 collective-permute-done.15.refs_3_
  117.6 2.2 %collective-permute-done.17.refs_4_ = bf16[64,1024]{1,0:T(8,128)(2,1)S(1)} collective-permute-done((bf16[64,1024]{1,0:T(8,128)(2,1)S(1)}, bf16[64,1024]{1,0:T(8,128)(2,1)S(1)}, u32[]{:S(2)}, u32[]{:S(2)}) %collective-permute-start.17) | collective-permute-done | bytes 131104 | tf_op jit(solution)/shard_map/ppermute | solution.py:39
  119.8 3.1 %collective-permute-done.19.refs_5_ = bf16[64,1024]{1,0:T(8,128)(2,1)S(1)} collective-permute-done((bf16[64,1024]{1,0:T(8,128)(2,1)S(1)}, bf16[64,1024]{1,0:T(8,128)(2,1)S(1)}, u32[]{:S(2)}, u32[]{:S(2)}) %collective-permute-start.19) | collective-permute-done | bytes 131104 | tf_op jit(solution)/shard_map/ppermute | solution.py:39
  123.0 0.6 copy-done.24
  123.5 0.8 copy-done.14
  124.4 4.3 %product.1 = bf16[4,8,64,256]{3,2,1,0:T(8,128)(2,1)} custom-call(s32[2]{0:T(128)} %pad_add_fusion.place_ref, bf16[64,1024]{1,0:T(8,128)(2,1)} %merge.1.refs_0_, bf16[64,1024]{1,0:T(8,128)(2,1)} %copy-done.18, bf16[64,1024]{1,0:T(8,128)(2,1)} %copy-done.21, bf16[64,1024]{1,0:T(8,128)(2,1)} %copy-done.22, bf16[64,1024]{1,0:T(8,128)(2,1)} %copy-done.23, ...), custom_call_target="tpu_custom_call" | custom-call | tf_op jit(solution)/shard_map/product/pallas_call | solution.py:286
  128.6 32.7 %all_to_all.5 = bf16[32,64,256]{2,1,0:T(8,128)(2,1)S(1)} all-to-all(bf16[32,64,256]{2,1,0:T(8,128)(2,1)} %bitcast.17), channel_id=1, replica_groups={{0,1,2,3,4,5,6,7,8,9,10,11,12,13,14,15,16,17,18,19,20,21,22,23,24,25,26..., dimensions={0} | all-to-all | bytes 2097152 | tf_op jit(solution)/shard_map/all_to_all | solution.py:343
  161.3 0.8 bitcast_reduce_fusion
  (61 shorter events, 0.2 us)
Async XLA Ops:
  0.0 18.2 %copy-start.25 = (s32[2048]{0:T(1024)S(1)}, s32[2048]{0:T(1024)}, u32[]{:S(2)}) copy-start(s32[2048]{0:T(1024)} %param.14) | copy-start | bytes 24580
  0.0 12.8 %collective-permute-start = (bf16[64,1024]{1,0:T(8,128)(2,1)}, bf16[64,1024]{1,0:T(8,128)(2,1)S(1)}, u32[]{:S(2)}, u32[]{:S(2)}) collective-permute-start(bf16[64,1024]{1,0:T(8,128)(2,1)} %refs_3_.5), channel_id=1, source_target_pairs={{0,128},{8,136},{16,144},{24,152},{32,160},{40,168},{48,176},{56,1... | collective-permute-start | bytes 393224 | tf_op jit(solution)/shard_map/ppermute | solution.py:39
  7.7 5.1 %collective-permute-start.1 = (bf16[64,1024]{1,0:T(8,128)(2,1)}, bf16[64,1024]{1,0:T(8,128)(2,1)S(1)}, u32[]{:S(2)}, u32[]{:S(2)}) collective-permute-start(bf16[64,1024]{1,0:T(8,128)(2,1)} %refs_3_.5), channel_id=1, source_target_pairs={{0,16},{8,24},{16,0},{24,8},{32,48},{40,56},{48,32},{56,40},{64,80... | collective-permute-start | bytes 393224 | tf_op jit(solution)/shard_map/ppermute | solution.py:39
  11.6 22.0 %copy-start = (bf16[2192,128]{1,0:T(8,128)(2,1)S(1)}, bf16[2192,128]{1,0:T(8,128)(2,1)}, u32[]{:S(2)}) copy-start(bf16[2192,128]{1,0:T(8,128)(2,1)} %pack.1.refs_4_.refs_8_) | copy-start | bytes 1683460
  11.6 9.5 %collective-permute-start.6 = (bf16[2192,128]{1,0:T(8,128)(2,1)}, bf16[2192,128]{1,0:T(8,128)(2,1)S(1)}, u32[]{:S(2)}, u32[]{:S(2)}) collective-permute-start(bf16[2192,128]{1,0:T(8,128)(2,1)} %pack.1.refs_4_.refs_8_), channel_id=1, source_target_pairs={{0,8},{8,0},{16,24},{24,16},{32,40},{40,32},{48,56},{56,48},{64,72... | collective-permute-start | bytes 1683464 | tf_op jit(solution)/shard_map/ppermute | solution.py:39
  12.8 8.3 %copy-start.8 = (bf16[64,1024]{1,0:T(8,128)(2,1)}, bf16[64,1024]{1,0:T(8,128)(2,1)S(1)}, u32[]{:S(2)}) copy-start(bf16[64,1024]{1,0:T(8,128)(2,1)S(1)} %collective-permute-done.refs_1_) | copy-start | bytes 393220
  12.8 8.3 %copy-start.9 = (bf16[64,1024]{1,0:T(8,128)(2,1)}, bf16[64,1024]{1,0:T(8,128)(2,1)S(1)}, u32[]{:S(2)}) copy-start(bf16[64,1024]{1,0:T(8,128)(2,1)S(1)} %collective-permute-done.1.refs_2_) | copy-start | bytes 393220
  12.8 18.5 %collective-permute-start.4 = (bf16[2192,128]{1,0:T(8,128)(2,1)}, bf16[2192,128]{1,0:T(8,128)(2,1)S(1)}, u32[]{:S(2)}, u32[]{:S(2)}) collective-permute-start(bf16[2192,128]{1,0:T(8,128)(2,1)} %pack.1.refs_4_.refs_8_), channel_id=1, source_target_pairs={{0,224},{8,232},{16,240},{24,248},{32,0},{40,8},{48,16},{56,24},{6... | collective-permute-start | bytes 1683464 | tf_op jit(solution)/shard_map/ppermute | solution.py:39
  16.9 14.7 %collective-permute-start.5 = (bf16[2192,128]{1,0:T(8,128)(2,1)}, bf16[2192,128]{1,0:T(8,128)(2,1)S(1)}, u32[]{:S(2)}, u32[]{:S(2)}) collective-permute-start(bf16[2192,128]{1,0:T(8,128)(2,1)} %pack.1.refs_4_.refs_8_), channel_id=1, source_target_pairs={{0,32},{8,40},{16,48},{24,56},{32,64},{40,72},{48,80},{56,88},{64,... | collective-permute-start | bytes 1683464 | tf_op jit(solution)/shard_map/ppermute | solution.py:39
  16.9 4.1 %collective-permute-start.2 = (bf16[64,1024]{1,0:T(8,128)(2,1)S(1)}, bf16[64,1024]{1,0:T(8,128)(2,1)S(1)}, u32[]{:S(2)}, u32[]{:S(2)}) collective-permute-start(bf16[64,1024]{1,0:T(8,128)(2,1)S(1)} %collective-permute-done.refs_1_), channel_id=1, source_target_pairs={{0,16},{8,24},{16,0},{24,8},{32,48},{40,56},{48,32},{56,40},{64,80... | collective-permute-start | bytes 393224 | tf_op jit(solution)/shard_map/ppermute | solution.py:39
  21.1 0.7 copy-start.10
  21.7 0.8 copy-start.1
  31.3 5.9 %copy-start.2 = (bf16[2192,128]{1,0:T(8,128)(2,1)}, bf16[2192,128]{1,0:T(8,128)(2,1)S(1)}, u32[]{:S(2)}) copy-start(bf16[2192,128]{1,0:T(8,128)(2,1)S(1)} %collective-permute-done.4.refs_4_.refs_10_) | copy-start | bytes 1683460
  31.6 5.5 %copy-start.3 = (bf16[2192,128]{1,0:T(8,128)(2,1)}, bf16[2192,128]{1,0:T(8,128)(2,1)S(1)}, u32[]{:S(2)}) copy-start(bf16[2192,128]{1,0:T(8,128)(2,1)S(1)} %collective-permute-done.5.refs_6_.refs_12_) | copy-start | bytes 1683460
  31.6 23.1 %copy-start.11 = (bf16[1024,256]{1,0:T(8,128)(2,1)S(1)}, bf16[1024,256]{1,0:T(8,128)(2,1)}, u32[]{:S(2)}) copy-start(bf16[1024,256]{1,0:T(8,128)(2,1)} %refs_8_.1) | copy-start | bytes 1572868
  31.6 5.5 %collective-permute-start.7 = (bf16[2192,128]{1,0:T(8,128)(2,1)S(1)}, bf16[2192,128]{1,0:T(8,128)(2,1)S(1)}, u32[]{:S(2)}, u32[]{:S(2)}) collective-permute-start(bf16[2192,128]{1,0:T(8,128)(2,1)S(1)} %collective-permute-done.4.refs_4_.refs_10_), channel_id=1, source_target_pairs={{0,8},{8,0},{16,24},{24,16},{32,40},{40,32},{48,56},{56,48},{64,72... | collective-permute-start | bytes 1683464 | tf_op jit(solution)/shard_map/ppermute | solution.py:39
  33.5 3.7 %collective-permute-start.8 = (bf16[2192,128]{1,0:T(8,128)(2,1)S(1)}, bf16[2192,128]{1,0:T(8,128)(2,1)S(1)}, u32[]{:S(2)}, u32[]{:S(2)}) collective-permute-start(bf16[2192,128]{1,0:T(8,128)(2,1)S(1)} %collective-permute-done.5.refs_6_.refs_12_), channel_id=1, source_target_pairs={{0,8},{8,0},{16,24},{24,16},{32,40},{40,32},{48,56},{56,48},{64,72... | collective-permute-start | bytes 1683464 | tf_op jit(solution)/shard_map/ppermute | solution.py:39
  33.6 21.2 %collective-permute-start.3 = (bf16[2192,128]{1,0:T(8,128)(2,1)S(1)}, bf16[2192,128]{1,0:T(8,128)(2,1)S(1)}, u32[]{:S(2)}, u32[]{:S(2)}) collective-permute-start(bf16[2192,128]{1,0:T(8,128)(2,1)S(1)} %copy-done), channel_id=1, source_target_pairs={{0,192},{8,200},{16,208},{24,216},{32,96},{40,104},{48,112},{56,12... | collective-permute-start | bytes 1683464 | tf_op jit(solution)/shard_map/ppermute | solution.py:39
  37.1 0.8 copy-start.4
  38.0 0.8 copy-start.5
  54.8 14.6 %copy-start.6 = (bf16[2192,128]{1,0:T(8,128)(2,1)}, bf16[2192,128]{1,0:T(8,128)(2,1)S(1)}, u32[]{:S(2)}) copy-start(bf16[2192,128]{1,0:T(8,128)(2,1)S(1)} %collective-permute-done.3.refs_4_.refs_14_) | copy-start | bytes 1683460
  54.8 13.1 %collective-permute-start.21 = (bf16[1024,256]{1,0:T(8,128)(2,1)S(1)}, bf16[1024,256]{1,0:T(8,128)(2,1)S(1)}, u32[]{:S(2)}, u32[]{:S(2)}) collective-permute-start(bf16[1024,256]{1,0:T(8,128)(2,1)S(1)} %copy-done.11), channel_id=1, source_target_pairs={{0,16},{8,24},{16,0},{24,8},{32,48},{40,56},{48,32},{56,40},{64,80... | collective-permute-start | bytes 1572872 | tf_op jit(solution)/shard_map/ppermute | solution.py:39
  56.4 13.0 %collective-permute-start.9 = (bf16[2192,128]{1,0:T(8,128)(2,1)S(1)}, bf16[2192,128]{1,0:T(8,128)(2,1)S(1)}, u32[]{:S(2)}, u32[]{:S(2)}) collective-permute-start(bf16[2192,128]{1,0:T(8,128)(2,1)S(1)} %collective-permute-done.3.refs_4_.refs_14_), channel_id=1, source_target_pairs={{0,8},{8,0},{16,24},{24,16},{32,40},{40,32},{48,56},{56,48},{64,72... | collective-permute-start | bytes 1683464 | tf_op jit(solution)/shard_map/ppermute | solution.py:39
  57.3 47.3 %collective-permute-start.20 = (bf16[1024,256]{1,0:T(8,128)(2,1)S(1)}, bf16[1024,256]{1,0:T(8,128)(2,1)S(1)}, u32[]{:S(2)}, u32[]{:S(2)}) collective-permute-start(bf16[1024,256]{1,0:T(8,128)(2,1)S(1)} %copy-done.11), channel_id=1, source_target_pairs={{0,8},{8,0},{16,24},{24,16},{32,40},{40,32},{48,56},{56,48},{64,72... | collective-permute-start | bytes 1572872 | tf_op jit(solution)/shard_map/ppermute | solution.py:39
  67.9 15.1 %copy-start.12 = (bf16[1024,256]{1,0:T(8,128)(2,1)}, bf16[1024,256]{1,0:T(8,128)(2,1)S(1)}, u32[]{:S(2)}) copy-start(bf16[1024,256]{1,0:T(8,128)(2,1)S(1)} %collective-permute-done.21.refs_10_) | copy-start | bytes 1572868
  67.9 55.1 %collective-permute-start.22 = (bf16[1024,256]{1,0:T(8,128)(2,1)S(1)}, bf16[1024,256]{1,0:T(8,128)(2,1)S(1)}, u32[]{:S(2)}, u32[]{:S(2)}) collective-permute-start(bf16[1024,256]{1,0:T(8,128)(2,1)S(1)} %collective-permute-done.21.refs_10_), channel_id=1, source_target_pairs={{0,8},{8,0},{16,24},{24,16},{32,40},{40,32},{48,56},{56,48},{64,72... | collective-permute-start | bytes 1572872 | tf_op jit(solution)/shard_map/ppermute | solution.py:39
  69.4 0.8 copy-start.7
  83.0 16.9 %collective-permute-start.10 = (bf16[64,1152]{1,0:T(8,128)(2,1)}, bf16[64,1152]{1,0:T(8,128)(2,1)S(1)}, u32[]{:S(2)}, u32[]{:S(2)}) collective-permute-start(bf16[64,1152]{1,0:T(8,128)(2,1)} %get-tuple-element.48), channel_id=1, source_target_pairs={{0,144},{8,152},{16,128},{24,136},{32,176},{40,184},{48,160},{56,1... | collective-permute-start | bytes 442376 | tf_op jit(solution)/shard_map/ppermute | solution.py:39
  83.1 17.1 %collective-permute-start.11 = (bf16[64,1152]{1,0:T(8,128)(2,1)}, bf16[64,1152]{1,0:T(8,128)(2,1)S(1)}, u32[]{:S(2)}, u32[]{:S(2)}) collective-permute-start(bf16[64,1152]{1,0:T(8,128)(2,1)} %get-tuple-element.49), channel_id=1, source_target_pairs={{0,128},{8,136},{16,144},{24,152},{32,160},{40,168},{48,176},{56,1... | collective-permute-start | bytes 442376 | tf_op jit(solution)/shard_map/ppermute | solution.py:39
  87.8 12.4 %collective-permute-start.12 = (bf16[64,1152]{1,0:T(8,128)(2,1)}, bf16[64,1152]{1,0:T(8,128)(2,1)S(1)}, u32[]{:S(2)}, u32[]{:S(2)}) collective-permute-start(bf16[64,1152]{1,0:T(8,128)(2,1)} %get-tuple-element.50), channel_id=1, source_target_pairs={{0,16},{8,24},{16,0},{24,8},{32,48},{40,56},{48,32},{56,40},{64,80... | collective-permute-start | bytes 442376 | tf_op jit(solution)/shard_map/ppermute | solution.py:39
  99.9 0.7 copy-start.15
  100.2 0.7 copy-start.16
  100.2 0.7 copy-start.17
  103.2 5.1 %collective-permute-start.13 = (bf16[64,1024]{1,0:T(8,128)(2,1)}, bf16[64,1024]{1,0:T(8,128)(2,1)S(1)}, u32[]{:S(2)}, u32[]{:S(2)}) collective-permute-start(bf16[64,1024]{1,0:T(8,128)(2,1)} %merge.1.refs_0_), channel_id=1, source_target_pairs={{0,224},{8,232},{16,240},{24,248},{32,0},{40,8},{48,16},{56,24},{6... | collective-permute-start | bytes 393224 | tf_op jit(solution)/shard_map/ppermute | solution.py:39
  103.2 9.5 %collective-permute-start.16 = (bf16[64,1024]{1,0:T(8,128)(2,1)}, bf16[64,1024]{1,0:T(8,128)(2,1)S(1)}, u32[]{:S(2)}, u32[]{:S(2)}) collective-permute-start(bf16[64,1024]{1,0:T(8,128)(2,1)} %merge.1.refs_0_), channel_id=1, source_target_pairs={{0,64},{8,72},{16,80},{24,88},{32,96},{40,104},{48,112},{56,120},{... | collective-permute-start | bytes 393224 | tf_op jit(solution)/shard_map/ppermute | solution.py:39
  103.2 12.5 %collective-permute-start.18 = (bf16[64,1024]{1,0:T(8,128)(2,1)}, bf16[64,1024]{1,0:T(8,128)(2,1)S(1)}, u32[]{:S(2)}, u32[]{:S(2)}) collective-permute-start(bf16[64,1024]{1,0:T(8,128)(2,1)} %merge.1.refs_0_), channel_id=1, source_target_pairs={{0,32},{8,40},{16,48},{24,56},{32,64},{40,72},{48,80},{56,88},{64,... | collective-permute-start | bytes 393224 | tf_op jit(solution)/shard_map/ppermute | solution.py:39
  104.6 18.3 %copy-start.13 = (bf16[1024,256]{1,0:T(8,128)(2,1)}, bf16[1024,256]{1,0:T(8,128)(2,1)S(1)}, u32[]{:S(2)}) copy-start(bf16[1024,256]{1,0:T(8,128)(2,1)S(1)} %collective-permute-done.20.refs_9_) | copy-start | bytes 1572868
  104.6 12.5 %collective-permute-start.14 = (bf16[64,1024]{1,0:T(8,128)(2,1)}, bf16[64,1024]{1,0:T(8,128)(2,1)S(1)}, u32[]{:S(2)}, u32[]{:S(2)}) collective-permute-start(bf16[64,1024]{1,0:T(8,128)(2,1)} %merge.1.refs_0_), channel_id=1, source_target_pairs={{0,192},{8,200},{16,208},{24,216},{32,224},{40,232},{48,240},{56,2... | collective-permute-start | bytes 393224 | tf_op jit(solution)/shard_map/ppermute | solution.py:39
  108.2 14.7 %copy-start.18 = (bf16[64,1024]{1,0:T(8,128)(2,1)}, bf16[64,1024]{1,0:T(8,128)(2,1)S(1)}, u32[]{:S(2)}) copy-start(bf16[64,1024]{1,0:T(8,128)(2,1)S(1)} %collective-permute-done.13.refs_1_) | copy-start | bytes 393220
  108.2 9.3 %collective-permute-start.15 = (bf16[64,1024]{1,0:T(8,128)(2,1)S(1)}, bf16[64,1024]{1,0:T(8,128)(2,1)S(1)}, u32[]{:S(2)}, u32[]{:S(2)}) collective-permute-start(bf16[64,1024]{1,0:T(8,128)(2,1)S(1)} %collective-permute-done.13.refs_1_), channel_id=1, source_target_pairs={{0,192},{8,200},{16,208},{24,216},{32,224},{40,232},{48,240},{56,2... | collective-permute-start | bytes 393224 | tf_op jit(solution)/shard_map/ppermute | solution.py:39
  112.7 10.2 %copy-start.19 = (bf16[64,1024]{1,0:T(8,128)(2,1)}, bf16[64,1024]{1,0:T(8,128)(2,1)S(1)}, u32[]{:S(2)}) copy-start(bf16[64,1024]{1,0:T(8,128)(2,1)S(1)} %collective-permute-done.16.refs_6_) | copy-start | bytes 393220
  112.7 7.1 %collective-permute-start.17 = (bf16[64,1024]{1,0:T(8,128)(2,1)S(1)}, bf16[64,1024]{1,0:T(8,128)(2,1)S(1)}, u32[]{:S(2)}, u32[]{:S(2)}) collective-permute-start(bf16[64,1024]{1,0:T(8,128)(2,1)S(1)} %collective-permute-done.16.refs_6_), channel_id=1, source_target_pairs={{0,64},{8,72},{16,80},{24,88},{32,96},{40,104},{48,112},{56,120},{... | collective-permute-start | bytes 393224 | tf_op jit(solution)/shard_map/ppermute | solution.py:39
  115.7 7.2 %copy-start.20 = (bf16[64,1024]{1,0:T(8,128)(2,1)}, bf16[64,1024]{1,0:T(8,128)(2,1)S(1)}, u32[]{:S(2)}) copy-start(bf16[64,1024]{1,0:T(8,128)(2,1)S(1)} %collective-permute-done.18.refs_7_) | copy-start | bytes 393220
  115.7 7.2 %collective-permute-start.19 = (bf16[64,1024]{1,0:T(8,128)(2,1)S(1)}, bf16[64,1024]{1,0:T(8,128)(2,1)S(1)}, u32[]{:S(2)}, u32[]{:S(2)}) collective-permute-start(bf16[64,1024]{1,0:T(8,128)(2,1)S(1)} %collective-permute-done.18.refs_7_), channel_id=1, source_target_pairs={{0,64},{8,72},{16,80},{24,88},{32,96},{40,104},{48,112},{56,120},{... | collective-permute-start | bytes 393224 | tf_op jit(solution)/shard_map/ppermute | solution.py:39
  117.1 5.8 %copy-start.21 = (bf16[64,1024]{1,0:T(8,128)(2,1)}, bf16[64,1024]{1,0:T(8,128)(2,1)S(1)}, u32[]{:S(2)}) copy-start(bf16[64,1024]{1,0:T(8,128)(2,1)S(1)} %collective-permute-done.14.refs_2_) | copy-start | bytes 393220
  117.6 5.4 %copy-start.22 = (bf16[64,1024]{1,0:T(8,128)(2,1)}, bf16[64,1024]{1,0:T(8,128)(2,1)S(1)}, u32[]{:S(2)}) copy-start(bf16[64,1024]{1,0:T(8,128)(2,1)S(1)} %collective-permute-done.15.refs_3_) | copy-start | bytes 393220
  119.8 3.2 %copy-start.23 = (bf16[64,1024]{1,0:T(8,128)(2,1)}, bf16[64,1024]{1,0:T(8,128)(2,1)S(1)}, u32[]{:S(2)}) copy-start(bf16[64,1024]{1,0:T(8,128)(2,1)S(1)} %collective-permute-done.17.refs_4_) | copy-start | bytes 393220
  123.5 0.8 copy-start.14
  (1 other events, 0.6 us)

commit v7 on v6

--- a/solution.py
+++ b/solution.py
@@ -327,18 +327,22 @@
     state = attention(q_blocks, next_pairs, state)
     kv_two, weight, *state = lax.optimization_barrier((kv_two, out_weight, *state))
     weight_y = over_y(weight)
-    weights = [out_weight, over_c(weight), weight_y, over_c(weight_y)]
+    weight_c = over_c(weight)
     last_pair = (kv_two, over_c(kv_two))
     new = (*own_pair, *next_pairs, *last_pair)
     cross, far, side, mine = attention(q_blocks, last_pair, state, new, ids, span)
+    weight_y, cross, far, side, mine = lax.optimization_barrier(
+        (weight_y, cross, far, side, mine)
+    )
+    weights = [out_weight, weight_c, weight_y, over_c(weight_y)]
     cross = seq_permute(cross, lambda z, y, c: (z + 4, 1 - y, c))
     attended = merge((cross, shift(far, 4), over_y(side), mine))
 
     blocks = [attended] + [None] * (Z - 1)
-    blocks[1], blocks[7] = shift(attended, -1), shift(attended, 1)
-    blocks[2], blocks[6] = shift(attended, -2), shift(attended, 2)
-    blocks[3], blocks[5] = shift(blocks[1], -2), shift(blocks[7], 2)
-    blocks[4] = shift(blocks[6], 2)
+    for k in (1, 2, 3):
+        blocks[k] = shift(blocks[k - 1], -1)
+        blocks[Z - k] = shift(blocks[(Z - k + 1) % Z], 1)
+    blocks[4] = shift(blocks[3], -1)
     shares = product(jnp.stack([z, yc]), blocks, weights).reshape(YC * Z, TOK, 256)
     shares = lax.all_to_all(
         shares, ("seq", "head"), 0, 0, axis_index_groups=PLANES, tiled=True

time: 162 us -> 147 us (0.907)
  waiting for transfers between devices: 35.8 us -> 22.9 us
  blocking collectives: 32.7 us -> 28.4 us
  starting transfers between devices: 38.1 us -> 41.6 us
  Pallas kernels: 45.9 us -> 42.7 us
    ppermute x23, waiting for transfers between devices: 35.8 us -> 22.9 us  [seq_permute(): return lax.ppermute(value, 'seq', pairs)]
    all_to_all x1, blocking collectives: 32.7 us -> 28.4 us  [body(): lax.all_to_all(shares, ('seq', 'head'), 0, 0, axis_index_groups=PLANES, t...]
    ppermute x23, starting transfers between devices: 38.1 us -> 41.6 us  [seq_permute(): return lax.ppermute(value, 'seq', pairs)]
    pallas_call x3, Pallas kernels: 37.5 us -> 34.3 us  [attention(): pl.pallas_call(functools.partial(attention_kernel, len(shards), first, la...]
  transfers between devices with their start and end apart: 23 -> 23, of which waited for: 10 -> 9; matrix products, arithmetic and copies ran while one was open for 1% -> 1% of each run, Pallas kernels for 26% -> 26%
where the time goes in v7:
time: 147 us; the launch traced here: 146 us
  Pallas kernels  42.7 us (29%)
  starting transfers between devices  41.6 us (28%)
  blocking collectives  28.4 us (19%)
  waiting for transfers between devices  22.9 us (16%)
  local copies, waits for them, and re-layouts  7.76 us (5%)
    ppermute x23, starting transfers between devices, seq_permute(): return lax.ppermute(value, 'seq', pairs)  41.6 us
    pallas_call x3, Pallas kernels, attention(): pl.pallas_call(functools.partial(attention_kernel, len(shards), first, la...  34.3 us
    all_to_all x1, blocking collectives, body(): lax.all_to_all(shares, ('seq', 'head'), 0, 0, axis_index_groups=PLANES, t...  28.4 us
    ppermute x23, waiting for transfers between devices, seq_permute(): return lax.ppermute(value, 'seq', pairs)  22.9 us
    unnamed x52, local copies, waits for them, and re-layouts  6.46 us
    pallas_call x1, Pallas kernels, product(): pl.pallas_call(product_kernel, out_shape=jax.ShapeDtypeStruct((YC, Z, TOK...  4.27 us
  transfers between devices with their start and end apart: 23, of which 9 were waited for; matrix products, arithmetic and copies ran while one was open for 1% of the time, Pallas kernels for 26%

profile of v7, /device:TPU:1, one launch (start us, length us, event | category | flops | bytes accessed | tf_op | source)
XLA Modules:
  0.0 145.7 jit_solution(11610075651464508900)
XLA Ops:
  0.0 7.7 %collective-permute-start = (bf16[64,1024]{1,0:T(8,128)(2,1)}, bf16[64,1024]{1,0:T(8,128)(2,1)S(1)}, u32[]{:S(2)}, u32[]{:S(2)}) collective-permute-start(bf16[64,1024]{1,0:T(8,128)(2,1)} %refs_3_.5), channel_id=1, source_target_pairs={{0,128},{8,136},{16,144},{24,152},{32,160},{40,168},{48,176},{56,1... | collective-permute-start | bytes 393224 | tf_op jit(solution)/shard_map/ppermute | solution.py:39
  7.7 1.3 collective-permute-start.1
  9.7 1.9 %pack.1.refs_4_.refs_8_ = bf16[2192,128]{1,0:T(8,128)(2,1)} custom-call(s32[1]{0:T(128)S(6)} %copy.9.length_ref, bf16[1,1024,128]{2,1,0:T(8,128)(2,1)} %k_ref.1, bf16[1,1024,128]{2,1,0:T(8,128)(2,1)} %v_ref.1, bf16[64,128]{1,0:T(8,128)(2,1)} %nk_ref.1, bf16[64,128]{1,0:T(8,128)(2,1)} %nv_ref.1), custom_call_target="tpu_custom_call" | custom-call | tf_op jit(solution)/shard_map/pack/pallas_call | solution.py:55
  11.6 1.2 collective-permute-start.6
  12.8 0.0 collective-permute-done.refs_1_
  12.8 4.1 %collective-permute-start.4 = (bf16[2192,128]{1,0:T(8,128)(2,1)}, bf16[2192,128]{1,0:T(8,128)(2,1)S(1)}, u32[]{:S(2)}, u32[]{:S(2)}) collective-permute-start(bf16[2192,128]{1,0:T(8,128)(2,1)} %pack.1.refs_4_.refs_8_), channel_id=1, source_target_pairs={{0,224},{8,232},{16,240},{24,248},{32,0},{40,8},{48,16},{56,24},{6... | collective-permute-start | bytes 1683464 | tf_op jit(solution)/shard_map/ppermute | solution.py:39
  16.9 1.3 collective-permute-start.2
  18.2 0.7 reshape.12.refs_17_
  18.9 0.6 stack.60.refs_16_
  19.5 1.5 %collective-permute-done.2.refs_0_ = bf16[64,1024]{1,0:T(8,128)(2,1)S(1)} collective-permute-done((bf16[64,1024]{1,0:T(8,128)(2,1)S(1)}, bf16[64,1024]{1,0:T(8,128)(2,1)S(1)}, u32[]{:S(2)}, u32[]{:S(2)}) %collective-permute-start.2) | collective-permute-done | bytes 131104 | tf_op jit(solution)/shard_map/ppermute | solution.py:39
  21.1 0.6 copy-done.10
  21.7 0.8 copy-done.1
  22.5 8.7 %attention.3 = (f32[1,2048]{1,0:T(1,128)}, f32[144,2048]{1,0:T(8,128)}) custom-call(bf16[64,1024]{1,0:T(8,128)(2,1)} %copy-done.10, bf16[64,1024]{1,0:T(8,128)(2,1)} %copy-done.8, bf16[64,1024]{1,0:T(8,128)(2,1)} %copy-done.9, bf16[64,1024]{1,0:T(8,128)(2,1)} %refs_3_.5, bf16[2192,128]{1,0:T(8,128)(2,1)} %pack.1.refs_4_.refs_8_, bf16[2192,128]{1,0:T(8,128)(2,1)} %copy-done.1), custom_call_target="tpu_custom_call" | custom-call | flops 1 | bytes 1 | tf_op jit(solution)/shard_map/attention/pallas_call | solution.py:234
  31.3 0.4 collective-permute-done.5.refs_6_.refs_12_
  31.6 1.8 %collective-permute-start.7 = (bf16[2192,128]{1,0:T(8,128)(2,1)S(1)}, bf16[2192,128]{1,0:T(8,128)(2,1)S(1)}, u32[]{:S(2)}, u32[]{:S(2)}) collective-permute-start(bf16[2192,128]{1,0:T(8,128)(2,1)S(1)} %collective-permute-done.4.refs_4_.refs_10_), channel_id=1, source_target_pairs={{0,8},{8,0},{16,24},{24,16},{32,40},{40,32},{48,56},{56,48},{64,72... | collective-permute-start | bytes 1683464 | tf_op jit(solution)/shard_map/ppermute | solution.py:39
  33.5 0.1 collective-permute-start.8
  33.6 5.1 %collective-permute-start.3 = (bf16[2192,128]{1,0:T(8,128)(2,1)S(1)}, bf16[2192,128]{1,0:T(8,128)(2,1)S(1)}, u32[]{:S(2)}, u32[]{:S(2)}) collective-permute-start(bf16[2192,128]{1,0:T(8,128)(2,1)S(1)} %copy-done), channel_id=1, source_target_pairs={{0,192},{8,200},{16,208},{24,216},{32,96},{40,104},{48,112},{56,12... | collective-permute-start | bytes 1683464 | tf_op jit(solution)/shard_map/ppermute | solution.py:39
  38.7 0.8 copy-done.4
  39.5 0.8 copy-done.5
  40.4 14.4 %attention.4 = (f32[1,2048]{1,0:T(1,128)}, f32[144,2048]{1,0:T(8,128)}) custom-call(bf16[64,1024]{1,0:T(8,128)(2,1)} %copy-done.10, bf16[64,1024]{1,0:T(8,128)(2,1)} %copy-done.8, bf16[64,1024]{1,0:T(8,128)(2,1)} %copy-done.9, bf16[64,1024]{1,0:T(8,128)(2,1)} %refs_3_.5, bf16[2192,128]{1,0:T(8,128)(2,1)} %copy-done.2, bf16[2192,128]{1,0:T(8,128)(2,1)} %copy-done.4, ...), custom_call_target="tpu_custom_call" | custom-call | flops 1 | bytes 1 | tf_op jit(solution)/shard_map/attention/pallas_call | solution.py:234
  54.8 1.0 collective-permute-start.10
  55.8 1.6 %collective-permute-done.10.refs_5_.refs_15_ = bf16[2192,128]{1,0:T(8,128)(2,1)S(1)} collective-permute-done((bf16[2192,128]{1,0:T(8,128)(2,1)S(1)}, bf16[2192,128]{1,0:T(8,128)(2,1)S(1)}, u32[]{:S(2)}, u32[]{:S(2)}) %collective-permute-start.10) | collective-permute-done | bytes 561184 | tf_op jit(solution)/shard_map/ppermute | solution.py:39
  57.4 0.8 copy-done.7
  58.2 11.1 %attention.5 = (bf16[64,1152]{1,0:T(8,128)(2,1)}, bf16[64,1152]{1,0:T(8,128)(2,1)}, bf16[64,1152]{1,0:T(8,128)(2,1)}, bf16[64,1152]{1,0:T(8,128)(2,1)}) custom-call(bf16[64,1024]{1,0:T(8,128)(2,1)} %copy-done.10, bf16[64,1024]{1,0:T(8,128)(2,1)} %copy-done.8, bf16[64,1024]{1,0:T(8,128)(2,1)} %copy-done.9, bf16[64,1024]{1,0:T(8,128)(2,1)} %refs_3_.5, ...), custom_call_target="tpu_custom_call" | custom-call | flops 1 | bytes 1 | tf_op jit(solution)/shard_map/attention/pallas_call | solution.py:234
  69.3 2.8 %collective-permute-start.11 = (bf16[64,1152]{1,0:T(8,128)(2,1)}, bf16[64,1152]{1,0:T(8,128)(2,1)S(1)}, u32[]{:S(2)}, u32[]{:S(2)}) collective-permute-start(bf16[64,1152]{1,0:T(8,128)(2,1)} %get-tuple-element.58), channel_id=1, source_target_pairs={{0,144},{8,152},{16,128},{24,136},{32,176},{40,184},{48,160},{56,1... | collective-permute-start | bytes 442376 | tf_op jit(solution)/shard_map/ppermute | solution.py:39
  72.1 4.0 %collective-permute-start.12 = (bf16[64,1152]{1,0:T(8,128)(2,1)}, bf16[64,1152]{1,0:T(8,128)(2,1)S(1)}, u32[]{:S(2)}, u32[]{:S(2)}) collective-permute-start(bf16[64,1152]{1,0:T(8,128)(2,1)} %get-tuple-element.59), channel_id=1, source_target_pairs={{0,128},{8,136},{16,144},{24,152},{32,160},{40,168},{48,176},{56,1... | collective-permute-start | bytes 442376 | tf_op jit(solution)/shard_map/ppermute | solution.py:39
  76.0 1.5 %collective-permute-start.21 = (bf16[1024,256]{1,0:T(8,128)(2,1)S(1)}, bf16[1024,256]{1,0:T(8,128)(2,1)S(1)}, u32[]{:S(2)}, u32[]{:S(2)}) collective-permute-start(bf16[1024,256]{1,0:T(8,128)(2,1)S(1)} %copy-done.11), channel_id=1, source_target_pairs={{0,8},{8,0},{16,24},{24,16},{32,40},{40,32},{48,56},{56,48},{64,72... | collective-permute-start | bytes 1572872 | tf_op jit(solution)/shard_map/ppermute | solution.py:39
  77.5 5.6 %collective-permute-done.11.refs_0_ = bf16[64,1152]{1,0:T(8,128)(2,1)S(1)} collective-permute-done((bf16[64,1152]{1,0:T(8,128)(2,1)}, bf16[64,1152]{1,0:T(8,128)(2,1)S(1)}, u32[]{:S(2)}, u32[]{:S(2)}) %collective-permute-start.11) | collective-permute-done | bytes 147488 | tf_op jit(solution)/shard_map/ppermute | solution.py:39
  83.2 5.9 %collective-permute-done.12.refs_1_ = bf16[64,1152]{1,0:T(8,128)(2,1)S(1)} collective-permute-done((bf16[64,1152]{1,0:T(8,128)(2,1)}, bf16[64,1152]{1,0:T(8,128)(2,1)S(1)}, u32[]{:S(2)}, u32[]{:S(2)}) %collective-permute-start.12) | collective-permute-done | bytes 147488 | tf_op jit(solution)/shard_map/ppermute | solution.py:39
  89.1 0.6 copy-done.16
  89.7 0.7 copy-done.17
  90.4 2.3 %merge.1.refs_0_ = bf16[64,1024]{1,0:T(8,128)(2,1)} custom-call(bf16[64,1152]{1,0:T(8,128)(2,1)} %copy-done.15, bf16[64,1152]{1,0:T(8,128)(2,1)} %copy-done.16, bf16[64,1152]{1,0:T(8,128)(2,1)} %copy-done.17, bf16[64,1152]{1,0:T(8,128)(2,1)} %get-tuple-element.61.refs_3_), custom_call_target="tpu_custom_call" | custom-call | tf_op jit(solution)/shard_map/merge/pallas_call | solution.py:266
  92.6 1.4 collective-permute-start.22
  94.0 1.7 %collective-permute-start.18 = (bf16[64,1024]{1,0:T(8,128)(2,1)}, bf16[64,1024]{1,0:T(8,128)(2,1)S(1)}, u32[]{:S(2)}, u32[]{:S(2)}) collective-permute-start(bf16[64,1024]{1,0:T(8,128)(2,1)} %merge.1.refs_0_), channel_id=1, source_target_pairs={{0,32},{8,40},{16,48},{24,56},{32,64},{40,72},{48,80},{56,88},{64,... | collective-permute-start | bytes 393224 | tf_op jit(solution)/shard_map/ppermute | solution.py:39
  95.8 0.9 collective-permute-done.14.refs_1_
  96.7 1.2 collective-permute-start.15
  97.9 2.6 %collective-permute-done.18.refs_7_ = bf16[64,1024]{1,0:T(8,128)(2,1)S(1)} collective-permute-done((bf16[64,1024]{1,0:T(8,128)(2,1)}, bf16[64,1024]{1,0:T(8,128)(2,1)S(1)}, u32[]{:S(2)}, u32[]{:S(2)}) %collective-permute-start.18) | collective-permute-done | bytes 131104 | tf_op jit(solution)/shard_map/ppermute | solution.py:39
  100.5 0.6 collective-permute-start.19
  101.1 2.1 %collective-permute-start.16 = (bf16[64,1024]{1,0:T(8,128)(2,1)S(1)}, bf16[64,1024]{1,0:T(8,128)(2,1)S(1)}, u32[]{:S(2)}, u32[]{:S(2)}) collective-permute-start(bf16[64,1024]{1,0:T(8,128)(2,1)S(1)} %collective-permute-done.15.refs_2_), channel_id=1, source_target_pairs={{0,224},{8,232},{16,240},{24,248},{32,0},{40,8},{48,16},{56,24},{6... | collective-permute-start | bytes 393224 | tf_op jit(solution)/shard_map/ppermute | solution.py:39
  103.2 2.7 %collective-permute-done.19.refs_6_ = bf16[64,1024]{1,0:T(8,128)(2,1)S(1)} collective-permute-done((bf16[64,1024]{1,0:T(8,128)(2,1)S(1)}, bf16[64,1024]{1,0:T(8,128)(2,1)S(1)}, u32[]{:S(2)}, u32[]{:S(2)}) %collective-permute-start.19) | collective-permute-done | bytes 131104 | tf_op jit(solution)/shard_map/ppermute | solution.py:39
  105.9 2.7 %collective-permute-start.17 = (bf16[64,1024]{1,0:T(8,128)(2,1)S(1)}, bf16[64,1024]{1,0:T(8,128)(2,1)S(1)}, u32[]{:S(2)}, u32[]{:S(2)}) collective-permute-start(bf16[64,1024]{1,0:T(8,128)(2,1)S(1)} %collective-permute-done.16.refs_3_), channel_id=1, source_target_pairs={{0,224},{8,232},{16,240},{24,248},{32,0},{40,8},{48,16},{56,24},{6... | collective-permute-start | bytes 393224 | tf_op jit(solution)/shard_map/ppermute | solution.py:39
  108.6 0.6 pad_add_fusion.place_ref
  109.3 1.7 %collective-permute-done.20.refs_5_ = bf16[64,1024]{1,0:T(8,128)(2,1)S(1)} collective-permute-done((bf16[64,1024]{1,0:T(8,128)(2,1)S(1)}, bf16[64,1024]{1,0:T(8,128)(2,1)S(1)}, u32[]{:S(2)}, u32[]{:S(2)}) %collective-permute-start.20) | collective-permute-done | bytes 131104 | tf_op jit(solution)/shard_map/ppermute | solution.py:39
  111.0 0.6 copy-done.23
  111.6 0.6 copy-done.24
  112.2 4.3 %product.1 = bf16[4,8,64,256]{3,2,1,0:T(8,128)(2,1)} custom-call(s32[2]{0:T(128)} %pad_add_fusion.place_ref, bf16[64,1024]{1,0:T(8,128)(2,1)} %merge.1.refs_0_, bf16[64,1024]{1,0:T(8,128)(2,1)} %copy-done.18, bf16[64,1024]{1,0:T(8,128)(2,1)} %copy-done.20, bf16[64,1024]{1,0:T(8,128)(2,1)} %copy-done.22, bf16[64,1024]{1,0:T(8,128)(2,1)} %copy-done.24, ...), custom_call_target="tpu_custom_call" | custom-call | tf_op jit(solution)/shard_map/product/pallas_call | solution.py:286
  116.5 28.4 %all_to_all.5 = bf16[32,64,256]{2,1,0:T(8,128)(2,1)S(1)} all-to-all(bf16[32,64,256]{2,1,0:T(8,128)(2,1)} %bitcast.17), channel_id=1, replica_groups={{0,1,2,3,4,5,6,7,8,9,10,11,12,13,14,15,16,17,18,19,20,21,22,23,24,25,26..., dimensions={0} | all-to-all | bytes 2097152 | tf_op jit(solution)/shard_map/all_to_all | solution.py:347
  144.9 0.8 bitcast_reduce_fusion
  (61 shorter events, 0.1 us)
Async XLA Ops:
  0.0 18.2 %copy-start.25 = (s32[2048]{0:T(1024)S(1)}, s32[2048]{0:T(1024)}, u32[]{:S(2)}) copy-start(s32[2048]{0:T(1024)} %param.14) | copy-start | bytes 24580
  0.0 12.8 %collective-permute-start = (bf16[64,1024]{1,0:T(8,128)(2,1)}, bf16[64,1024]{1,0:T(8,128)(2,1)S(1)}, u32[]{:S(2)}, u32[]{:S(2)}) collective-permute-start(bf16[64,1024]{1,0:T(8,128)(2,1)} %refs_3_.5), channel_id=1, source_target_pairs={{0,128},{8,136},{16,144},{24,152},{32,160},{40,168},{48,176},{56,1... | collective-permute-start | bytes 393224 | tf_op jit(solution)/shard_map/ppermute | solution.py:39
  7.7 5.1 %collective-permute-start.1 = (bf16[64,1024]{1,0:T(8,128)(2,1)}, bf16[64,1024]{1,0:T(8,128)(2,1)S(1)}, u32[]{:S(2)}, u32[]{:S(2)}) collective-permute-start(bf16[64,1024]{1,0:T(8,128)(2,1)} %refs_3_.5), channel_id=1, source_target_pairs={{0,16},{8,24},{16,0},{24,8},{32,48},{40,56},{48,32},{56,40},{64,80... | collective-permute-start | bytes 393224 | tf_op jit(solution)/shard_map/ppermute | solution.py:39
  11.6 22.0 %copy-start = (bf16[2192,128]{1,0:T(8,128)(2,1)S(1)}, bf16[2192,128]{1,0:T(8,128)(2,1)}, u32[]{:S(2)}) copy-start(bf16[2192,128]{1,0:T(8,128)(2,1)} %pack.1.refs_4_.refs_8_) | copy-start | bytes 1683460
  11.6 9.5 %collective-permute-start.6 = (bf16[2192,128]{1,0:T(8,128)(2,1)}, bf16[2192,128]{1,0:T(8,128)(2,1)S(1)}, u32[]{:S(2)}, u32[]{:S(2)}) collective-permute-start(bf16[2192,128]{1,0:T(8,128)(2,1)} %pack.1.refs_4_.refs_8_), channel_id=1, source_target_pairs={{0,8},{8,0},{16,24},{24,16},{32,40},{40,32},{48,56},{56,48},{64,72... | collective-permute-start | bytes 1683464 | tf_op jit(solution)/shard_map/ppermute | solution.py:39
  12.8 8.3 %copy-start.8 = (bf16[64,1024]{1,0:T(8,128)(2,1)}, bf16[64,1024]{1,0:T(8,128)(2,1)S(1)}, u32[]{:S(2)}) copy-start(bf16[64,1024]{1,0:T(8,128)(2,1)S(1)} %collective-permute-done.refs_1_) | copy-start | bytes 393220
  12.8 8.3 %copy-start.9 = (bf16[64,1024]{1,0:T(8,128)(2,1)}, bf16[64,1024]{1,0:T(8,128)(2,1)S(1)}, u32[]{:S(2)}) copy-start(bf16[64,1024]{1,0:T(8,128)(2,1)S(1)} %collective-permute-done.1.refs_2_) | copy-start | bytes 393220
  12.8 18.5 %collective-permute-start.4 = (bf16[2192,128]{1,0:T(8,128)(2,1)}, bf16[2192,128]{1,0:T(8,128)(2,1)S(1)}, u32[]{:S(2)}, u32[]{:S(2)}) collective-permute-start(bf16[2192,128]{1,0:T(8,128)(2,1)} %pack.1.refs_4_.refs_8_), channel_id=1, source_target_pairs={{0,224},{8,232},{16,240},{24,248},{32,0},{40,8},{48,16},{56,24},{6... | collective-permute-start | bytes 1683464 | tf_op jit(solution)/shard_map/ppermute | solution.py:39
  16.9 14.7 %collective-permute-start.5 = (bf16[2192,128]{1,0:T(8,128)(2,1)}, bf16[2192,128]{1,0:T(8,128)(2,1)S(1)}, u32[]{:S(2)}, u32[]{:S(2)}) collective-permute-start(bf16[2192,128]{1,0:T(8,128)(2,1)} %pack.1.refs_4_.refs_8_), channel_id=1, source_target_pairs={{0,32},{8,40},{16,48},{24,56},{32,64},{40,72},{48,80},{56,88},{64,... | collective-permute-start | bytes 1683464 | tf_op jit(solution)/shard_map/ppermute | solution.py:39
  16.9 4.1 %collective-permute-start.2 = (bf16[64,1024]{1,0:T(8,128)(2,1)S(1)}, bf16[64,1024]{1,0:T(8,128)(2,1)S(1)}, u32[]{:S(2)}, u32[]{:S(2)}) collective-permute-start(bf16[64,1024]{1,0:T(8,128)(2,1)S(1)} %collective-permute-done.refs_1_), channel_id=1, source_target_pairs={{0,16},{8,24},{16,0},{24,8},{32,48},{40,56},{48,32},{56,40},{64,80... | collective-permute-start | bytes 393224 | tf_op jit(solution)/shard_map/ppermute | solution.py:39
  21.1 0.7 copy-start.10
  21.7 0.8 copy-start.1
  31.3 7.5 %copy-start.2 = (bf16[2192,128]{1,0:T(8,128)(2,1)}, bf16[2192,128]{1,0:T(8,128)(2,1)S(1)}, u32[]{:S(2)}) copy-start(bf16[2192,128]{1,0:T(8,128)(2,1)S(1)} %collective-permute-done.4.refs_4_.refs_10_) | copy-start | bytes 1683460
  31.6 7.1 %copy-start.3 = (bf16[2192,128]{1,0:T(8,128)(2,1)}, bf16[2192,128]{1,0:T(8,128)(2,1)S(1)}, u32[]{:S(2)}) copy-start(bf16[2192,128]{1,0:T(8,128)(2,1)S(1)} %collective-permute-done.5.refs_6_.refs_12_) | copy-start | bytes 1683460
  31.6 24.1 %copy-start.11 = (bf16[1024,256]{1,0:T(8,128)(2,1)S(1)}, bf16[1024,256]{1,0:T(8,128)(2,1)}, u32[]{:S(2)}) copy-start(bf16[1024,256]{1,0:T(8,128)(2,1)} %refs_8_.1) | copy-start | bytes 1572868
  31.6 7.1 %collective-permute-start.7 = (bf16[2192,128]{1,0:T(8,128)(2,1)S(1)}, bf16[2192,128]{1,0:T(8,128)(2,1)S(1)}, u32[]{:S(2)}, u32[]{:S(2)}) collective-permute-start(bf16[2192,128]{1,0:T(8,128)(2,1)S(1)} %collective-permute-done.4.refs_4_.refs_10_), channel_id=1, source_target_pairs={{0,8},{8,0},{16,24},{24,16},{32,40},{40,32},{48,56},{56,48},{64,72... | collective-permute-start | bytes 1683464 | tf_op jit(solution)/shard_map/ppermute | solution.py:39
  33.5 5.2 %collective-permute-start.8 = (bf16[2192,128]{1,0:T(8,128)(2,1)S(1)}, bf16[2192,128]{1,0:T(8,128)(2,1)S(1)}, u32[]{:S(2)}, u32[]{:S(2)}) collective-permute-start(bf16[2192,128]{1,0:T(8,128)(2,1)S(1)} %collective-permute-done.5.refs_6_.refs_12_), channel_id=1, source_target_pairs={{0,8},{8,0},{16,24},{24,16},{32,40},{40,32},{48,56},{56,48},{64,72... | collective-permute-start | bytes 1683464 | tf_op jit(solution)/shard_map/ppermute | solution.py:39
  33.6 21.2 %collective-permute-start.3 = (bf16[2192,128]{1,0:T(8,128)(2,1)S(1)}, bf16[2192,128]{1,0:T(8,128)(2,1)S(1)}, u32[]{:S(2)}, u32[]{:S(2)}) collective-permute-start(bf16[2192,128]{1,0:T(8,128)(2,1)S(1)} %copy-done), channel_id=1, source_target_pairs={{0,192},{8,200},{16,208},{24,216},{32,96},{40,104},{48,112},{56,12... | collective-permute-start | bytes 1683464 | tf_op jit(solution)/shard_map/ppermute | solution.py:39
  38.7 0.8 copy-start.4
  39.5 0.8 copy-start.5
  54.8 2.6 %copy-start.6 = (bf16[2192,128]{1,0:T(8,128)(2,1)}, bf16[2192,128]{1,0:T(8,128)(2,1)S(1)}, u32[]{:S(2)}) copy-start(bf16[2192,128]{1,0:T(8,128)(2,1)S(1)} %collective-permute-done.3.refs_4_.refs_14_) | copy-start | bytes 1683460
  54.8 2.5 %collective-permute-start.10 = (bf16[2192,128]{1,0:T(8,128)(2,1)S(1)}, bf16[2192,128]{1,0:T(8,128)(2,1)S(1)}, u32[]{:S(2)}, u32[]{:S(2)}) collective-permute-start(bf16[2192,128]{1,0:T(8,128)(2,1)S(1)} %collective-permute-done.3.refs_4_.refs_14_), channel_id=1, source_target_pairs={{0,8},{8,0},{16,24},{24,16},{32,40},{40,32},{48,56},{56,48},{64,72... | collective-permute-start | bytes 1683464 | tf_op jit(solution)/shard_map/ppermute | solution.py:39
  55.8 13.5 %collective-permute-start.9 = (bf16[1024,256]{1,0:T(8,128)(2,1)S(1)}, bf16[1024,256]{1,0:T(8,128)(2,1)S(1)}, u32[]{:S(2)}, u32[]{:S(2)}) collective-permute-start(bf16[1024,256]{1,0:T(8,128)(2,1)S(1)} %copy-done.11), channel_id=1, source_target_pairs={{0,16},{8,24},{16,0},{24,8},{32,48},{40,56},{48,32},{56,40},{64,80... | collective-permute-start | bytes 1572872 | tf_op jit(solution)/shard_map/ppermute | solution.py:39
  57.4 0.8 copy-start.7
  69.3 41.6 %copy-start.12 = (bf16[1024,256]{1,0:T(8,128)(2,1)}, bf16[1024,256]{1,0:T(8,128)(2,1)S(1)}, u32[]{:S(2)}) copy-start(bf16[1024,256]{1,0:T(8,128)(2,1)S(1)} %collective-permute-done.9.refs_10_) | copy-start | bytes 1572868
  69.3 13.8 %collective-permute-start.11 = (bf16[64,1152]{1,0:T(8,128)(2,1)}, bf16[64,1152]{1,0:T(8,128)(2,1)S(1)}, u32[]{:S(2)}, u32[]{:S(2)}) collective-permute-start(bf16[64,1152]{1,0:T(8,128)(2,1)} %get-tuple-element.58), channel_id=1, source_target_pairs={{0,144},{8,152},{16,128},{24,136},{32,176},{40,184},{48,160},{56,1... | collective-permute-start | bytes 442376 | tf_op jit(solution)/shard_map/ppermute | solution.py:39
  72.1 17.0 %collective-permute-start.12 = (bf16[64,1152]{1,0:T(8,128)(2,1)}, bf16[64,1152]{1,0:T(8,128)(2,1)S(1)}, u32[]{:S(2)}, u32[]{:S(2)}) collective-permute-start(bf16[64,1152]{1,0:T(8,128)(2,1)} %get-tuple-element.59), channel_id=1, source_target_pairs={{0,128},{8,136},{16,144},{24,152},{32,160},{40,168},{48,176},{56,1... | collective-permute-start | bytes 442376 | tf_op jit(solution)/shard_map/ppermute | solution.py:39
  76.0 13.0 %collective-permute-start.13 = (bf16[64,1152]{1,0:T(8,128)(2,1)}, bf16[64,1152]{1,0:T(8,128)(2,1)S(1)}, u32[]{:S(2)}, u32[]{:S(2)}) collective-permute-start(bf16[64,1152]{1,0:T(8,128)(2,1)} %get-tuple-element.60), channel_id=1, source_target_pairs={{0,16},{8,24},{16,0},{24,8},{32,48},{40,56},{48,32},{56,40},{64,80... | collective-permute-start | bytes 442376 | tf_op jit(solution)/shard_map/ppermute | solution.py:39
  76.0 33.2 %collective-permute-start.21 = (bf16[1024,256]{1,0:T(8,128)(2,1)S(1)}, bf16[1024,256]{1,0:T(8,128)(2,1)S(1)}, u32[]{:S(2)}, u32[]{:S(2)}) collective-permute-start(bf16[1024,256]{1,0:T(8,128)(2,1)S(1)} %copy-done.11), channel_id=1, source_target_pairs={{0,8},{8,0},{16,24},{24,16},{32,40},{40,32},{48,56},{56,48},{64,72... | collective-permute-start | bytes 1572872 | tf_op jit(solution)/shard_map/ppermute | solution.py:39
  83.2 5.9 %copy-start.15 = (bf16[64,1152]{1,0:T(8,128)(2,1)}, bf16[64,1152]{1,0:T(8,128)(2,1)S(1)}, u32[]{:S(2)}) copy-start(bf16[64,1152]{1,0:T(8,128)(2,1)S(1)} %collective-permute-done.11.refs_0_) | copy-start | bytes 442372
  89.7 0.7 copy-start.17
  92.6 4.0 %collective-permute-start.14 = (bf16[64,1024]{1,0:T(8,128)(2,1)}, bf16[64,1024]{1,0:T(8,128)(2,1)S(1)}, u32[]{:S(2)}, u32[]{:S(2)}) collective-permute-start(bf16[64,1024]{1,0:T(8,128)(2,1)} %merge.1.refs_0_), channel_id=1, source_target_pairs={{0,224},{8,232},{16,240},{24,248},{32,0},{40,8},{48,16},{56,24},{6... | collective-permute-start | bytes 393224 | tf_op jit(solution)/shard_map/ppermute | solution.py:39
  92.6 16.6 %collective-permute-start.22 = (bf16[1024,256]{1,0:T(8,128)(2,1)S(1)}, bf16[1024,256]{1,0:T(8,128)(2,1)S(1)}, u32[]{:S(2)}, u32[]{:S(2)}) collective-permute-start(bf16[1024,256]{1,0:T(8,128)(2,1)S(1)} %collective-permute-done.9.refs_10_), channel_id=1, source_target_pairs={{0,8},{8,0},{16,24},{24,16},{32,40},{40,32},{48,56},{56,48},{64,72... | collective-permute-start | bytes 1572872 | tf_op jit(solution)/shard_map/ppermute | solution.py:39
  94.0 6.5 %collective-permute-start.18 = (bf16[64,1024]{1,0:T(8,128)(2,1)}, bf16[64,1024]{1,0:T(8,128)(2,1)S(1)}, u32[]{:S(2)}, u32[]{:S(2)}) collective-permute-start(bf16[64,1024]{1,0:T(8,128)(2,1)} %merge.1.refs_0_), channel_id=1, source_target_pairs={{0,32},{8,40},{16,48},{24,56},{32,64},{40,72},{48,80},{56,88},{64,... | collective-permute-start | bytes 393224 | tf_op jit(solution)/shard_map/ppermute | solution.py:39
  96.7 14.3 %copy-start.18 = (bf16[64,1024]{1,0:T(8,128)(2,1)}, bf16[64,1024]{1,0:T(8,128)(2,1)S(1)}, u32[]{:S(2)}) copy-start(bf16[64,1024]{1,0:T(8,128)(2,1)S(1)} %collective-permute-done.14.refs_1_) | copy-start | bytes 393220
  96.7 4.4 %collective-permute-start.15 = (bf16[64,1024]{1,0:T(8,128)(2,1)S(1)}, bf16[64,1024]{1,0:T(8,128)(2,1)S(1)}, u32[]{:S(2)}, u32[]{:S(2)}) collective-permute-start(bf16[64,1024]{1,0:T(8,128)(2,1)S(1)} %collective-permute-done.14.refs_1_), channel_id=1, source_target_pairs={{0,224},{8,232},{16,240},{24,248},{32,0},{40,8},{48,16},{56,24},{6... | collective-permute-start | bytes 393224 | tf_op jit(solution)/shard_map/ppermute | solution.py:39
  100.5 10.4 %copy-start.19 = (bf16[64,1024]{1,0:T(8,128)(2,1)}, bf16[64,1024]{1,0:T(8,128)(2,1)S(1)}, u32[]{:S(2)}) copy-start(bf16[64,1024]{1,0:T(8,128)(2,1)S(1)} %collective-permute-done.18.refs_7_) | copy-start | bytes 393220
  100.5 5.4 %collective-permute-start.19 = (bf16[64,1024]{1,0:T(8,128)(2,1)S(1)}, bf16[64,1024]{1,0:T(8,128)(2,1)S(1)}, u32[]{:S(2)}, u32[]{:S(2)}) collective-permute-start(bf16[64,1024]{1,0:T(8,128)(2,1)S(1)} %collective-permute-done.18.refs_7_), channel_id=1, source_target_pairs={{0,32},{8,40},{16,48},{24,56},{32,64},{40,72},{48,80},{56,88},{64,... | collective-permute-start | bytes 393224 | tf_op jit(solution)/shard_map/ppermute | solution.py:39
  101.1 9.9 %copy-start.20 = (bf16[64,1024]{1,0:T(8,128)(2,1)}, bf16[64,1024]{1,0:T(8,128)(2,1)S(1)}, u32[]{:S(2)}) copy-start(bf16[64,1024]{1,0:T(8,128)(2,1)S(1)} %collective-permute-done.15.refs_2_) | copy-start | bytes 393220
  101.1 4.8 %collective-permute-start.16 = (bf16[64,1024]{1,0:T(8,128)(2,1)S(1)}, bf16[64,1024]{1,0:T(8,128)(2,1)S(1)}, u32[]{:S(2)}, u32[]{:S(2)}) collective-permute-start(bf16[64,1024]{1,0:T(8,128)(2,1)S(1)} %collective-permute-done.15.refs_2_), channel_id=1, source_target_pairs={{0,224},{8,232},{16,240},{24,248},{32,0},{40,8},{48,16},{56,24},{6... | collective-permute-start | bytes 393224 | tf_op jit(solution)/shard_map/ppermute | solution.py:39
  105.9 5.1 %copy-start.21 = (bf16[64,1024]{1,0:T(8,128)(2,1)}, bf16[64,1024]{1,0:T(8,128)(2,1)S(1)}, u32[]{:S(2)}) copy-start(bf16[64,1024]{1,0:T(8,128)(2,1)S(1)} %collective-permute-done.19.refs_6_) | copy-start | bytes 393220
  105.9 5.0 %collective-permute-start.20 = (bf16[64,1024]{1,0:T(8,128)(2,1)S(1)}, bf16[64,1024]{1,0:T(8,128)(2,1)S(1)}, u32[]{:S(2)}, u32[]{:S(2)}) collective-permute-start(bf16[64,1024]{1,0:T(8,128)(2,1)S(1)} %collective-permute-done.19.refs_6_), channel_id=1, source_target_pairs={{0,32},{8,40},{16,48},{24,56},{32,64},{40,72},{48,80},{56,88},{64,... | collective-permute-start | bytes 393224 | tf_op jit(solution)/shard_map/ppermute | solution.py:39
  105.9 5.1 %copy-start.22 = (bf16[64,1024]{1,0:T(8,128)(2,1)}, bf16[64,1024]{1,0:T(8,128)(2,1)S(1)}, u32[]{:S(2)}) copy-start(bf16[64,1024]{1,0:T(8,128)(2,1)S(1)} %collective-permute-done.16.refs_3_) | copy-start | bytes 393220
  105.9 5.0 %collective-permute-start.17 = (bf16[64,1024]{1,0:T(8,128)(2,1)S(1)}, bf16[64,1024]{1,0:T(8,128)(2,1)S(1)}, u32[]{:S(2)}, u32[]{:S(2)}) collective-permute-start(bf16[64,1024]{1,0:T(8,128)(2,1)S(1)} %collective-permute-done.16.refs_3_), channel_id=1, source_target_pairs={{0,224},{8,232},{16,240},{24,248},{32,0},{40,8},{48,16},{56,24},{6... | collective-permute-start | bytes 393224 | tf_op jit(solution)/shard_map/ppermute | solution.py:39
  109.2 1.8 %copy-start.13 = (bf16[1024,256]{1,0:T(8,128)(2,1)}, bf16[1024,256]{1,0:T(8,128)(2,1)S(1)}, u32[]{:S(2)}) copy-start(bf16[1024,256]{1,0:T(8,128)(2,1)S(1)} %collective-permute-done.21.refs_9_) | copy-start | bytes 1572868
  109.2 1.8 %copy-start.14 = (bf16[1024,256]{1,0:T(8,128)(2,1)}, bf16[1024,256]{1,0:T(8,128)(2,1)S(1)}, u32[]{:S(2)}) copy-start(bf16[1024,256]{1,0:T(8,128)(2,1)S(1)} %collective-permute-done.22.refs_11_) | copy-start | bytes 1572868
  110.9 0.6 copy-start.23
  111.6 0.6 copy-start.24
  (1 other events, 0.6 us)

commit v8 on v7

--- a/solution.py
+++ b/solution.py
@@ -319,7 +319,8 @@
         ids += [row(n, yc), row(n, yc ^ 1)]
     ids, span = jnp.stack(ids), span_rank.reshape(Z * YC, TOK)
 
-    ids, span, own = lax.optimization_barrier((ids, span, own))
+    place = jnp.stack([z, yc])
+    place, ids, span, own = lax.optimization_barrier((place, ids, span, own))
     own_pair = (own, own_pair[1])
     state = attention(q_blocks, own_pair)
     kv_up, kv_down, *state = lax.optimization_barrier((kv_up, kv_down, *state))
@@ -334,16 +335,19 @@
     weight_y, cross, far, side, mine = lax.optimization_barrier(
         (weight_y, cross, far, side, mine)
     )
-    weights = [out_weight, weight_c, weight_y, over_c(weight_y)]
+    weight_yc = over_c(weight_y)
     cross = seq_permute(cross, lambda z, y, c: (z + 4, 1 - y, c))
-    attended = merge((cross, shift(far, 4), over_y(side), mine))
+    parts = (cross, shift(far, 4), over_y(side), mine)
+    weight_c, weight_yc, *parts = lax.optimization_barrier((weight_c, weight_yc, *parts))
+    weights = [out_weight, weight_c, weight_y, weight_yc]
+    attended = merge(parts)
 
     blocks = [attended] + [None] * (Z - 1)
     for k in (1, 2, 3):
         blocks[k] = shift(blocks[k - 1], -1)
         blocks[Z - k] = shift(blocks[(Z - k + 1) % Z], 1)
     blocks[4] = shift(blocks[3], -1)
-    shares = product(jnp.stack([z, yc]), blocks, weights).reshape(YC * Z, TOK, 256)
+    shares = product(place, blocks, weights).reshape(YC * Z, TOK, 256)
     shares = lax.all_to_all(
         shares, ("seq", "head"), 0, 0, axis_index_groups=PLANES, tiled=True
     )

time: 147 us -> 147 us (level)
  starting transfers between devices: 41.6 us -> 38.1 us
  waiting for transfers between devices: 22.9 us -> 24.7 us
  Pallas kernels: 42.7 us -> 44.5 us
  local copies, waits for them, and re-layouts: 7.76 us -> 6.26 us
    ppermute x23, starting transfers between devices: 41.6 us -> 38.1 us  [seq_permute(): return lax.ppermute(value, 'seq', pairs)]
    ppermute x23, waiting for transfers between devices: 22.9 us -> 24.7 us  [seq_permute(): return lax.ppermute(value, 'seq', pairs)]
    pallas_call x3, Pallas kernels: 34.3 us -> 35.9 us  [attention(): pl.pallas_call(functools.partial(attention_kernel, len(shards), first, la...]
    unnamed x52, local copies, waits for them, and re-layouts: 6.46 us -> 4.95 us
  transfers between devices with their start and end apart: 23 -> 23, of which waited for: 9 -> 10; matrix products, arithmetic and copies ran while one was open for 1% -> 1% of each run, Pallas kernels for 26% -> 26%
where the time goes in v8:
time: 147 us; the launch traced here: 145 us
  Pallas kernels  44.5 us (30%)
  starting transfers between devices  38.1 us (26%)
  blocking collectives  29.5 us (20%)
  waiting for transfers between devices  24.7 us (17%)
  local copies, waits for them, and re-layouts  6.26 us (4%)
    ppermute x23, starting transfers between devices, seq_permute(): return lax.ppermute(value, 'seq', pairs)  38.1 us
    pallas_call x3, Pallas kernels, attention(): pl.pallas_call(functools.partial(attention_kernel, len(shards), first, la...  35.9 us
    all_to_all x1, blocking collectives, body(): lax.all_to_all(shares, ('seq', 'head'), 0, 0, axis_index_groups=PLANES, t...  29.5 us
    ppermute x23, waiting for transfers between devices, seq_permute(): return lax.ppermute(value, 'seq', pairs)  24.7 us
    unnamed x52, local copies, waits for them, and re-layouts  4.95 us
    pallas_call x1, Pallas kernels, product(): pl.pallas_call(product_kernel, out_shape=jax.ShapeDtypeStruct((YC, Z, TOK...  4.3 us
  transfers between devices with their start and end apart: 23, of which 10 were waited for; matrix products, arithmetic and copies ran while one was open for 1% of the time, Pallas kernels for 26%

profile of v8, /device:TPU:1, one launch (start us, length us, event | category | flops | bytes accessed | tf_op | source)
XLA Modules:
  0.0 145.4 jit_solution(3089494620927808967)
XLA Ops:
  0.0 7.7 %collective-permute-start = (bf16[64,1024]{1,0:T(8,128)(2,1)}, bf16[64,1024]{1,0:T(8,128)(2,1)S(1)}, u32[]{:S(2)}, u32[]{:S(2)}) collective-permute-start(bf16[64,1024]{1,0:T(8,128)(2,1)} %refs_3_.5), channel_id=1, source_target_pairs={{0,128},{8,136},{16,144},{24,152},{32,160},{40,168},{48,176},{56,1... | collective-permute-start | bytes 393224 | tf_op jit(solution)/shard_map/ppermute | solution.py:39
  7.7 1.3 collective-permute-start.1
  9.7 1.9 %pack.1.refs_4_.refs_8_ = bf16[2192,128]{1,0:T(8,128)(2,1)} custom-call(s32[1]{0:T(128)S(6)} %copy.9.length_ref, bf16[1,1024,128]{2,1,0:T(8,128)(2,1)} %k_ref.1, bf16[1,1024,128]{2,1,0:T(8,128)(2,1)} %v_ref.1, bf16[64,128]{1,0:T(8,128)(2,1)} %nk_ref.1, bf16[64,128]{1,0:T(8,128)(2,1)} %nv_ref.1), custom_call_target="tpu_custom_call" | custom-call | tf_op jit(solution)/shard_map/pack/pallas_call | solution.py:55
  11.6 1.2 collective-permute-start.6
  12.8 4.1 %collective-permute-start.4 = (bf16[2192,128]{1,0:T(8,128)(2,1)}, bf16[2192,128]{1,0:T(8,128)(2,1)S(1)}, u32[]{:S(2)}, u32[]{:S(2)}) collective-permute-start(bf16[2192,128]{1,0:T(8,128)(2,1)} %pack.1.refs_4_.refs_8_), channel_id=1, source_target_pairs={{0,224},{8,232},{16,240},{24,248},{32,0},{40,8},{48,16},{56,24},{6... | collective-permute-start | bytes 1683464 | tf_op jit(solution)/shard_map/ppermute | solution.py:39
  16.9 1.3 collective-permute-start.2
  18.2 0.7 reshape.12.refs_17_
  18.9 0.6 stack.60.refs_16_
  19.6 0.7 pad_add_fusion.place_ref
  20.2 0.9 collective-permute-done.2.refs_0_
  21.1 0.6 copy-done.10
  21.7 0.8 copy-done.1
  22.5 8.7 %attention.3 = (f32[1,2048]{1,0:T(1,128)}, f32[144,2048]{1,0:T(8,128)}) custom-call(bf16[64,1024]{1,0:T(8,128)(2,1)} %copy-done.10, bf16[64,1024]{1,0:T(8,128)(2,1)} %copy-done.8, bf16[64,1024]{1,0:T(8,128)(2,1)} %copy-done.9, bf16[64,1024]{1,0:T(8,128)(2,1)} %refs_3_.5, bf16[2192,128]{1,0:T(8,128)(2,1)} %pack.1.refs_4_.refs_8_, bf16[2192,128]{1,0:T(8,128)(2,1)} %copy-done.1), custom_call_target="tpu_custom_call" | custom-call | flops 1 | bytes 1 | tf_op jit(solution)/shard_map/attention/pallas_call | solution.py:234
  31.3 0.4 collective-permute-done.5.refs_6_.refs_12_
  31.6 1.8 %collective-permute-start.7 = (bf16[2192,128]{1,0:T(8,128)(2,1)S(1)}, bf16[2192,128]{1,0:T(8,128)(2,1)S(1)}, u32[]{:S(2)}, u32[]{:S(2)}) collective-permute-start(bf16[2192,128]{1,0:T(8,128)(2,1)S(1)} %collective-permute-done.4.refs_4_.refs_10_), channel_id=1, source_target_pairs={{0,8},{8,0},{16,24},{24,16},{32,40},{40,32},{48,56},{56,48},{64,72... | collective-permute-start | bytes 1683464 | tf_op jit(solution)/shard_map/ppermute | solution.py:39
  33.5 0.1 collective-permute-start.8
  33.6 1.9 %collective-permute-start.3 = (bf16[2192,128]{1,0:T(8,128)(2,1)S(1)}, bf16[2192,128]{1,0:T(8,128)(2,1)S(1)}, u32[]{:S(2)}, u32[]{:S(2)}) collective-permute-start(bf16[2192,128]{1,0:T(8,128)(2,1)S(1)} %copy-done), channel_id=1, source_target_pairs={{0,192},{8,200},{16,208},{24,216},{32,96},{40,104},{48,112},{56,12... | collective-permute-start | bytes 1683464 | tf_op jit(solution)/shard_map/ppermute | solution.py:39
  35.5 0.4 collective-permute-done.8.refs_7_.refs_13_
  35.9 0.5 copy-done.4
  36.4 0.8 copy-done.5
  37.2 16.0 %attention.4 = (f32[1,2048]{1,0:T(1,128)}, f32[144,2048]{1,0:T(8,128)}) custom-call(bf16[64,1024]{1,0:T(8,128)(2,1)} %copy-done.10, bf16[64,1024]{1,0:T(8,128)(2,1)} %copy-done.8, bf16[64,1024]{1,0:T(8,128)(2,1)} %copy-done.9, bf16[64,1024]{1,0:T(8,128)(2,1)} %refs_3_.5, bf16[2192,128]{1,0:T(8,128)(2,1)} %copy-done.2, bf16[2192,128]{1,0:T(8,128)(2,1)} %copy-done.4, ...), custom_call_target="tpu_custom_call" | custom-call | flops 1 | bytes 1 | tf_op jit(solution)/shard_map/attention/pallas_call | solution.py:234
  53.2 1.0 collective-permute-start.11
  54.2 0.2 collective-permute-start.9
  54.4 1.4 collective-permute-done.11.refs_5_.refs_15_
  55.8 0.8 copy-done.7
  56.6 11.1 %attention.5 = (bf16[64,1152]{1,0:T(8,128)(2,1)}, bf16[64,1152]{1,0:T(8,128)(2,1)}, bf16[64,1152]{1,0:T(8,128)(2,1)}, bf16[64,1152]{1,0:T(8,128)(2,1)}) custom-call(bf16[64,1024]{1,0:T(8,128)(2,1)} %copy-done.10, bf16[64,1024]{1,0:T(8,128)(2,1)} %copy-done.8, bf16[64,1024]{1,0:T(8,128)(2,1)} %copy-done.9, bf16[64,1024]{1,0:T(8,128)(2,1)} %refs_3_.5, ...), custom_call_target="tpu_custom_call" | custom-call | flops 1 | bytes 1 | tf_op jit(solution)/shard_map/attention/pallas_call | solution.py:234
  67.7 0.8 collective-permute-start.12
  68.5 4.3 %collective-permute-start.13 = (bf16[64,1152]{1,0:T(8,128)(2,1)}, bf16[64,1152]{1,0:T(8,128)(2,1)S(1)}, u32[]{:S(2)}, u32[]{:S(2)}) collective-permute-start(bf16[64,1152]{1,0:T(8,128)(2,1)} %get-tuple-element.67), channel_id=1, source_target_pairs={{0,144},{8,152},{16,128},{24,136},{32,176},{40,184},{48,160},{56,1... | collective-permute-start | bytes 442376 | tf_op jit(solution)/shard_map/ppermute | solution.py:39
  72.9 2.1 %collective-permute-start.14 = (bf16[64,1152]{1,0:T(8,128)(2,1)}, bf16[64,1152]{1,0:T(8,128)(2,1)S(1)}, u32[]{:S(2)}, u32[]{:S(2)}) collective-permute-start(bf16[64,1152]{1,0:T(8,128)(2,1)} %get-tuple-element.68), channel_id=1, source_target_pairs={{0,128},{8,136},{16,144},{24,152},{32,160},{40,168},{48,176},{56,1... | collective-permute-start | bytes 442376 | tf_op jit(solution)/shard_map/ppermute | solution.py:39
  75.0 0.1 collective-permute-start.15
  75.1 7.9 %collective-permute-done.13.refs_0_ = bf16[64,1152]{1,0:T(8,128)(2,1)S(1)} collective-permute-done((bf16[64,1152]{1,0:T(8,128)(2,1)}, bf16[64,1152]{1,0:T(8,128)(2,1)S(1)}, u32[]{:S(2)}, u32[]{:S(2)}) %collective-permute-start.13) | collective-permute-done | bytes 147488 | tf_op jit(solution)/shard_map/ppermute | solution.py:39
  83.0 5.4 %collective-permute-done.14.refs_1_ = bf16[64,1152]{1,0:T(8,128)(2,1)S(1)} collective-permute-done((bf16[64,1152]{1,0:T(8,128)(2,1)}, bf16[64,1152]{1,0:T(8,128)(2,1)S(1)}, u32[]{:S(2)}, u32[]{:S(2)}) %collective-permute-start.14) | collective-permute-done | bytes 147488 | tf_op jit(solution)/shard_map/ppermute | solution.py:39
  88.4 0.6 copy-done.16
  89.1 0.1 copy-done.17
  89.1 2.4 %merge.1.refs_0_ = bf16[64,1024]{1,0:T(8,128)(2,1)} custom-call(bf16[64,1152]{1,0:T(8,128)(2,1)} %copy-done.15, bf16[64,1152]{1,0:T(8,128)(2,1)} %copy-done.16, bf16[64,1152]{1,0:T(8,128)(2,1)} %copy-done.17, bf16[64,1152]{1,0:T(8,128)(2,1)} %get-tuple-element.74.refs_3_), custom_call_target="tpu_custom_call" | custom-call | tf_op jit(solution)/shard_map/merge/pallas_call | solution.py:266
  91.6 1.2 collective-permute-start.16
  92.8 0.3 collective-permute-start.20
  93.0 2.6 %collective-permute-done.16.refs_1_ = bf16[64,1024]{1,0:T(8,128)(2,1)S(1)} collective-permute-done((bf16[64,1024]{1,0:T(8,128)(2,1)}, bf16[64,1024]{1,0:T(8,128)(2,1)S(1)}, u32[]{:S(2)}, u32[]{:S(2)}) %collective-permute-start.16) | collective-permute-done | bytes 131104 | tf_op jit(solution)/shard_map/ppermute | solution.py:39
  95.6 2.4 %collective-permute-start.17 = (bf16[64,1024]{1,0:T(8,128)(2,1)S(1)}, bf16[64,1024]{1,0:T(8,128)(2,1)S(1)}, u32[]{:S(2)}, u32[]{:S(2)}) collective-permute-start(bf16[64,1024]{1,0:T(8,128)(2,1)S(1)} %collective-permute-done.16.refs_1_), channel_id=1, source_target_pairs={{0,224},{8,232},{16,240},{24,248},{32,0},{40,8},{48,16},{56,24},{6... | collective-permute-start | bytes 393224 | tf_op jit(solution)/shard_map/ppermute | solution.py:39
  98.0 1.9 %collective-permute-done.17.refs_2_ = bf16[64,1024]{1,0:T(8,128)(2,1)S(1)} collective-permute-done((bf16[64,1024]{1,0:T(8,128)(2,1)S(1)}, bf16[64,1024]{1,0:T(8,128)(2,1)S(1)}, u32[]{:S(2)}, u32[]{:S(2)}) %collective-permute-start.17) | collective-permute-done | bytes 131104 | tf_op jit(solution)/shard_map/ppermute | solution.py:39
  100.0 3.1 %collective-permute-start.18 = (bf16[64,1024]{1,0:T(8,128)(2,1)S(1)}, bf16[64,1024]{1,0:T(8,128)(2,1)S(1)}, u32[]{:S(2)}, u32[]{:S(2)}) collective-permute-start(bf16[64,1024]{1,0:T(8,128)(2,1)S(1)} %collective-permute-done.17.refs_2_), channel_id=1, source_target_pairs={{0,224},{8,232},{16,240},{24,248},{32,0},{40,8},{48,16},{56,24},{6... | collective-permute-start | bytes 393224 | tf_op jit(solution)/shard_map/ppermute | solution.py:39
  103.1 1.9 %collective-permute-done.18.refs_3_ = bf16[64,1024]{1,0:T(8,128)(2,1)S(1)} collective-permute-done((bf16[64,1024]{1,0:T(8,128)(2,1)S(1)}, bf16[64,1024]{1,0:T(8,128)(2,1)S(1)}, u32[]{:S(2)}, u32[]{:S(2)}) %collective-permute-start.18) | collective-permute-done | bytes 131104 | tf_op jit(solution)/shard_map/ppermute | solution.py:39
  105.0 3.1 %collective-permute-start.19 = (bf16[64,1024]{1,0:T(8,128)(2,1)S(1)}, bf16[64,1024]{1,0:T(8,128)(2,1)S(1)}, u32[]{:S(2)}, u32[]{:S(2)}) collective-permute-start(bf16[64,1024]{1,0:T(8,128)(2,1)S(1)} %collective-permute-done.18.refs_3_), channel_id=1, source_target_pairs={{0,224},{8,232},{16,240},{24,248},{32,0},{40,8},{48,16},{56,24},{6... | collective-permute-start | bytes 393224 | tf_op jit(solution)/shard_map/ppermute | solution.py:39
  108.1 2.0 %collective-permute-done.19.refs_4_ = bf16[64,1024]{1,0:T(8,128)(2,1)S(1)} collective-permute-done((bf16[64,1024]{1,0:T(8,128)(2,1)S(1)}, bf16[64,1024]{1,0:T(8,128)(2,1)S(1)}, u32[]{:S(2)}, u32[]{:S(2)}) %collective-permute-start.19) | collective-permute-done | bytes 131104 | tf_op jit(solution)/shard_map/ppermute | solution.py:39
  110.1 0.6 copy-done.24
  110.8 4.3 %product.1 = bf16[4,8,64,256]{3,2,1,0:T(8,128)(2,1)} custom-call(s32[2]{0:T(128)} %pad_add_fusion.place_ref, bf16[64,1024]{1,0:T(8,128)(2,1)} %merge.1.refs_0_, bf16[64,1024]{1,0:T(8,128)(2,1)} %copy-done.18, bf16[64,1024]{1,0:T(8,128)(2,1)} %copy-done.20, bf16[64,1024]{1,0:T(8,128)(2,1)} %copy-done.22, bf16[64,1024]{1,0:T(8,128)(2,1)} %copy-done.24, ...), custom_call_target="tpu_custom_call" | custom-call | tf_op jit(solution)/shard_map/product/pallas_call | solution.py:286
  115.1 29.5 %all_to_all.5 = bf16[32,64,256]{2,1,0:T(8,128)(2,1)S(1)} all-to-all(bf16[32,64,256]{2,1,0:T(8,128)(2,1)} %bitcast.17), channel_id=1, replica_groups={{0,1,2,3,4,5,6,7,8,9,10,11,12,13,14,15,16,17,18,19,20,21,22,23,24,25,26..., dimensions={0} | all-to-all | bytes 2097152 | tf_op jit(solution)/shard_map/all_to_all | solution.py:351
  144.6 0.8 bitcast_reduce_fusion
  (61 shorter events, 0.1 us)
Async XLA Ops:
  0.0 18.2 %copy-start.25 = (s32[2048]{0:T(1024)S(1)}, s32[2048]{0:T(1024)}, u32[]{:S(2)}) copy-start(s32[2048]{0:T(1024)} %param.14) | copy-start | bytes 24580
  0.0 12.8 %collective-permute-start = (bf16[64,1024]{1,0:T(8,128)(2,1)}, bf16[64,1024]{1,0:T(8,128)(2,1)S(1)}, u32[]{:S(2)}, u32[]{:S(2)}) collective-permute-start(bf16[64,1024]{1,0:T(8,128)(2,1)} %refs_3_.5), channel_id=1, source_target_pairs={{0,128},{8,136},{16,144},{24,152},{32,160},{40,168},{48,176},{56,1... | collective-permute-start | bytes 393224 | tf_op jit(solution)/shard_map/ppermute | solution.py:39
  7.7 5.1 %collective-permute-start.1 = (bf16[64,1024]{1,0:T(8,128)(2,1)}, bf16[64,1024]{1,0:T(8,128)(2,1)S(1)}, u32[]{:S(2)}, u32[]{:S(2)}) collective-permute-start(bf16[64,1024]{1,0:T(8,128)(2,1)} %refs_3_.5), channel_id=1, source_target_pairs={{0,16},{8,24},{16,0},{24,8},{32,48},{40,56},{48,32},{56,40},{64,80... | collective-permute-start | bytes 393224 | tf_op jit(solution)/shard_map/ppermute | solution.py:39
  11.6 22.0 %copy-start = (bf16[2192,128]{1,0:T(8,128)(2,1)S(1)}, bf16[2192,128]{1,0:T(8,128)(2,1)}, u32[]{:S(2)}) copy-start(bf16[2192,128]{1,0:T(8,128)(2,1)} %pack.1.refs_4_.refs_8_) | copy-start | bytes 1683460
  11.6 9.5 %collective-permute-start.6 = (bf16[2192,128]{1,0:T(8,128)(2,1)}, bf16[2192,128]{1,0:T(8,128)(2,1)S(1)}, u32[]{:S(2)}, u32[]{:S(2)}) collective-permute-start(bf16[2192,128]{1,0:T(8,128)(2,1)} %pack.1.refs_4_.refs_8_), channel_id=1, source_target_pairs={{0,8},{8,0},{16,24},{24,16},{32,40},{40,32},{48,56},{56,48},{64,72... | collective-permute-start | bytes 1683464 | tf_op jit(solution)/shard_map/ppermute | solution.py:39
  12.8 8.3 %copy-start.8 = (bf16[64,1024]{1,0:T(8,128)(2,1)}, bf16[64,1024]{1,0:T(8,128)(2,1)S(1)}, u32[]{:S(2)}) copy-start(bf16[64,1024]{1,0:T(8,128)(2,1)S(1)} %collective-permute-done.refs_1_) | copy-start | bytes 393220
  12.8 8.3 %copy-start.9 = (bf16[64,1024]{1,0:T(8,128)(2,1)}, bf16[64,1024]{1,0:T(8,128)(2,1)S(1)}, u32[]{:S(2)}) copy-start(bf16[64,1024]{1,0:T(8,128)(2,1)S(1)} %collective-permute-done.1.refs_2_) | copy-start | bytes 393220
  12.8 18.4 %collective-permute-start.4 = (bf16[2192,128]{1,0:T(8,128)(2,1)}, bf16[2192,128]{1,0:T(8,128)(2,1)S(1)}, u32[]{:S(2)}, u32[]{:S(2)}) collective-permute-start(bf16[2192,128]{1,0:T(8,128)(2,1)} %pack.1.refs_4_.refs_8_), channel_id=1, source_target_pairs={{0,224},{8,232},{16,240},{24,248},{32,0},{40,8},{48,16},{56,24},{6... | collective-permute-start | bytes 1683464 | tf_op jit(solution)/shard_map/ppermute | solution.py:39
  16.9 14.7 %collective-permute-start.5 = (bf16[2192,128]{1,0:T(8,128)(2,1)}, bf16[2192,128]{1,0:T(8,128)(2,1)S(1)}, u32[]{:S(2)}, u32[]{:S(2)}) collective-permute-start(bf16[2192,128]{1,0:T(8,128)(2,1)} %pack.1.refs_4_.refs_8_), channel_id=1, source_target_pairs={{0,32},{8,40},{16,48},{24,56},{32,64},{40,72},{48,80},{56,88},{64,... | collective-permute-start | bytes 1683464 | tf_op jit(solution)/shard_map/ppermute | solution.py:39
  16.9 4.1 %collective-permute-start.2 = (bf16[64,1024]{1,0:T(8,128)(2,1)S(1)}, bf16[64,1024]{1,0:T(8,128)(2,1)S(1)}, u32[]{:S(2)}, u32[]{:S(2)}) collective-permute-start(bf16[64,1024]{1,0:T(8,128)(2,1)S(1)} %collective-permute-done.refs_1_), channel_id=1, source_target_pairs={{0,16},{8,24},{16,0},{24,8},{32,48},{40,56},{48,32},{56,40},{64,80... | collective-permute-start | bytes 393224 | tf_op jit(solution)/shard_map/ppermute | solution.py:39
  21.1 0.7 copy-start.10
  21.7 0.8 copy-start.1
  31.3 4.6 %copy-start.2 = (bf16[2192,128]{1,0:T(8,128)(2,1)}, bf16[2192,128]{1,0:T(8,128)(2,1)S(1)}, u32[]{:S(2)}) copy-start(bf16[2192,128]{1,0:T(8,128)(2,1)S(1)} %collective-permute-done.4.refs_4_.refs_10_) | copy-start | bytes 1683460
  31.6 4.3 %copy-start.3 = (bf16[2192,128]{1,0:T(8,128)(2,1)}, bf16[2192,128]{1,0:T(8,128)(2,1)S(1)}, u32[]{:S(2)}) copy-start(bf16[2192,128]{1,0:T(8,128)(2,1)S(1)} %collective-permute-done.5.refs_6_.refs_12_) | copy-start | bytes 1683460
  31.6 22.5 %copy-start.11 = (bf16[1024,256]{1,0:T(8,128)(2,1)S(1)}, bf16[1024,256]{1,0:T(8,128)(2,1)}, u32[]{:S(2)}) copy-start(bf16[1024,256]{1,0:T(8,128)(2,1)} %refs_8_.1) | copy-start | bytes 1572868
  31.6 3.9 %collective-permute-start.7 = (bf16[2192,128]{1,0:T(8,128)(2,1)S(1)}, bf16[2192,128]{1,0:T(8,128)(2,1)S(1)}, u32[]{:S(2)}, u32[]{:S(2)}) collective-permute-start(bf16[2192,128]{1,0:T(8,128)(2,1)S(1)} %collective-permute-done.4.refs_4_.refs_10_), channel_id=1, source_target_pairs={{0,8},{8,0},{16,24},{24,16},{32,40},{40,32},{48,56},{56,48},{64,72... | collective-permute-start | bytes 1683464 | tf_op jit(solution)/shard_map/ppermute | solution.py:39
  33.5 2.4 %collective-permute-start.8 = (bf16[2192,128]{1,0:T(8,128)(2,1)S(1)}, bf16[2192,128]{1,0:T(8,128)(2,1)S(1)}, u32[]{:S(2)}, u32[]{:S(2)}) collective-permute-start(bf16[2192,128]{1,0:T(8,128)(2,1)S(1)} %collective-permute-done.5.refs_6_.refs_12_), channel_id=1, source_target_pairs={{0,8},{8,0},{16,24},{24,16},{32,40},{40,32},{48,56},{56,48},{64,72... | collective-permute-start | bytes 1683464 | tf_op jit(solution)/shard_map/ppermute | solution.py:39
  33.6 19.6 %collective-permute-start.3 = (bf16[2192,128]{1,0:T(8,128)(2,1)S(1)}, bf16[2192,128]{1,0:T(8,128)(2,1)S(1)}, u32[]{:S(2)}, u32[]{:S(2)}) collective-permute-start(bf16[2192,128]{1,0:T(8,128)(2,1)S(1)} %copy-done), channel_id=1, source_target_pairs={{0,192},{8,200},{16,208},{24,216},{32,96},{40,104},{48,112},{56,12... | collective-permute-start | bytes 1683464 | tf_op jit(solution)/shard_map/ppermute | solution.py:39
  35.5 0.8 copy-start.4
  36.3 0.8 copy-start.5
  53.2 2.6 %copy-start.6 = (bf16[2192,128]{1,0:T(8,128)(2,1)}, bf16[2192,128]{1,0:T(8,128)(2,1)S(1)}, u32[]{:S(2)}) copy-start(bf16[2192,128]{1,0:T(8,128)(2,1)S(1)} %collective-permute-done.3.refs_4_.refs_14_) | copy-start | bytes 1683460
  53.2 2.5 %collective-permute-start.11 = (bf16[2192,128]{1,0:T(8,128)(2,1)S(1)}, bf16[2192,128]{1,0:T(8,128)(2,1)S(1)}, u32[]{:S(2)}, u32[]{:S(2)}) collective-permute-start(bf16[2192,128]{1,0:T(8,128)(2,1)S(1)} %collective-permute-done.3.refs_4_.refs_14_), channel_id=1, source_target_pairs={{0,8},{8,0},{16,24},{24,16},{32,40},{40,32},{48,56},{56,48},{64,72... | collective-permute-start | bytes 1683464 | tf_op jit(solution)/shard_map/ppermute | solution.py:39
  54.2 13.5 %collective-permute-start.10 = (bf16[1024,256]{1,0:T(8,128)(2,1)S(1)}, bf16[1024,256]{1,0:T(8,128)(2,1)S(1)}, u32[]{:S(2)}, u32[]{:S(2)}) collective-permute-start(bf16[1024,256]{1,0:T(8,128)(2,1)S(1)} %copy-done.11), channel_id=1, source_target_pairs={{0,16},{8,24},{16,0},{24,8},{32,48},{40,56},{48,32},{56,40},{64,80... | collective-permute-start | bytes 1572872 | tf_op jit(solution)/shard_map/ppermute | solution.py:39
  54.2 20.9 %collective-permute-start.9 = (bf16[1024,256]{1,0:T(8,128)(2,1)S(1)}, bf16[1024,256]{1,0:T(8,128)(2,1)S(1)}, u32[]{:S(2)}, u32[]{:S(2)}) collective-permute-start(bf16[1024,256]{1,0:T(8,128)(2,1)S(1)} %copy-done.11), channel_id=1, source_target_pairs={{0,8},{8,0},{16,24},{24,16},{32,40},{40,32},{48,56},{56,48},{64,72... | collective-permute-start | bytes 1572872 | tf_op jit(solution)/shard_map/ppermute | solution.py:39
  55.8 0.8 copy-start.7
  67.7 42.4 %copy-start.12 = (bf16[1024,256]{1,0:T(8,128)(2,1)}, bf16[1024,256]{1,0:T(8,128)(2,1)S(1)}, u32[]{:S(2)}) copy-start(bf16[1024,256]{1,0:T(8,128)(2,1)S(1)} %collective-permute-done.10.refs_10_) | copy-start | bytes 1572868
  67.7 20.7 %collective-permute-start.12 = (bf16[1024,256]{1,0:T(8,128)(2,1)S(1)}, bf16[1024,256]{1,0:T(8,128)(2,1)S(1)}, u32[]{:S(2)}, u32[]{:S(2)}) collective-permute-start(bf16[1024,256]{1,0:T(8,128)(2,1)S(1)} %collective-permute-done.10.refs_10_), channel_id=1, source_target_pairs={{0,8},{8,0},{16,24},{24,16},{32,40},{40,32},{48,56},{56,48},{64,72... | collective-permute-start | bytes 1572872 | tf_op jit(solution)/shard_map/ppermute | solution.py:39
  68.5 14.5 %collective-permute-start.13 = (bf16[64,1152]{1,0:T(8,128)(2,1)}, bf16[64,1152]{1,0:T(8,128)(2,1)S(1)}, u32[]{:S(2)}, u32[]{:S(2)}) collective-permute-start(bf16[64,1152]{1,0:T(8,128)(2,1)} %get-tuple-element.67), channel_id=1, source_target_pairs={{0,144},{8,152},{16,128},{24,136},{32,176},{40,184},{48,160},{56,1... | collective-permute-start | bytes 442376 | tf_op jit(solution)/shard_map/ppermute | solution.py:39
  72.9 15.5 %collective-permute-start.14 = (bf16[64,1152]{1,0:T(8,128)(2,1)}, bf16[64,1152]{1,0:T(8,128)(2,1)S(1)}, u32[]{:S(2)}, u32[]{:S(2)}) collective-permute-start(bf16[64,1152]{1,0:T(8,128)(2,1)} %get-tuple-element.68), channel_id=1, source_target_pairs={{0,128},{8,136},{16,144},{24,152},{32,160},{40,168},{48,176},{56,1... | collective-permute-start | bytes 442376 | tf_op jit(solution)/shard_map/ppermute | solution.py:39
  75.0 13.4 %collective-permute-start.15 = (bf16[64,1152]{1,0:T(8,128)(2,1)}, bf16[64,1152]{1,0:T(8,128)(2,1)S(1)}, u32[]{:S(2)}, u32[]{:S(2)}) collective-permute-start(bf16[64,1152]{1,0:T(8,128)(2,1)} %get-tuple-element.69), channel_id=1, source_target_pairs={{0,16},{8,24},{16,0},{24,8},{32,48},{40,56},{48,32},{56,40},{64,80... | collective-permute-start | bytes 442376 | tf_op jit(solution)/shard_map/ppermute | solution.py:39
  75.1 35.0 %copy-start.13 = (bf16[1024,256]{1,0:T(8,128)(2,1)}, bf16[1024,256]{1,0:T(8,128)(2,1)S(1)}, u32[]{:S(2)}) copy-start(bf16[1024,256]{1,0:T(8,128)(2,1)S(1)} %collective-permute-done.9.refs_9_) | copy-start | bytes 1572868
  83.0 5.4 %copy-start.15 = (bf16[64,1152]{1,0:T(8,128)(2,1)}, bf16[64,1152]{1,0:T(8,128)(2,1)S(1)}, u32[]{:S(2)}) copy-start(bf16[64,1152]{1,0:T(8,128)(2,1)S(1)} %collective-permute-done.13.refs_0_) | copy-start | bytes 442372
  88.4 0.7 copy-start.16
  88.4 0.7 copy-start.17
  89.1 21.0 %copy-start.14 = (bf16[1024,256]{1,0:T(8,128)(2,1)}, bf16[1024,256]{1,0:T(8,128)(2,1)S(1)}, u32[]{:S(2)}) copy-start(bf16[1024,256]{1,0:T(8,128)(2,1)S(1)} %collective-permute-done.12.refs_11_) | copy-start | bytes 1572868
  91.6 4.0 %collective-permute-start.16 = (bf16[64,1024]{1,0:T(8,128)(2,1)}, bf16[64,1024]{1,0:T(8,128)(2,1)S(1)}, u32[]{:S(2)}, u32[]{:S(2)}) collective-permute-start(bf16[64,1024]{1,0:T(8,128)(2,1)} %merge.1.refs_0_), channel_id=1, source_target_pairs={{0,224},{8,232},{16,240},{24,248},{32,0},{40,8},{48,16},{56,24},{6... | collective-permute-start | bytes 393224 | tf_op jit(solution)/shard_map/ppermute | solution.py:39
  92.8 5.2 %collective-permute-start.20 = (bf16[64,1024]{1,0:T(8,128)(2,1)}, bf16[64,1024]{1,0:T(8,128)(2,1)S(1)}, u32[]{:S(2)}, u32[]{:S(2)}) collective-permute-start(bf16[64,1024]{1,0:T(8,128)(2,1)} %merge.1.refs_0_), channel_id=1, source_target_pairs={{0,32},{8,40},{16,48},{24,56},{32,64},{40,72},{48,80},{56,88},{64,... | collective-permute-start | bytes 393224 | tf_op jit(solution)/shard_map/ppermute | solution.py:39
  95.6 14.5 %copy-start.18 = (bf16[64,1024]{1,0:T(8,128)(2,1)}, bf16[64,1024]{1,0:T(8,128)(2,1)S(1)}, u32[]{:S(2)}) copy-start(bf16[64,1024]{1,0:T(8,128)(2,1)S(1)} %collective-permute-done.16.refs_1_) | copy-start | bytes 393220
  95.6 4.4 %collective-permute-start.17 = (bf16[64,1024]{1,0:T(8,128)(2,1)S(1)}, bf16[64,1024]{1,0:T(8,128)(2,1)S(1)}, u32[]{:S(2)}, u32[]{:S(2)}) collective-permute-start(bf16[64,1024]{1,0:T(8,128)(2,1)S(1)} %collective-permute-done.16.refs_1_), channel_id=1, source_target_pairs={{0,224},{8,232},{16,240},{24,248},{32,0},{40,8},{48,16},{56,24},{6... | collective-permute-start | bytes 393224 | tf_op jit(solution)/shard_map/ppermute | solution.py:39
  98.0 12.1 %copy-start.19 = (bf16[64,1024]{1,0:T(8,128)(2,1)}, bf16[64,1024]{1,0:T(8,128)(2,1)S(1)}, u32[]{:S(2)}) copy-start(bf16[64,1024]{1,0:T(8,128)(2,1)S(1)} %collective-permute-done.20.refs_7_) | copy-start | bytes 393220
  98.0 5.0 %collective-permute-start.21 = (bf16[64,1024]{1,0:T(8,128)(2,1)S(1)}, bf16[64,1024]{1,0:T(8,128)(2,1)S(1)}, u32[]{:S(2)}, u32[]{:S(2)}) collective-permute-start(bf16[64,1024]{1,0:T(8,128)(2,1)S(1)} %collective-permute-done.20.refs_7_), channel_id=1, source_target_pairs={{0,32},{8,40},{16,48},{24,56},{32,64},{40,72},{48,80},{56,88},{64,... | collective-permute-start | bytes 393224 | tf_op jit(solution)/shard_map/ppermute | solution.py:39
  100.0 10.1 %copy-start.20 = (bf16[64,1024]{1,0:T(8,128)(2,1)}, bf16[64,1024]{1,0:T(8,128)(2,1)S(1)}, u32[]{:S(2)}) copy-start(bf16[64,1024]{1,0:T(8,128)(2,1)S(1)} %collective-permute-done.17.refs_2_) | copy-start | bytes 393220
  100.0 5.0 %collective-permute-start.18 = (bf16[64,1024]{1,0:T(8,128)(2,1)S(1)}, bf16[64,1024]{1,0:T(8,128)(2,1)S(1)}, u32[]{:S(2)}, u32[]{:S(2)}) collective-permute-start(bf16[64,1024]{1,0:T(8,128)(2,1)S(1)} %collective-permute-done.17.refs_2_), channel_id=1, source_target_pairs={{0,224},{8,232},{16,240},{24,248},{32,0},{40,8},{48,16},{56,24},{6... | collective-permute-start | bytes 393224 | tf_op jit(solution)/shard_map/ppermute | solution.py:39
  103.1 7.1 %copy-start.21 = (bf16[64,1024]{1,0:T(8,128)(2,1)}, bf16[64,1024]{1,0:T(8,128)(2,1)S(1)}, u32[]{:S(2)}) copy-start(bf16[64,1024]{1,0:T(8,128)(2,1)S(1)} %collective-permute-done.21.refs_6_) | copy-start | bytes 393220
  103.1 5.0 %collective-permute-start.22 = (bf16[64,1024]{1,0:T(8,128)(2,1)S(1)}, bf16[64,1024]{1,0:T(8,128)(2,1)S(1)}, u32[]{:S(2)}, u32[]{:S(2)}) collective-permute-start(bf16[64,1024]{1,0:T(8,128)(2,1)S(1)} %collective-permute-done.21.refs_6_), channel_id=1, source_target_pairs={{0,32},{8,40},{16,48},{24,56},{32,64},{40,72},{48,80},{56,88},{64,... | collective-permute-start | bytes 393224 | tf_op jit(solution)/shard_map/ppermute | solution.py:39
  105.0 5.1 %copy-start.22 = (bf16[64,1024]{1,0:T(8,128)(2,1)}, bf16[64,1024]{1,0:T(8,128)(2,1)S(1)}, u32[]{:S(2)}) copy-start(bf16[64,1024]{1,0:T(8,128)(2,1)S(1)} %collective-permute-done.18.refs_3_) | copy-start | bytes 393220
  105.0 5.1 %collective-permute-start.19 = (bf16[64,1024]{1,0:T(8,128)(2,1)S(1)}, bf16[64,1024]{1,0:T(8,128)(2,1)S(1)}, u32[]{:S(2)}, u32[]{:S(2)}) collective-permute-start(bf16[64,1024]{1,0:T(8,128)(2,1)S(1)} %collective-permute-done.18.refs_3_), channel_id=1, source_target_pairs={{0,224},{8,232},{16,240},{24,248},{32,0},{40,8},{48,16},{56,24},{6... | collective-permute-start | bytes 393224 | tf_op jit(solution)/shard_map/ppermute | solution.py:39
  108.1 2.0 %copy-start.23 = (bf16[64,1024]{1,0:T(8,128)(2,1)}, bf16[64,1024]{1,0:T(8,128)(2,1)S(1)}, u32[]{:S(2)}) copy-start(bf16[64,1024]{1,0:T(8,128)(2,1)S(1)} %collective-permute-done.22.refs_5_) | copy-start | bytes 393220
  (1 other events, 0.6 us)
